TPU v7x, 128 devices: a whole 4x4x4 slice. The times are simulated.
128 devices in a mesh: group: 2 (over z_lo), dp: 8 (over x, z_hi), space: 8 (over y, core).
Axes of the slice: x: 4, y: 4, z: 4 (z_hi: 2, z_lo: 2; z = z_hi * 2 + z_lo), core: 2. Of those that a mesh axis runs over, the one named last changes fastest.
Arguments:
- velocity: float32 [3, 320, 32, 1024], P(None, ('group', 'dp'), None, 'space'), may hold values from -6 to 6
- conv_first: bfloat16 [27, 64, 3], replicated, may hold values from -3 to 3
- conv_mid: bfloat16 [27, 64, 64], replicated, may hold values from -0.15625 to 0.15625
- conv_last: bfloat16 [6, 64], replicated, may hold values from -0.75 to 0.75
- corner_x: int32 [16, 8], replicated, may hold values from 0 to 4
- corner_z: int32 [16, 8], replicated, may hold values from 0 to 16
- corner_y: int32 [16, 8], replicated, may hold values from 0 to 112
- patch_live: int32 [16, 8], replicated, may hold values from 0 to 1, as said below
- patch_dest: int32 [16, 8], replicated, may hold values from 0 to 15, as said below
Outputs:
- velocity_next: float32 [3, 320, 32, 1024], P(None, ('group', 'dp'), None, 'space')
- filtered: float32 [3, 320, 32, 1024], P(None, ('group', 'dp'), None, 'space')
- stress: float32 [6, 320, 32, 1024], P(None, ('group', 'dp'), None, 'space')
- grad_first: float32 [27, 64, 3], replicated
- grad_mid: float32 [27, 64, 64], replicated
- grad_last: float32 [6, 64], replicated
- replica_loss: float32 [16], P(('group', 'dp'))
Inputs may be any that keep to these rules, and one draw needn't show every extreme that they name: `patch_live`: each row of blocks (first index) holds exactly 2 ones. `patch_dest`: among the blocks with patch_live = 1, no replica is named more than 4 times, and some replica exactly 4 times.
All inputs are finite; a program needn't handle non-finite values.
Results may differ from a plain program's by a relative error of at most 0.0003.
Values may be sent and summed in bfloat16 or wider, within the bound.
No kernel may reach another device: no remote copies, remote signals or barrier semaphores. Data moves between devices by JAX's collectives and lax.ppermute only.
A program may use at most 64 MiB of HBM per device.

v0:
```python
import jax
import jax.numpy as jnp
from jax import lax
from jax.sharding import PartitionSpec as P

PE = 16
SOLVER_STEPS = 2
FILTER_PASSES = 3
LIVE_ROW = 2
CAP = 4


time_step = 0.05
viscosity = 0.1


def with_halo(shard, sides, width, wrap):
    for axis, dim in sides:
        count, length = (lax.axis_size(axis), shard.shape[dim])
        up = [(i, (i + 1) % count) for i in range(count if wrap else count - 1)]
        down = [(j, i) for i, j in up]
        last = lax.slice_in_dim(shard, length - width, length, axis=dim)
        initial = lax.slice_in_dim(shard, 0, width, axis=dim)
        before = lax.ppermute(last, axis, up)
        after = lax.ppermute(initial, axis, down)
        shard = jnp.concatenate([before, shard, after], axis=dim)
    return shard


def products(field):
    return jnp.stack(
        [
            field[0] * field[0],
            field[1] * field[1],
            field[2] * field[2],
            field[0] * field[1],
            field[0] * field[2],
            field[1] * field[2],
        ]
    )


def combine(middle, x_plus, x_minus, y_plus, y_minus, z_plus, z_minus):
    advect = (
        middle[0:1] * ((x_plus - x_minus) * 0.5)
        + middle[1:2] * ((y_plus - y_minus) * 0.5)
        + middle[2:3] * ((z_plus - z_minus) * 0.5)
    )
    laplace = x_plus + x_minus + y_plus + y_minus + z_plus + z_minus - 6.0 * middle
    return middle + time_step * (viscosity * laplace - advect)


def advance(widened):
    middle = widened[:, 1:-1, :, 1:-1]
    padded = jnp.pad(middle, ((0, 0), (0, 0), (1, 1), (0, 0)))
    return combine(
        middle,
        widened[:, 2:, :, 1:-1],
        widened[:, :-2, :, 1:-1],
        widened[:, 1:-1, :, 2:],
        widened[:, 1:-1, :, :-2],
        padded[:, :, 2:],
        padded[:, :, :-2],
    )


def smooth_inner(widened):
    along_x = 0.25 * widened[:, :-2] + 0.5 * widened[:, 1:-1] + 0.25 * widened[:, 2:]
    return 0.25 * along_x[..., :-2] + 0.5 * along_x[..., 1:-1] + 0.25 * along_x[..., 2:]


def live_slots(live_flags, dest_table):
    live_rank = jnp.cumsum(live_flags, axis=1) - 1
    slot_index = jnp.arange(LIVE_ROW, dtype=jnp.int32)
    slot_hit = (live_flags[:, None, :] == 1) & (live_rank[:, None, :] == slot_index[None, :, None])
    column = jnp.arange(live_flags.shape[1], dtype=jnp.int32)
    owner_col = jnp.sum(jnp.where(slot_hit, column[None, None, :], 0), axis=2)
    target_row = jnp.sum(jnp.where(slot_hit, dest_table[:, None, :], 0), axis=2)
    return (owner_col, target_row)


def table_entry(lookup_table, row_index, col_index):
    rows_hit = jnp.arange(lookup_table.shape[0]) == row_index
    cols_hit = jnp.arange(lookup_table.shape[1]) == col_index
    return jnp.sum(jnp.where(rows_hit[:, None] & cols_hit[None, :], lookup_table, 0))


def silu_slope(value):
    sigmoid = jax.nn.sigmoid(value)
    return sigmoid * (1.0 + value * (1.0 - sigmoid))


def shifted_views(source, direction):
    margin = PE + 1
    flat_width = PE * PE
    padded = jnp.pad(source, ((0, 0), (0, 0), (0, 0), (margin, margin)))
    column = jnp.arange(flat_width) % PE
    shifted = {}
    for step_z in (-1, 0, 1):
        for step_y in (-1, 0, 1):
            offset = direction * (step_z * PE + step_y)
            moved = lax.slice_in_dim(padded, margin + offset, margin + offset + flat_width, axis=3)
            inside = (
                (column + direction * step_y >= 0) & (column + direction * step_y < PE)
            ).astype(source.dtype)
            shifted[step_z, step_y] = moved * inside
    return shifted


def convolve(shifted, weight, count_rows):
    accumulated = None
    for step_x in (-1, 0, 1):
        for step_z in (-1, 0, 1):
            for step_y in (-1, 0, 1):
                kernel_index = (step_x + 1) * 9 + (step_z + 1) * 3 + (step_y + 1)
                window_part = lax.slice_in_dim(
                    shifted[step_z, step_y], step_x + 1, step_x + 1 + count_rows, axis=2
                )
                addend = jnp.einsum(
                    "oc,scxv->soxv",
                    weight[kernel_index],
                    window_part,
                    preferred_element_type=jnp.float32,
                )
                accumulated = addend if accumulated is None else accumulated + addend
    return accumulated


def convolve_back(shifted, weight, count_rows):
    accumulated = None
    for step_x in (-1, 0, 1):
        for step_z in (-1, 0, 1):
            for step_y in (-1, 0, 1):
                kernel_index = (step_x + 1) * 9 + (step_z + 1) * 3 + (step_y + 1)
                window_part = lax.slice_in_dim(
                    shifted[step_z, step_y], 1 - step_x, 1 - step_x + count_rows, axis=2
                )
                addend = jnp.einsum(
                    "oc,soxv->scxv",
                    weight[kernel_index],
                    window_part,
                    preferred_element_type=jnp.float32,
                )
                accumulated = addend if accumulated is None else accumulated + addend
    return accumulated


def correlate(gradient, shifted, count_rows):
    pieces = []
    for step_x in (-1, 0, 1):
        for step_z in (-1, 0, 1):
            for step_y in (-1, 0, 1):
                window_part = lax.slice_in_dim(
                    shifted[step_z, step_y], step_x + 1, step_x + 1 + count_rows, axis=2
                )
                pieces.append(
                    jnp.einsum(
                        "soxv,scxv->oc", gradient, window_part, preferred_element_type=jnp.float32
                    )
                )
    return jnp.stack(pieces)


def train_slots(slot_data, weights, slot_targets, conv_first, conv_mid, conv_last, row_count):
    count_rows = slot_data.shape[2]
    inputs = slot_data[:, 0:3]
    target = slot_data[:, 3:9].astype(jnp.float32)
    rim_input = with_halo(inputs, (("space", 2),), 1, False)
    input_views = shifted_views(rim_input, 1)
    pre_first = convolve(input_views, conv_first, count_rows)
    hidden_first = jax.nn.silu(pre_first).astype(jnp.bfloat16)
    rim_hidden = with_halo(hidden_first, (("space", 2),), 1, False)
    hidden_views = shifted_views(rim_hidden, 1)
    pre_mid = convolve(hidden_views, conv_mid, count_rows)
    hidden_mid = jax.nn.silu(pre_mid).astype(jnp.bfloat16)
    predicted = jnp.einsum(
        "oc,scxv->soxv", conv_last, hidden_mid, preferred_element_type=jnp.float32
    )
    mismatch = predicted - target
    squared = jnp.sum(mismatch * mismatch, axis=(1, 2, 3))
    grad_scale = 2.0 / (PE**3 * row_count * LIVE_ROW)
    grad_pred = (mismatch * (grad_scale * weights)[:, None, None, None]).astype(jnp.bfloat16)
    grad_last = jnp.einsum(
        "soxv,scxv->oc", grad_pred, hidden_mid, preferred_element_type=jnp.float32
    )
    grad_hidden = jnp.einsum(
        "oc,soxv->scxv", conv_last, grad_pred, preferred_element_type=jnp.float32
    )
    grad_pre_mid = (grad_hidden * silu_slope(pre_mid)).astype(jnp.bfloat16)
    grad_mid = correlate(grad_pre_mid, hidden_views, count_rows)
    rim_grad = with_halo(grad_pre_mid, (("space", 2),), 1, False)
    back_views = shifted_views(rim_grad, -1)
    grad_first_hidden = convolve_back(back_views, conv_mid, count_rows)
    grad_pre_first = (grad_first_hidden * silu_slope(pre_first)).astype(jnp.bfloat16)
    grad_first = correlate(grad_pre_first, input_views, count_rows)
    replica_onehot = (
        jnp.arange(row_count, dtype=jnp.int32)[None, :] == slot_targets[:, None]
    ).astype(jnp.float32)
    loss_share = jnp.sum(replica_onehot * (weights * squared)[:, None], axis=0) / (PE**3 * LIVE_ROW)
    return (grad_first, grad_mid, grad_last, loss_share)


def local(
    velocity, conv_first, conv_mid, conv_last, corner_x, corner_z, corner_y, patch_live, patch_dest
):
    row_count = patch_live.shape[0]
    my_row = lax.axis_index("group") * lax.axis_size("dp") + lax.axis_index("dp")
    my_col = lax.axis_index("space")
    velocity_now = velocity
    for repeat in range(SOLVER_STEPS):
        widened = with_halo(velocity_now, ((("group", "dp"), 1), ("space", 3)), 1, True)
        velocity_now = advance(widened)
    fields = jnp.concatenate([velocity_now, products(velocity_now)], axis=0)
    for repeat in range(FILTER_PASSES):
        widened = with_halo(fields, ((("group", "dp"), 1), ("space", 3)), 1, True)
        fields = smooth_inner(widened)
    filtered = fields[0:3]
    stress = fields[3:9] - products(filtered)
    begin_x = table_entry(corner_x, my_row, my_col)
    begin_z = table_entry(corner_z, my_row, my_col)
    begin_y = table_entry(corner_y, my_row, my_col)
    zero_index = jnp.zeros((), jnp.int32)
    patch_block = lax.dynamic_slice(
        fields, (zero_index, begin_x, begin_z, begin_y), (9, PE, PE, PE)
    )
    patch_input = jnp.concatenate(
        [patch_block[0:3], patch_block[3:9] - products(patch_block[0:3])], axis=0
    ).astype(jnp.bfloat16)
    spatial = lax.axis_size("space")
    slab_rows = PE // spatial
    outgoing = patch_input.reshape(9, spatial, slab_rows, PE * PE).transpose(1, 0, 2, 3)
    received = lax.all_to_all(outgoing, "space", split_axis=0, concat_axis=0, tiled=True)
    owner_col, target_row = live_slots(patch_live, patch_dest)
    my_owner = lax.dynamic_index_in_dim(owner_col, my_row, 0, keepdims=False)
    compact = jnp.take(received, my_owner, axis=0)
    gathered = lax.all_gather(compact, ("group", "dp"), axis=0, tiled=True)
    flat_target = target_row.reshape(-1)
    wanted = (flat_target == my_row).astype(jnp.int32)
    order_rank = jnp.cumsum(wanted) - 1
    slot_index = jnp.arange(CAP, dtype=jnp.int32)
    chosen_hit = (wanted[None, :] == 1) & (order_rank[None, :] == slot_index[:, None])
    everywhere = jnp.arange(flat_target.shape[0], dtype=jnp.int32)
    chosen = jnp.sum(jnp.where(chosen_hit, everywhere[None, :], 0), axis=1)
    weights = jnp.any(chosen_hit, axis=1).astype(jnp.float32)
    slot_data = jnp.take(gathered, chosen, axis=0)
    slot_targets = jnp.zeros((CAP,), jnp.int32) + my_row
    grad_first, grad_mid, grad_last, loss_share = train_slots(
        slot_data, weights, slot_targets, conv_first, conv_mid, conv_last, row_count
    )
    summed = lax.psum((grad_first, grad_mid, grad_last, loss_share), ("group", "dp", "space"))
    replica_loss = lax.dynamic_slice_in_dim(summed[3], my_row, 1)
    return (velocity_now, filtered, stress, summed[0], summed[1], summed[2], replica_loss)


def solution(mesh):
    in_specs = (P(None, ("group", "dp"), None, "space"), P(), P(), P(), P(), P(), P(), P(), P())
    out_specs = (
        P(None, ("group", "dp"), None, "space"),
        P(None, ("group", "dp"), None, "space"),
        P(None, ("group", "dp"), None, "space"),
        P(),
        P(),
        P(),
        P(("group", "dp")),
    )
    return jax.shard_map(local, mesh=mesh, in_specs=in_specs, out_specs=out_specs, check_vma=False)
```

profile of v0, /device:TPU:1, one launch (start us, length us, event | category | flops | bytes accessed | tf_op | source)
XLA Modules:
  0.0 437.6 jit_solution(10566935002662681413)
XLA Ops:
  8.1 4.5 %collective-permute-start.1 = (f32[3,1,32,128]{3,2,1,0:T(8,128)S(1)}, f32[3,1,32,128]{3,2,1,0:T(8,128)S(1)}, u32[]{:S(2)}, u32[]{:S(2)}) collective-permute-start(f32[3,1,32,128]{3,2,1,0:T(8,128)S(1)} %get-tuple-element.95), channel_id=1, source_target_pairs={{0,8},{8,16},{16,24},{24,32},{32,40},{40,48},{48,56},{56,64},{64,7... | collective-permute-start | bytes 147464 | tf_op jit(solution)/shard_map/ppermute | solution.py:24
  12.6 2.4 collective-permute-start
  15.0 2.1 multiply_bitcast_fusion.2
  20.0 1.6 fusion.402
  21.6 1.7 fusion.401
  24.0 1.8 fusion.395
  25.7 1.7 copy.691
  28.4 1.7 copy.692
  31.5 1.5 copy.448
  34.5 2.9 multiply_add_fusion.1
  37.4 3.2 collective-permute-start.4
  41.9 4.9 %collective-permute-done.5 = f32[3,1,32,128]{3,2,1,0:T(8,128)S(1)} collective-permute-done((f32[3,1,32,128]{3,2,1,0:T(8,128)S(1)}, f32[3,1,32,128]{3,2,1,0:T(8,128)S(1)}, u32[]{:S(2)}, u32[]{:S(2)}) %collective-permute-start.5) | collective-permute-done | bytes 49184 | tf_op jit(solution)/shard_map/ppermute | solution.py:24
  47.8 5.1 %collective-permute-start.6 = (f32[3,22,32,1]{2,1,3,0:T(8,128)S(1)}, f32[3,22,32,1]{2,1,3,0:T(8,128)S(1)}, u32[]{:S(2)}, u32[]{:S(2)}) collective-permute-start(f32[3,22,32,1]{2,1,3,0:T(8,128)S(1)} %copy.693), channel_id=1, source_target_pairs={{1,0},{2,1},{3,2},{4,3},{5,4},{6,5},{7,6},{0,7},{9,8},{10,9},{11,1... | collective-permute-start | bytes 25352 | tf_op jit(solution)/shard_map/ppermute | solution.py:25
  54.3 1.5 copy.452
  57.3 5.6 %constant_dynamic-update-slice_fusion.3 = (f32[9,20,32,128]{3,2,1,0:T(8,128)S(1)}, f32[3,20,32,128]{3,2,1,0:T(8,128)S(1)}) fusion(f32[3,20,32,128]{3,2,1,0:T(8,128)} %copy-done.1, f32[20,32,128]{2,1,0:T(8,128)} %get-tuple-element.90, f32[20,32,128]{2,1,0:T(8,128)} %get-tuple-element.89, f32[20,32,128]{2,1,0:T(8,128)S(1)} %get-tuple-element.88, ...), kind=kLoop, calls=%fused_computation.412 | loop fusion | flops 6635519 | bytes 4047360
  63.3 4.9 %collective-permute-start.9 = (f32[9,1,32,128]{3,2,1,0:T(8,128)S(1)}, f32[9,1,32,128]{3,2,1,0:T(8,128)S(1)}, u32[]{:S(2)}, u32[]{:S(2)}) collective-permute-start(f32[9,1,32,128]{3,2,1,0:T(8,128)S(1)} %get-tuple-element.81), channel_id=1, source_target_pairs={{8,0},{16,8},{24,16},{32,24},{40,32},{48,40},{56,48},{64,56},{72,6... | collective-permute-start | bytes 442376 | tf_op jit(solution)/shard_map/ppermute | solution.py:25
  69.4 1.7 collective-permute-done.8
  71.5 3.8 fusion.390
  75.3 3.1 copy.695
  78.4 2.8 collective-permute-start.10
  81.2 3.6 copy.696
  86.0 2.7 copy.457
  89.4 3.4 copy.458
  92.7 5.9 %pad_maximum_fusion = f32[9,22,32,130]{3,2,1,0:T(8,128)S(1)} fusion(f32[9,22,32,1]{3,2,1,0:T(8,128)} %copy.458, f32[9,1,32,128]{3,2,1,0:T(8,128)S(1)} %collective-permute-done.9, f32[9,20,32,128]{3,2,1,0:T(8,128)S(1)} %multiply_dynamic-update-slice_fusion.6, f32[9,1,32,128]{3,2,1,0:T(8,128)S(1)} %collective-permute-done.8, f32[9,22,32,1]{3,2,1,0:T(8,128)} %copy.457), kind=kLoop, calls=%fused_computation.2 | loop fusion | flops 3294720 | bytes 6589440 | tf_op jit(solution)/shard_map/concatenate | solution.py:26
  98.7 2.2 fusion.4
  100.9 1.6 fusion.10
  102.6 5.0 %collective-permute-start.13 = (f32[9,1,32,128]{3,2,1,0:T(8,128)S(1)}, f32[9,1,32,128]{3,2,1,0:T(8,128)S(1)}, u32[]{:S(2)}, u32[]{:S(2)}) collective-permute-start(f32[9,1,32,128]{3,2,1,0:T(8,128)S(1)} %get-tuple-element.79), channel_id=1, source_target_pairs={{8,0},{16,8},{24,16},{32,24},{40,32},{48,40},{56,48},{64,56},{72,6... | collective-permute-start | bytes 442376 | tf_op jit(solution)/shard_map/ppermute | solution.py:25
  108.1 2.1 collective-permute-done.12
  110.7 3.8 fusion.389
  114.5 3.1 copy.697
  117.6 4.4 %collective-permute-start.14 = (f32[9,22,32,1]{2,1,3,0:T(8,128)S(1)}, f32[9,22,32,1]{2,1,3,0:T(8,128)S(1)}, u32[]{:S(2)}, u32[]{:S(2)}) collective-permute-start(f32[9,22,32,1]{2,1,3,0:T(8,128)S(1)} %copy.697), channel_id=1, source_target_pairs={{0,1},{1,2},{2,3},{3,4},{4,5},{5,6},{6,7},{7,0},{8,9},{9,10},{10,1... | collective-permute-start | bytes 76040 | tf_op jit(solution)/shard_map/ppermute | solution.py:24
  122.0 3.6 copy.698
  125.7 2.7 copy.461
  128.4 1.7 collective-permute-done.15
  130.1 3.4 copy.462
  133.5 5.9 %pad_maximum_fusion.1 = f32[9,22,32,130]{3,2,1,0:T(8,128)S(1)} fusion(f32[9,22,32,1]{3,2,1,0:T(8,128)} %copy.462, f32[9,1,32,128]{3,2,1,0:T(8,128)S(1)} %collective-permute-done.13, f32[9,20,32,128]{3,2,1,0:T(8,128)S(1)} %fusion.10, f32[9,1,32,128]{3,2,1,0:T(8,128)S(1)} %collective-permute-done.12, f32[9,22,32,1]{3,2,1,0:T(8,128)} %copy.461), kind=kLoop, calls=%fused_computation.3 | loop fusion | flops 3294720 | bytes 6589440 | tf_op jit(solution)/shard_map/concatenate | solution.py:26
  139.4 2.2 fusion.2
  141.7 1.6 fusion.8
  143.4 5.2 %collective-permute-start.17 = (f32[9,1,32,128]{3,2,1,0:T(8,128)S(1)}, f32[9,1,32,128]{3,2,1,0:T(8,128)S(1)}, u32[]{:S(2)}, u32[]{:S(2)}) collective-permute-start(f32[9,1,32,128]{3,2,1,0:T(8,128)S(1)} %get-tuple-element.77), channel_id=1, source_target_pairs={{8,0},{16,8},{24,16},{32,24},{40,32},{48,40},{56,48},{64,56},{72,6... | collective-permute-start | bytes 442376 | tf_op jit(solution)/shard_map/ppermute | solution.py:25
  149.3 4.0 collective-permute-done.16
  153.7 3.8 fusion.388
  157.5 3.1 copy.699
  161.9 3.6 copy.700
  171.6 2.7 copy.465
  174.3 3.4 copy.466
  177.7 5.9 %pad_maximum_fusion.2 = f32[9,22,32,130]{3,2,1,0:T(8,128)S(1)} fusion(f32[9,22,32,1]{3,2,1,0:T(8,128)} %copy.466, f32[9,1,32,128]{3,2,1,0:T(8,128)S(1)} %collective-permute-done.17, f32[9,20,32,128]{3,2,1,0:T(8,128)S(1)} %fusion.8, f32[9,1,32,128]{3,2,1,0:T(8,128)S(1)} %collective-permute-done.16, f32[9,22,32,1]{3,2,1,0:T(8,128)} %copy.465), kind=kLoop, calls=%fused_computation.4 | loop fusion | flops 3294720 | bytes 6589440 | tf_op jit(solution)/shard_map/concatenate | solution.py:26
  183.6 2.2 fusion
  185.8 1.6 fusion.6
  192.2 6.2 %all-to-all-start = ((bf16[8,9,2,256]{3,2,1,0:T(2,128)(2,1)}), bf16[8,9,2,256]{3,2,1,0:T(2,128)(2,1)S(1)}, u32[]{:S(2)}, u32[]{:S(2)}) async-start(bf16[8,9,2,256]{3,2,1,0:T(2,128)(2,1)} %copy.470), calls=%async_computation | async-start | bytes 147456 | tf_op jit(solution)/shard_map/all_to_all | solution.py:232
  201.5 1.9 all-to-all-done
  204.8 32.9 %all_gather.3 = bf16[32,9,2,256]{3,2,1,0:T(2,128)(2,1)S(1)} all-gather(bf16[2,9,2,256]{3,2,1,0:T(2,128)(2,1)S(1)} %broadcast_select_fusion), channel_id=1, replica_groups=mesh['group'=2,'dp'=8,'space'=8] {'group','dp'}, dimensions={0}, use_global_device_ids=true | all-gather | bytes 313344 | tf_op jit(solution)/shard_map/all_gather | solution.py:236
  239.2 10.1 %collective-permute-start.20 = (bf16[4,3,1,256]{3,1,2,0:T(4,128)(2,1)S(1)}, bf16[4,3,1,256]{3,1,2,0:T(4,128)(2,1)S(1)}, u32[]{:S(2)}, u32[]{:S(2)}) collective-permute-start(bf16[4,3,1,256]{3,1,2,0:T(4,128)(2,1)S(1)} %get-tuple-element.115), channel_id=1, source_target_pairs={{0,1},{1,2},{2,3},{3,4},{4,5},{5,6},{6,7},{8,9},{9,10},{10,11},{11... | collective-permute-start | bytes 18440 | tf_op jit(solution)/shard_map/ppermute | solution.py:24
  249.3 2.1 collective-permute-start.21
  252.2 2.1 collective-permute-done.21
  263.3 1.9 collective-permute-start.22
  265.2 2.4 collective-permute-start.23
  267.6 1.7 slice_subtract_fusion
  271.6 1.5 fusion.116
  286.7 2.0 collective-permute-start.24
  288.8 2.5 collective-permute-start.25
  291.6 3.5 collective-permute-done.25
  309.7 62.8 %all-reduce.5 = (f32[27,64,3]{1,2,0:T(4,128)S(1)}, f32[6,64]{1,0:T(8,128)}, f32[16]{0:T(128)S(1)}) all-reduce(f32[27,64,3]{1,2,0:T(4,128)S(1)} %fusion.81, f32[6,64]{1,0:T(8,128)S(1)} %convolution_bitcast_fusion.59, f32[16]{0:T(128)S(1)} %broadcast_multiply_fusion.2), channel_id=1, replica_groups=mesh['group'=2,'dp'=8,'space'=8] {'group','dp','space'}, use_global_device_ids=true, to_apply=%region_9.10 | all-reduce | flops 5584 | bytes 44672 | tf_op jit(solution)/shard_map/psum | solution.py:250
  373.7 54.6 %all-reduce.8.cloned.1.call-done = f32[27,64,64]{2,1,0:T(8,128)} async-done(((f32[27,64,64]{2,1,0:T(8,128)}), f32[27,64,64]{2,1,0:T(8,128)}) %all-reduce.8.cloned.1.call-update) | async-done | bytes 442384 | tf_op jit(solution)/shard_map/psum | solution.py:250
  428.3 2.2 copy.856
  (333 shorter events, 72.2 us)
Async XLA Ops:
  7.2 271.8 %copy-start = (bf16[6,64]{1,0:T(8,128)(2,1)S(1)}, bf16[6,64]{1,0:T(8,128)(2,1)}, u32[]{:S(2)}) copy-start(bf16[6,64]{1,0:T(8,128)(2,1)} %param.12) | copy-start | bytes 2308
  7.2 16.7 %copy-start.3 = (f32[3,20,32,128]{3,2,1,0:T(8,128)S(1)}, f32[3,20,32,128]{3,2,1,0:T(8,128)}, u32[]{:S(2)}) copy-start(f32[3,20,32,128]{3,2,1,0:T(8,128)} %param.9) | copy-start | bytes 2949124
  8.1 15.7 %collective-permute-start.1 = (f32[3,1,32,128]{3,2,1,0:T(8,128)S(1)}, f32[3,1,32,128]{3,2,1,0:T(8,128)S(1)}, u32[]{:S(2)}, u32[]{:S(2)}) collective-permute-start(f32[3,1,32,128]{3,2,1,0:T(8,128)S(1)} %get-tuple-element.95), channel_id=1, source_target_pairs={{0,8},{8,16},{16,24},{24,32},{32,40},{40,48},{48,56},{56,64},{64,7... | collective-permute-start | bytes 147464 | tf_op jit(solution)/shard_map/ppermute | solution.py:24
  12.6 11.3 %collective-permute-start = (f32[3,1,32,128]{3,2,1,0:T(8,128)S(1)}, f32[3,1,32,128]{3,2,1,0:T(8,128)S(1)}, u32[]{:S(2)}, u32[]{:S(2)}) collective-permute-start(f32[3,1,32,128]{3,2,1,0:T(8,128)S(1)} %get-tuple-element.94), channel_id=1, source_target_pairs={{8,0},{16,8},{24,16},{32,24},{40,32},{48,40},{56,48},{64,56},{72,6... | collective-permute-start | bytes 147464 | tf_op jit(solution)/shard_map/ppermute | solution.py:25
  27.4 4.0 collective-permute-start.2
  30.1 2.9 collective-permute-start.3
  37.3 16.0 %copy-start.1 = (f32[3,20,32,128]{3,2,1,0:T(8,128)}, f32[3,20,32,128]{3,2,1,0:T(8,128)S(1)}, u32[]{:S(2)}) copy-start(f32[3,20,32,128]{3,2,1,0:T(8,128)S(1)} %multiply_add_fusion.1) | copy-start | bytes 2949124
  37.4 4.5 %collective-permute-start.4 = (f32[3,1,32,128]{3,2,1,0:T(8,128)S(1)}, f32[3,1,32,128]{3,2,1,0:T(8,128)S(1)}, u32[]{:S(2)}, u32[]{:S(2)}) collective-permute-start(f32[3,1,32,128]{3,2,1,0:T(8,128)S(1)} %get-tuple-element.87), channel_id=1, source_target_pairs={{8,0},{16,8},{24,16},{32,24},{40,32},{48,40},{56,48},{64,56},{72,6... | collective-permute-start | bytes 147464 | tf_op jit(solution)/shard_map/ppermute | solution.py:25
  40.5 6.3 %collective-permute-start.5 = (f32[3,1,32,128]{3,2,1,0:T(8,128)S(1)}, f32[3,1,32,128]{3,2,1,0:T(8,128)S(1)}, u32[]{:S(2)}, u32[]{:S(2)}) collective-permute-start(f32[3,1,32,128]{3,2,1,0:T(8,128)S(1)} %get-tuple-element.86), channel_id=1, source_target_pairs={{0,8},{8,16},{16,24},{24,32},{32,40},{40,48},{48,56},{56,64},{64,7... | collective-permute-start | bytes 147464 | tf_op jit(solution)/shard_map/ppermute | solution.py:24
  47.8 6.5 %collective-permute-start.6 = (f32[3,22,32,1]{2,1,3,0:T(8,128)S(1)}, f32[3,22,32,1]{2,1,3,0:T(8,128)S(1)}, u32[]{:S(2)}, u32[]{:S(2)}) collective-permute-start(f32[3,22,32,1]{2,1,3,0:T(8,128)S(1)} %copy.693), channel_id=1, source_target_pairs={{1,0},{2,1},{3,2},{4,3},{5,4},{6,5},{7,6},{0,7},{9,8},{10,9},{11,1... | collective-permute-start | bytes 25352 | tf_op jit(solution)/shard_map/ppermute | solution.py:25
  53.4 2.4 collective-permute-start.7
  62.9 8.2 %copy-start.2 = (f32[3,20,32,128]{3,2,1,0:T(8,128)}, f32[3,20,32,128]{3,2,1,0:T(8,128)S(1)}, u32[]{:S(2)}) copy-start(f32[3,20,32,128]{3,2,1,0:T(8,128)S(1)} %get-tuple-element.168) | copy-start | bytes 2949124
  63.2 7.9 %collective-permute-start.8 = (f32[9,1,32,128]{3,2,1,0:T(8,128)S(1)}, f32[9,1,32,128]{3,2,1,0:T(8,128)S(1)}, u32[]{:S(2)}, u32[]{:S(2)}) collective-permute-start(f32[9,1,32,128]{3,2,1,0:T(8,128)S(1)} %get-tuple-element.80), channel_id=1, source_target_pairs={{0,8},{8,16},{16,24},{24,32},{32,40},{40,48},{48,56},{56,64},{64,7... | collective-permute-start | bytes 442376 | tf_op jit(solution)/shard_map/ppermute | solution.py:24
  63.3 7.8 %collective-permute-start.9 = (f32[9,1,32,128]{3,2,1,0:T(8,128)S(1)}, f32[9,1,32,128]{3,2,1,0:T(8,128)S(1)}, u32[]{:S(2)}, u32[]{:S(2)}) collective-permute-start(f32[9,1,32,128]{3,2,1,0:T(8,128)S(1)} %get-tuple-element.81), channel_id=1, source_target_pairs={{8,0},{16,8},{24,16},{32,24},{40,32},{48,40},{56,48},{64,56},{72,6... | collective-permute-start | bytes 442376 | tf_op jit(solution)/shard_map/ppermute | solution.py:25
  78.4 7.6 %collective-permute-start.10 = (f32[9,22,32,1]{2,1,3,0:T(8,128)S(1)}, f32[9,22,32,1]{2,1,3,0:T(8,128)S(1)}, u32[]{:S(2)}, u32[]{:S(2)}) collective-permute-start(f32[9,22,32,1]{2,1,3,0:T(8,128)S(1)} %copy.695), channel_id=1, source_target_pairs={{0,1},{1,2},{2,3},{3,4},{4,5},{5,6},{6,7},{7,0},{8,9},{9,10},{10,1... | collective-permute-start | bytes 76040 | tf_op jit(solution)/shard_map/ppermute | solution.py:24
  84.9 4.5 %collective-permute-start.11 = (f32[9,22,32,1]{2,1,3,0:T(8,128)}, f32[9,22,32,1]{2,1,3,0:T(8,128)}, u32[]{:S(2)}, u32[]{:S(2)}) collective-permute-start(f32[9,22,32,1]{2,1,3,0:T(8,128)} %copy.696), channel_id=1, source_target_pairs={{1,0},{2,1},{3,2},{4,3},{5,4},{6,5},{7,6},{0,7},{9,8},{10,9},{11,1... | collective-permute-start | bytes 76040 | tf_op jit(solution)/shard_map/ppermute | solution.py:25
  102.5 7.8 %collective-permute-start.12 = (f32[9,1,32,128]{3,2,1,0:T(8,128)S(1)}, f32[9,1,32,128]{3,2,1,0:T(8,128)S(1)}, u32[]{:S(2)}, u32[]{:S(2)}) collective-permute-start(f32[9,1,32,128]{3,2,1,0:T(8,128)S(1)} %get-tuple-element.78), channel_id=1, source_target_pairs={{0,8},{8,16},{16,24},{24,32},{32,40},{40,48},{48,56},{56,64},{64,7... | collective-permute-start | bytes 442376 | tf_op jit(solution)/shard_map/ppermute | solution.py:24
  102.6 7.7 %collective-permute-start.13 = (f32[9,1,32,128]{3,2,1,0:T(8,128)S(1)}, f32[9,1,32,128]{3,2,1,0:T(8,128)S(1)}, u32[]{:S(2)}, u32[]{:S(2)}) collective-permute-start(f32[9,1,32,128]{3,2,1,0:T(8,128)S(1)} %get-tuple-element.79), channel_id=1, source_target_pairs={{8,0},{16,8},{24,16},{32,24},{40,32},{48,40},{56,48},{64,56},{72,6... | collective-permute-start | bytes 442376 | tf_op jit(solution)/shard_map/ppermute | solution.py:25
  117.6 8.1 %collective-permute-start.14 = (f32[9,22,32,1]{2,1,3,0:T(8,128)S(1)}, f32[9,22,32,1]{2,1,3,0:T(8,128)S(1)}, u32[]{:S(2)}, u32[]{:S(2)}) collective-permute-start(f32[9,22,32,1]{2,1,3,0:T(8,128)S(1)} %copy.697), channel_id=1, source_target_pairs={{0,1},{1,2},{2,3},{3,4},{4,5},{5,6},{6,7},{7,0},{8,9},{9,10},{10,1... | collective-permute-start | bytes 76040 | tf_op jit(solution)/shard_map/ppermute | solution.py:24
  125.6 4.5 %collective-permute-start.15 = (f32[9,22,32,1]{2,1,3,0:T(8,128)}, f32[9,22,32,1]{2,1,3,0:T(8,128)}, u32[]{:S(2)}, u32[]{:S(2)}) collective-permute-start(f32[9,22,32,1]{2,1,3,0:T(8,128)} %copy.698), channel_id=1, source_target_pairs={{1,0},{2,1},{3,2},{4,3},{5,4},{6,5},{7,6},{0,7},{9,8},{10,9},{11,1... | collective-permute-start | bytes 76040 | tf_op jit(solution)/shard_map/ppermute | solution.py:25
  141.6 6.9 %copy-start.33 = (s32[16,8]{0,1:T(8,128)S(1)}, s32[16,8]{0,1:T(8,128)}, u32[]{:S(2)}) copy-start(s32[16,8]{0,1:T(8,128)} %param.15) | copy-start | bytes 1540
  141.6 6.9 %copy-start.34 = (s32[16,8]{0,1:T(8,128)S(1)}, s32[16,8]{0,1:T(8,128)}, u32[]{:S(2)}) copy-start(s32[16,8]{0,1:T(8,128)} %param.14) | copy-start | bytes 1540
  141.6 6.9 %copy-start.35 = (s32[16,8]{0,1:T(8,128)S(1)}, s32[16,8]{0,1:T(8,128)}, u32[]{:S(2)}) copy-start(s32[16,8]{0,1:T(8,128)} %param.13) | copy-start | bytes 1540
  143.3 10.0 %collective-permute-start.16 = (f32[9,1,32,128]{3,2,1,0:T(8,128)S(1)}, f32[9,1,32,128]{3,2,1,0:T(8,128)S(1)}, u32[]{:S(2)}, u32[]{:S(2)}) collective-permute-start(f32[9,1,32,128]{3,2,1,0:T(8,128)S(1)} %get-tuple-element.76), channel_id=1, source_target_pairs={{0,8},{8,16},{16,24},{24,32},{32,40},{40,48},{48,56},{56,64},{64,7... | collective-permute-start | bytes 442376 | tf_op jit(solution)/shard_map/ppermute | solution.py:24
  143.4 10.0 %collective-permute-start.17 = (f32[9,1,32,128]{3,2,1,0:T(8,128)S(1)}, f32[9,1,32,128]{3,2,1,0:T(8,128)S(1)}, u32[]{:S(2)}, u32[]{:S(2)}) collective-permute-start(f32[9,1,32,128]{3,2,1,0:T(8,128)S(1)} %get-tuple-element.77), channel_id=1, source_target_pairs={{8,0},{16,8},{24,16},{32,24},{40,32},{48,40},{56,48},{64,56},{72,6... | collective-permute-start | bytes 442376 | tf_op jit(solution)/shard_map/ppermute | solution.py:25
  160.6 11.0 %collective-permute-start.18 = (f32[9,22,32,1]{2,1,3,0:T(8,128)S(1)}, f32[9,22,32,1]{2,1,3,0:T(8,128)S(1)}, u32[]{:S(2)}, u32[]{:S(2)}) collective-permute-start(f32[9,22,32,1]{2,1,3,0:T(8,128)S(1)} %copy.699), channel_id=1, source_target_pairs={{0,1},{1,2},{2,3},{3,4},{4,5},{5,6},{6,7},{7,0},{8,9},{9,10},{10,1... | collective-permute-start | bytes 76040 | tf_op jit(solution)/shard_map/ppermute | solution.py:24
  165.5 8.8 %collective-permute-start.19 = (f32[9,22,32,1]{2,1,3,0:T(8,128)}, f32[9,22,32,1]{2,1,3,0:T(8,128)}, u32[]{:S(2)}, u32[]{:S(2)}) collective-permute-start(f32[9,22,32,1]{2,1,3,0:T(8,128)} %copy.700), channel_id=1, source_target_pairs={{1,0},{2,1},{3,2},{4,3},{5,4},{6,5},{7,6},{0,7},{9,8},{10,9},{11,1... | collective-permute-start | bytes 76040 | tf_op jit(solution)/shard_map/ppermute | solution.py:25
  190.4 64.1 %copy-start.13 = (bf16[1,64,3]{1,0,2:T(2,128)(2,1)S(1)}, bf16[1,64,3]{1,0,2:T(2,128)(2,1)}, u32[]{:S(2)}) copy-start(bf16[1,64,3]{1,0,2:T(2,128)(2,1)} %get-tuple-element.152) | copy-start | bytes 1156
  192.2 11.1 %all-to-all-start = ((bf16[8,9,2,256]{3,2,1,0:T(2,128)(2,1)}), bf16[8,9,2,256]{3,2,1,0:T(2,128)(2,1)S(1)}, u32[]{:S(2)}, u32[]{:S(2)}) async-start(bf16[8,9,2,256]{3,2,1,0:T(2,128)(2,1)} %copy.470), calls=%async_computation | async-start | bytes 147456 | tf_op jit(solution)/shard_map/all_to_all | solution.py:232
  198.4 56.4 %copy-start.29 = (bf16[1,64,3]{1,0,2:T(2,128)(2,1)S(1)}, bf16[1,64,3]{1,0,2:T(2,128)(2,1)}, u32[]{:S(2)}) copy-start(bf16[1,64,3]{1,0,2:T(2,128)(2,1)} %get-tuple-element.143) | copy-start | bytes 1156
  198.4 229.9 %all-reduce.8.cloned.1.call-start = ((), (), s32[]{:S(2)}) async-start(), calls=%async_computation.1 | async-start | bytes 1769472 | tf_op jit(solution)/shard_map/psum | solution.py:250
  199.2 56.0 %copy-start.12 = (bf16[1,64,3]{1,0,2:T(2,128)(2,1)S(1)}, bf16[1,64,3]{1,0,2:T(2,128)(2,1)}, u32[]{:S(2)}) copy-start(bf16[1,64,3]{1,0,2:T(2,128)(2,1)} %get-tuple-element.157) | copy-start | bytes 1156
  199.9 55.5 %copy-start.28 = (bf16[1,64,3]{1,0,2:T(2,128)(2,1)S(1)}, bf16[1,64,3]{1,0,2:T(2,128)(2,1)}, u32[]{:S(2)}) copy-start(bf16[1,64,3]{1,0,2:T(2,128)(2,1)} %get-tuple-element.140) | copy-start | bytes 1156
  199.9 55.8 %copy-start.11 = (bf16[1,64,3]{1,0,2:T(2,128)(2,1)S(1)}, bf16[1,64,3]{1,0,2:T(2,128)(2,1)}, u32[]{:S(2)}) copy-start(bf16[1,64,3]{1,0,2:T(2,128)(2,1)} %get-tuple-element.156) | copy-start | bytes 1156
  200.7 55.3 %copy-start.10 = (bf16[1,64,3]{1,0,2:T(2,128)(2,1)S(1)}, bf16[1,64,3]{1,0,2:T(2,128)(2,1)}, u32[]{:S(2)}) copy-start(bf16[1,64,3]{1,0,2:T(2,128)(2,1)} %get-tuple-element.155) | copy-start | bytes 1156
  238.4 17.8 %copy-start.9 = (bf16[1,64,3]{1,0,2:T(2,128)(2,1)S(1)}, bf16[1,64,3]{1,0,2:T(2,128)(2,1)}, u32[]{:S(2)}) copy-start(bf16[1,64,3]{1,0,2:T(2,128)(2,1)} %get-tuple-element.154) | copy-start | bytes 1156
  239.2 13.0 %collective-permute-start.20 = (bf16[4,3,1,256]{3,1,2,0:T(4,128)(2,1)S(1)}, bf16[4,3,1,256]{3,1,2,0:T(4,128)(2,1)S(1)}, u32[]{:S(2)}, u32[]{:S(2)}) collective-permute-start(bf16[4,3,1,256]{3,1,2,0:T(4,128)(2,1)S(1)} %get-tuple-element.115), channel_id=1, source_target_pairs={{0,1},{1,2},{2,3},{3,4},{4,5},{5,6},{6,7},{8,9},{9,10},{10,11},{11... | collective-permute-start | bytes 18440 | tf_op jit(solution)/shard_map/ppermute | solution.py:24
  249.3 5.0 %collective-permute-start.21 = (bf16[4,3,1,256]{3,1,2,0:T(4,128)(2,1)S(1)}, bf16[4,3,1,256]{3,1,2,0:T(4,128)(2,1)S(1)}, u32[]{:S(2)}, u32[]{:S(2)}) collective-permute-start(bf16[4,3,1,256]{3,1,2,0:T(4,128)(2,1)S(1)} %get-tuple-element.116), channel_id=1, source_target_pairs={{1,0},{2,1},{3,2},{4,3},{5,4},{6,5},{7,6},{9,8},{10,9},{11,10},{12... | collective-permute-start | bytes 18440 | tf_op jit(solution)/shard_map/ppermute | solution.py:25
  252.2 4.4 %copy-start.30 = (bf16[1,64,3]{1,0,2:T(2,128)(2,1)S(1)}, bf16[1,64,3]{1,0,2:T(2,128)(2,1)}, u32[]{:S(2)}) copy-start(bf16[1,64,3]{1,0,2:T(2,128)(2,1)} %get-tuple-element.153) | copy-start | bytes 1156
  255.1 1.8 copy-start.8
  255.7 1.5 copy-start.7
  256.0 1.5 copy-start.27
  256.3 1.5 copy-start.26
  256.6 1.5 copy-start.25
  256.9 1.5 copy-start.24
  257.2 1.5 copy-start.23
  257.4 1.5 copy-start.32
  257.8 1.5 copy-start.22
  258.0 1.5 copy-start.31
  258.3 1.5 copy-start.21
  258.6 1.5 copy-start.20
  258.9 1.5 copy-start.19
  259.2 1.5 copy-start.18
  259.5 1.5 copy-start.17
  259.8 1.5 copy-start.16
  260.1 1.5 copy-start.15
  260.4 1.5 copy-start.14
  260.7 1.5 copy-start.36
  261.3 6.3 %copy-start.4 = (f32[6,20,32,128]{3,2,1,0:T(8,128)S(1)}, f32[6,20,32,128]{3,2,1,0:T(8,128)}, u32[]{:S(2)}) copy-start(f32[6,20,32,128]{3,2,1,0:T(8,128)} %multiply_dynamic-update-slice_fusion) | copy-start | bytes 5898244
  263.3 7.1 %collective-permute-start.22 = (bf16[4,64,1,256]{3,1,2,0:T(8,128)(2,1)S(1)}, bf16[4,64,1,256]{3,1,2,0:T(8,128)(2,1)S(1)}, u32[]{:S(2)}, u32[]{:S(2)}) collective-permute-start(bf16[4,64,1,256]{3,1,2,0:T(8,128)(2,1)S(1)} %get-tuple-element.113), channel_id=1, source_target_pairs={{0,1},{1,2},{2,3},{3,4},{4,5},{5,6},{6,7},{8,9},{9,10},{10,11},{11... | collective-permute-start | bytes 393224 | tf_op jit(solution)/shard_map/ppermute | solution.py:24
  265.2 6.3 %collective-permute-start.23 = (bf16[4,64,1,256]{3,1,2,0:T(8,128)(2,1)S(1)}, bf16[4,64,1,256]{3,1,2,0:T(8,128)(2,1)S(1)}, u32[]{:S(2)}, u32[]{:S(2)}) collective-permute-start(bf16[4,64,1,256]{3,1,2,0:T(8,128)(2,1)S(1)} %get-tuple-element.114), channel_id=1, source_target_pairs={{1,0},{2,1},{3,2},{4,3},{5,4},{6,5},{7,6},{9,8},{10,9},{11,10},{12... | collective-permute-start | bytes 393224 | tf_op jit(solution)/shard_map/ppermute | solution.py:25
  270.3 2.7 copy-start.5
  286.7 4.9 %collective-permute-start.24 = (bf16[4,64,1,256]{3,1,2,0:T(8,128)(2,1)S(1)}, bf16[4,64,1,256]{3,1,2,0:T(8,128)(2,1)S(1)}, u32[]{:S(2)}, u32[]{:S(2)}) collective-permute-start(bf16[4,64,1,256]{3,1,2,0:T(8,128)(2,1)S(1)} %get-tuple-element.111), channel_id=1, source_target_pairs={{0,1},{1,2},{2,3},{3,4},{4,5},{5,6},{6,7},{8,9},{9,10},{10,11},{11... | collective-permute-start | bytes 393224 | tf_op jit(solution)/shard_map/ppermute | solution.py:24
  288.8 6.3 %collective-permute-start.25 = (bf16[4,64,1,256]{3,1,2,0:T(8,128)(2,1)S(1)}, bf16[4,64,1,256]{3,1,2,0:T(8,128)(2,1)S(1)}, u32[]{:S(2)}, u32[]{:S(2)}) collective-permute-start(bf16[4,64,1,256]{3,1,2,0:T(8,128)(2,1)S(1)} %get-tuple-element.112), channel_id=1, source_target_pairs={{1,0},{2,1},{3,2},{4,3},{5,4},{6,5},{7,6},{9,8},{10,9},{11,10},{12... | collective-permute-start | bytes 393224 | tf_op jit(solution)/shard_map/ppermute | solution.py:25
  (3 other events, 3.0 us)
Sparse Core Ops, SparseCore 0:
  286.8 141.4 all-reduce.7
where the time goes:
time: 445 us; the launch traced here: 438 us
  blocking collectives  95.7 us (22%)
  waiting for transfers between devices  79.8 us (18%)
  local copies, waits for them, and re-layouts  76.6 us (17%)
  starting transfers between devices  69.2 us (16%)
  other arithmetic  59.8 us (13%)
  matrix products  34.5 us (8%)
  between operations  21.9 us (5%)
    psum x1, blocking collectives, local(): lax.psum((grad_first, grad_mid, grad_last, loss_share), ('group', 'dp', '...  62.8 us
    psum x1, waiting for transfers between devices, local(): lax.psum((grad_first, grad_mid, grad_last, loss_share), ('group', 'dp', '...  54.6 us
    ppermute x13, starting transfers between devices, with_halo(): after = lax.ppermute(initial, axis, down)  34.5 us
    all_gather x1, blocking collectives, local(): gathered = lax.all_gather(compact, ('group', 'dp'), axis=0, tiled=True)  32.9 us
    unnamed x92, local copies, waits for them, and re-layouts  28.8 us
    ppermute x13, starting transfers between devices, with_halo(): before = lax.ppermute(last, axis, up)  28.5 us
    concatenate x8, other arithmetic, with_halo(): shard = jnp.concatenate([before, shard, after], axis=dim)  19.1 us
    dot_general x54, matrix products, convolve(): jnp.einsum('oc,scxv->soxv', weight[kernel_index], window_part, preferred_...  13.7 us
  transfers between devices with their start and end apart: 28, of which 13 were waited for; matrix products, arithmetic and copies ran while one was open for 14% of the time, Pallas kernels for 0%

commit v1 on v0

v1 whole, which is shorter than its diff:
```python
import functools

import jax
import jax.numpy as jnp
from jax import lax
from jax.experimental import pallas as pl
from jax.experimental.pallas import tpu as pltpu
from jax.sharding import PartitionSpec as P

PE = 16
CELLS = PE * PE
LIVE_ROW = 2
HALO = 5
LANES = 128
ROWS = ("group", "dp")
EVERY = ("group", "dp", "space")
VIEWS = [(dz, dy) for dz in (-1, 0, 1) for dy in (-1, 0, 1)]
F32 = jnp.float32
BF16 = jnp.bfloat16


def lane_of(shape):
    return lax.broadcasted_iota(jnp.int32, shape, len(shape) - 1)


def roll(value, shift, axis=1):
    size = value.shape[axis]
    if isinstance(shift, int):
        shift = shift % size
        if shift == 0:
            return value
    return pltpu.roll(value, shift, axis)


def pack_kernel(vel, lo, hi):
    count = vel.shape[1]
    lane = lane_of((vel.shape[2], LANES))
    for c in range(3):
        first = jnp.zeros(lane.shape, F32)
        last = jnp.zeros(lane.shape, F32)
        for r in range(count):
            here = (lane >= HALO * r) & (lane < HALO * r + HALO)
            row = vel[c, r]
            first = jnp.where(here, roll(row, HALO * r), first)
            last = jnp.where(here, roll(row, HALO * r + HALO), last)
        lo[c] = first
        hi[c] = last


def corner_kernel(left, right, out):
    lane = lane_of((left.shape[1], LANES))
    wide = HALO * HALO
    for c in range(3):
        lhs = left[c]
        rhs = right[c]
        value = jnp.where((lane >= wide) & (lane < 2 * wide), roll(rhs, wide), lhs)
        out[c] = jnp.where((lane >= 2 * wide) & (lane < 3 * wide), roll(rhs, -wide), value)


def products(a, b, c):
    return [a * a, b * b, c * c, a * b, a * c, b * c]


def slab_kernel(vel, xlo, xhi, left, right, below, above, nxt, filt, stress, wa, wb):
    count = vel.shape[1]
    levels = vel.shape[2]
    lane = lane_of((levels, LANES))
    wide = HALO * HALO
    for c in range(3):
        for r in range(count + 2 * HALO):
            if r < HALO:
                main = xlo[c, r]
                lsrc, lat = below[c], 3 * wide + HALO * r
                rsrc, rat = below[c], 2 * wide + HALO * r
            elif r < count + HALO:
                q = r - HALO
                main = vel[c, q]
                lsrc, lat = left[c], HALO * q
                rsrc, rat = right[c], HALO * q
            else:
                q = r - HALO - count
                main = xhi[c, q]
                lsrc, lat = above[c], HALO * q
                rsrc, rat = above[c], wide + HALO * q
            wa[c, r, :, 0:LANES] = main
            wa[c, r, :, LANES:] = jnp.where(
                lane < 64, roll(rsrc, -rat), roll(lsrc, LANES - HALO - lat)
            )
    level = lax.broadcasted_iota(jnp.int32, (levels, 2 * LANES), 0)

    def step(src, dst, n):
        def body(r, carry):
            mids = [src[c, r + 1] for c in range(3)]
            for c in range(3):
                mid = mids[c]
                xp = src[c, r + 2]
                xm = src[c, r]
                yp = roll(mid, -1)
                ym = roll(mid, 1)
                zp = jnp.where(level == levels - 1, 0.0, roll(mid, -1, 0))
                zm = jnp.where(level == 0, 0.0, roll(mid, 1, 0))
                adv = mids[0] * (xp - xm) + mids[1] * (yp - ym) + mids[2] * (zp - zm)
                lap = (xp + xm) + (yp + ym) + (zp + zm) - 6.0 * mid
                dst[c, r] = mid + (0.005 * lap - 0.025 * adv)
            return carry

        lax.fori_loop(0, n, body, 0)

    step(wa, wb, count + 2 * HALO - 2)
    step(wb, wa, count + 2 * HALO - 4)
    for c in range(3):
        nxt[c] = wa[c, 3 : 3 + count, :, 0:LANES]
    tile = 8
    lanes = lane_of((tile, LANES))

    def along_x(rows):
        return (
            20.0 * rows[3]
            + 15.0 * (rows[2] + rows[4])
            + 6.0 * (rows[1] + rows[5])
            + (rows[0] + rows[6])
        )

    def along_y(f):
        m, e = f[:, :LANES], f[:, LANES:]
        rm, re = roll(m, -1), roll(e, -1)
        up_m = jnp.where(lanes == LANES - 1, re, rm)
        up_e = jnp.where(lanes == LANES - 1, rm, re)
        rm, re = roll(m, 1), roll(e, 1)
        dn_m = jnp.where(lanes == 0, re, rm)
        dn_e = jnp.where(lanes == 0, rm, re)
        far_up = jnp.where(
            lanes >= LANES - 2, roll(6.0 * e + up_e, -2), roll(6.0 * m + up_m, -2)
        )
        far_dn = jnp.where(lanes < 2, roll(6.0 * e + dn_e, 2), roll(6.0 * m + dn_m, 2))
        return (20.0 * m + 15.0 * (up_m + dn_m) + (far_up + far_dn)) * (1.0 / 4096.0)

    def filter_row(r, carry):
        for t in range(levels // tile):
            zs = slice(t * tile, (t + 1) * tile)
            rows = [[wa[c, r + k, zs, :] for k in range(7)] for c in range(3)]
            done = [along_y(along_x(rows[c])) for c in range(3)]
            for c in range(3):
                filt[c, r, zs, :] = done[c]
            small = products(*done)
            pairs = [(0, 0), (1, 1), (2, 2), (0, 1), (0, 2), (1, 2)]
            for i, (a, b) in enumerate(pairs):
                big = along_y(along_x([rows[a][k] * rows[b][k] for k in range(7)]))
                stress[i, r, zs, :] = big - small[i]
        return carry

    lax.fori_loop(0, count, filter_row, 0)


def views_of(halves, width):
    lane = lane_of(halves[0].shape)
    column = lane & (PE - 1)
    by_y = {
        0: halves,
        1: [jnp.where(column == PE - 1, 0.0, roll(h, -1)) for h in halves],
        -1: [jnp.where(column == 0, 0.0, roll(h, 1)) for h in halves],
    }
    out = []
    for dz, dy in VIEWS:
        a, b = by_y[dy]
        if dz == 0:
            out.append((a, b))
        elif dz == 1:
            ra, rb = roll(a, -PE), roll(b, -PE)
            inner = lane < LANES - PE
            out.append((jnp.where(inner, ra, rb), jnp.where(inner, rb, 0.0)))
        else:
            ra, rb = roll(a, PE), roll(b, PE)
            inner = lane >= PE
            out.append((jnp.where(inner, ra, 0.0), jnp.where(inner, rb, ra)))
    return out


def silu_parts(value):
    sigmoid = 1.0 / (1.0 + jnp.exp(-value))
    return value * sigmoid, sigmoid * (1.0 + value * (1.0 - sigmoid))


def dot_nn(a, b):
    return lax.dot_general(a, b, (((1,), (0,)), ((), ())), preferred_element_type=F32)


def dot_nt(a, b):
    return lax.dot_general(a, b, (((1,), (1,)), ((), ())), preferred_element_type=F32)


def cols(x, offset=0):
    return pl.ds(pl.multiple_of((x + offset) * CELLS, CELLS), CELLS)


def half_cols(x, half):
    return pl.ds(pl.multiple_of(x * CELLS + half * LANES, LANES), LANES)


def train_kernel(
    grad_scale, where, filt, stress, w1, w2, w2b, wl, wlt, out, src, tgt, xv, vv, yy, s1, s2, gs, acc
):
    live = where[0]

    @pl.when(live == 0)
    def _():
        out[...] = jnp.zeros(out.shape, F32)

    @pl.when(live != 0)
    def _():
        bx, bz, by, dest = where[1], where[2], where[3], where[4]
        src[...] = jnp.zeros(src.shape, F32)
        tgt[...] = jnp.zeros(tgt.shape, F32)
        lane16 = lane_of((PE, LANES)) // PE
        for f in range(9):
            ref, g = (filt, f) if f < 3 else (stress, f - 3)
            halves = [jnp.zeros((PE, LANES), F32)] * 2
            for z in range(PE):
                piece = ref[g, pl.ds(bx * 32 + bz + z, PE, stride=32), :]
                moved = roll(piece, lax.rem(PE * z - by + 2 * LANES, LANES))
                halves[z // 8] = jnp.where(lane16 == z % 8, moved, halves[z // 8])
            to = src if f < 3 else tgt
            for x in range(PE):
                for half in range(2):
                    at = x * CELLS + half * LANES
                    to[g : g + 1, at : at + LANES] = halves[half][x : x + 1, :]
        edge = jnp.zeros((yy.shape[0], CELLS), F32)
        yy[:, 0:CELLS] = edge
        yy[:, (PE + 1) * CELLS :] = edge

        def forward(x):
            return (
                yy[0:64, cols(x)] + yy[64:128, cols(x, 1)] + yy[128:192, cols(x, 2)]
            )

        def backward(x):
            return (
                yy[0:64, cols(x, 2)] + yy[64:128, cols(x, 1)] + yy[128:192, cols(x)]
            )

        def store_views(to, x, values, height):
            for k, pair in enumerate(views_of([values[:, :LANES], values[:, LANES:]], height)):
                for half in range(2):
                    to[height * k : height * (k + 1), half_cols(x, half)] = pair[half].astype(BF16)

        def input_views(x, carry):
            value = src[:, cols(x)].astype(BF16).astype(F32)
            for k, pair in enumerate(views_of([value[:, :LANES], value[:, LANES:]], 8)):
                for half in range(2):
                    xv[8 * k : 8 * (k + 1), half_cols(x, half)] = pair[half]
            return carry

        lax.fori_loop(0, PE, input_views, 0)

        def conv_a(x, carry):
            yy[:, cols(x, 1)] = dot_nn(w1[...], xv[:, cols(x)].astype(BF16))
            return carry

        lax.fori_loop(0, PE, conv_a, 0, unroll=2)

        def hidden_a(x, carry):
            hidden, slope = silu_parts(forward(x))
            s1[:, cols(x)] = slope
            store_views(vv, x, hidden.astype(BF16).astype(F32), 64)
            return carry

        lax.fori_loop(0, PE, hidden_a, 0)

        def conv_b(x, carry):
            yy[:, cols(x, 1)] = dot_nn(w2[...], vv[:, cols(x)])
            return carry

        lax.fori_loop(0, PE, conv_b, 0, unroll=2)

        none = jnp.zeros((64, CELLS), BF16)
        gs[0:64, (PE - 1) * CELLS :] = none
        gs[128:192, 0:CELLS] = none

        def last(x, carry):
            total, grad_last = carry
            hidden, slope = silu_parts(forward(x))
            hidden = hidden.astype(BF16)
            goal = tgt[:, cols(x)].astype(BF16).astype(F32)
            miss = dot_nn(wl[...], hidden) - goal
            total = total + miss * miss
            grad_pred = (miss * grad_scale).astype(BF16)
            grad_last = grad_last + dot_nt(grad_pred, hidden)
            grad = (dot_nn(wlt[...], grad_pred) * slope).astype(BF16)
            s2[:, cols(x)] = grad

            gs[64:128, cols(x)] = grad

            @pl.when(x > 0)
            def _():
                gs[0:64, cols(x, -1)] = grad

            @pl.when(x < PE - 1)
            def _():
                gs[128:192, cols(x, 1)] = grad

            return total, grad_last

        zero = (jnp.zeros((8, CELLS), F32), jnp.zeros((8, 64), F32))
        total, grad_last = lax.fori_loop(0, PE, last, zero)

        acc[...] = jnp.zeros(acc.shape, F32)
        span = 4 * CELLS

        def weight_b(i, carry):
            at = pl.ds(pl.multiple_of(i * span, span), span)
            acc[...] += dot_nt(gs[:, at], vv[:, at])
            return carry

        lax.fori_loop(0, PE * CELLS // span, weight_b, 0)

        def grad_views(x, carry):
            store_views(vv, x, s2[:, cols(x)].astype(F32), 64)
            return carry

        lax.fori_loop(0, PE, grad_views, 0)

        def conv_c(x, carry):
            yy[:, cols(x, 1)] = dot_nn(w2b[...], vv[:, cols(x)])
            return carry

        lax.fori_loop(0, PE, conv_c, 0, unroll=2)

        def first(x, carry):
            grad = (backward(x) * s1[:, cols(x)]).astype(BF16)
            gs[64:128, cols(x)] = grad

            @pl.when(x > 0)
            def _():
                gs[0:64, cols(x, -1)] = grad

            @pl.when(x < PE - 1)
            def _():
                gs[128:192, cols(x, 1)] = grad

            return carry

        lax.fori_loop(0, PE, first, 0)
        grad_first = dot_nt(xv[...].astype(BF16), gs[...])

        for i in range(24):
            for j in range(4):
                out[4 * i + j] = acc[8 * i : 8 * i + 8, LANES * j : LANES * (j + 1)]
        for i in range(12):
            out[96 + i] = jnp.concatenate(
                [acc[8 * i : 8 * i + 8, 512:576], acc[8 * i + 96 : 8 * i + 104, 512:576]], axis=1
            )
        for i in range(9):
            out[108 + i] = grad_first[8 * i : 8 * i + 8, 0:LANES]
        for i in range(5):
            j = min(i + 5, 8)
            out[117 + i] = jnp.concatenate(
                [grad_first[8 * i : 8 * i + 8, 128:192], grad_first[8 * j : 8 * j + 8, 128:192]],
                axis=1,
            )
        loss = jnp.sum(total) * (1.0 / (PE**3 * LIVE_ROW))
        corner = lane_of((8, LANES))
        deep = lax.broadcasted_iota(jnp.int32, (8, LANES), 0)
        padded = jnp.concatenate([grad_last, jnp.zeros((8, 64), F32)], axis=1)
        out[122] = jnp.where((deep == 7) & (corner == 64 + dest), loss, padded)
        for i in range(123, 128):
            out[i] = jnp.zeros((8, LANES), F32)


def unpack_kernel(where, parts, first, mid, last, loss):
    for dx in range(3):
        for t in range(8):
            i = 8 * dx + t
            for k in range(9):
                if k < 8:
                    block, half = parts[4 * i + k // 2], k % 2
                else:
                    block, half = parts[96 + i % 12], i // 12
                mid[9 * dx + k, 8 * t : 8 * t + 8, :] = block[:, 64 * half : 64 * half + 64]
    for k in range(9):
        tail = parts[117 + k % 5]
        half = k // 5
        wide = jnp.concatenate([parts[108 + k], tail[:, 64 * half : 64 * half + 64]], axis=1)
        turned = wide.T
        for dx in range(3):
            first[9 * dx + k] = turned[64 * dx : 64 * dx + 64, 0:3]
    final = parts[122]
    last[...] = final[0:6, 0:64]
    corner = lane_of((8, LANES))
    deep = lax.broadcasted_iota(jnp.int32, (8, LANES), 0)
    mine = (deep == 7) & (corner == 64 + where[5])
    loss[0] = jnp.sum(jnp.where(mine, final, 0.0))


def table_entry(table, row, col):
    hit = (jnp.arange(table.shape[0])[:, None] == row) & (jnp.arange(table.shape[1])[None] == col)
    return jnp.sum(jnp.where(hit, table, 0))


VMEM = pl.BlockSpec(memory_space=pltpu.VMEM)
SMEM = pl.BlockSpec(memory_space=pltpu.SMEM)


def params(mib):
    return pltpu.CompilerParams(vmem_limit_bytes=mib * 1024 * 1024)


def train_call(where, filt, stress, conv_first, conv_mid, conv_last, row_count):
    count, levels = filt.shape[1], filt.shape[2]
    w1 = conv_first.reshape(3, 9, 64, 3).transpose(0, 2, 1, 3)
    w1 = jnp.pad(w1, ((0, 0), (0, 0), (0, 0), (0, 5))).reshape(192, 72)
    by_k = conv_mid.reshape(3, 9, 64, 64)
    w2 = by_k.transpose(0, 2, 1, 3).reshape(192, 576)
    w2b = by_k[:, ::-1].transpose(0, 3, 1, 2).reshape(192, 576)
    wl = jnp.pad(conv_last, ((0, 2), (0, 0)))
    grad_scale = 2.0 / (PE**3 * row_count * LIVE_ROW)
    whole = PE * CELLS
    return pl.pallas_call(
        functools.partial(train_kernel, grad_scale),
        out_shape=jax.ShapeDtypeStruct((128, 8, LANES), F32),
        in_specs=[SMEM] + [VMEM] * 7,
        out_specs=VMEM,
        scratch_shapes=[
            pltpu.VMEM((8, whole), F32),
            pltpu.VMEM((8, whole), F32),
            pltpu.VMEM((72, whole), F32),
            pltpu.VMEM((576, whole), BF16),
            pltpu.VMEM((192, whole + 2 * CELLS), F32),
            pltpu.VMEM((64, whole), F32),
            pltpu.VMEM((64, whole), BF16),
            pltpu.VMEM((192, whole), BF16),
            pltpu.VMEM((192, 576), F32),
        ],
        compiler_params=params(48),
    )(
        where,
        filt.reshape(3, count * levels, LANES),
        stress.reshape(6, count * levels, LANES),
        w1,
        w2,
        w2b,
        wl,
        wl.T,
    )


def local(
    velocity, conv_first, conv_mid, conv_last, corner_x, corner_z, corner_y, patch_live, patch_dest
):
    row_count = patch_live.shape[0]
    my_row = lax.axis_index("group") * lax.axis_size("dp") + lax.axis_index("dp")
    my_col = lax.axis_index("space")
    _, count, levels, _ = velocity.shape
    strip = jax.ShapeDtypeStruct((3, levels, LANES), F32)
    up_row = [(i, (i + 1) % row_count) for i in range(row_count)]
    down_row = [(j, i) for i, j in up_row]
    cols_n = lax.axis_size("space")
    up_col = [(i, (i + 1) % cols_n) for i in range(cols_n)]
    down_col = [(j, i) for i, j in up_col]

    lo, hi = pl.pallas_call(
        pack_kernel, out_shape=(strip, strip), in_specs=[VMEM], out_specs=(VMEM, VMEM)
    )(velocity)
    left = lax.ppermute(hi, "space", up_col)
    right = lax.ppermute(lo, "space", down_col)
    xlo = lax.ppermute(velocity[:, count - HALO :], ROWS, up_row)
    xhi = lax.ppermute(velocity[:, :HALO], ROWS, down_row)
    corners = pl.pallas_call(
        corner_kernel, out_shape=strip, in_specs=[VMEM, VMEM], out_specs=VMEM
    )(left, right)
    below = lax.ppermute(corners, ROWS, up_row)
    above = lax.ppermute(corners, ROWS, down_row)
    wide = 2 * LANES
    nxt, filt, stress = pl.pallas_call(
        slab_kernel,
        out_shape=(
            jax.ShapeDtypeStruct(velocity.shape, F32),
            jax.ShapeDtypeStruct(velocity.shape, F32),
            jax.ShapeDtypeStruct((6,) + velocity.shape[1:], F32),
        ),
        in_specs=[VMEM] * 7,
        out_specs=(VMEM, VMEM, VMEM),
        scratch_shapes=[
            pltpu.VMEM((3, count + 2 * HALO, levels, wide), F32),
            pltpu.VMEM((3, count + 2 * HALO - 2, levels, wide), F32),
        ],
        compiler_params=params(32),
    )(velocity, xlo, xhi, left, right, below, above)

    tables = (patch_live, corner_x, corner_z, corner_y, patch_dest)
    where = jnp.stack([table_entry(t, my_row, my_col) for t in tables] + [my_row]).astype(jnp.int32)
    parts = train_call(where, filt, stress, conv_first, conv_mid, conv_last, row_count)

    shares = lax.all_to_all(parts, EVERY, 0, 0, tiled=True)
    mine = jnp.sum(shares, axis=0, keepdims=True)
    summed = lax.all_to_all(jnp.broadcast_to(mine, parts.shape), EVERY, 0, 0, tiled=True)
    grad_first, grad_mid, grad_last, loss = pl.pallas_call(
        unpack_kernel,
        out_shape=(
            jax.ShapeDtypeStruct((27, 64, 3), F32),
            jax.ShapeDtypeStruct((27, 64, 64), F32),
            jax.ShapeDtypeStruct((6, 64), F32),
            jax.ShapeDtypeStruct((1,), F32),
        ),
        in_specs=[SMEM, VMEM],
        out_specs=(VMEM, VMEM, VMEM, SMEM),
        compiler_params=params(16),
    )(where, summed)
    return (nxt, filt, stress, grad_first, grad_mid, grad_last, loss)


def solution(mesh):
    block = P(None, ("group", "dp"), None, "space")
    in_specs = (block,) + (P(),) * 8
    out_specs = (block, block, block, P(), P(), P(), P(("group", "dp")))
    return jax.shard_map(local, mesh=mesh, in_specs=in_specs, out_specs=out_specs, check_vma=False)
```

time: 445 us -> 146 us (0.33); the launches traced: 438 us -> 146 us
  waiting for transfers between devices: 79.8 us -> 0.02 us
  local copies, waits for them, and re-layouts: 76.6 us -> 16.8 us
  other arithmetic: 59.8 us -> 0.99 us
  starting transfers between devices: 69.2 us -> 13.4 us
  Pallas kernels: 0 us -> 47.1 us
  matrix products: 34.5 us -> 0 us
  blocking collectives: 95.7 us -> 67.2 us
  between operations: 21.9 us -> 0.9 us
    all_to_all x0 -> x2, blocking collectives: none -> 67.2 us  [the longest x1 49.5 us: local(): shares = lax.all_to_all(parts, EVERY, 0, 0, tiled=True)]
    psum x1 -> x0, blocking collectives: 62.8 us -> none  [local(): lax.psum((grad_first, grad_mid, grad_last, loss_share), ('group', 'dp', '...]
    psum x1 -> x0, waiting for transfers between devices: 54.6 us -> none  [local(): lax.psum((grad_first, grad_mid, grad_last, loss_share), ('group', 'dp', '...]
    ppermute x26 -> x6, starting transfers between devices: 63 us -> 13.4 us  [the longest x1 5.95 us: local(): xhi = lax.ppermute(velocity[:, :HALO], ROWS, down_row)]
    pallas_call x0 -> x5, Pallas kernels: none -> 47.1 us  [the longest x1 40.7 us: local(): pl.pallas_call(slab_kernel, out_shape=(jax.ShapeDtypeStruct(velocity.shap...]
    dot_general x138 -> x0, matrix products: 34.5 us -> none  [the longest x54 13.7 us: convolve(): jnp.einsum('oc,scxv->soxv', weight[kernel_index], window_part, preferred_...]
    all_gather x1 -> x0, blocking collectives: 32.9 us -> none  [local(): gathered = lax.all_gather(compact, ('group', 'dp'), axis=0, tiled=True)]
    ppermute x10 -> x0, local copies, waits for them, and re-layouts: 24.2 us -> none  [the longest x5 13.1 us: with_halo(): after = lax.ppermute(initial, axis, down)]
  transfers between devices with their start and end apart: 28 -> 6, of which waited for: 13 -> 0; matrix products, arithmetic and copies ran while one was open for 14% -> 9% of each run, Pallas kernels for 0% -> 1%
where the time goes in v1:
time: 146 us
  blocking collectives  67.2 us (46%)
  Pallas kernels  47.1 us (32%)
  local copies, waits for them, and re-layouts  16.8 us (12%)
  starting transfers between devices  13.4 us (9%)
    all_to_all x1, blocking collectives, local(): shares = lax.all_to_all(parts, EVERY, 0, 0, tiled=True)  49.5 us
    pallas_call x1, Pallas kernels, local(): pl.pallas_call(slab_kernel, out_shape=(jax.ShapeDtypeStruct(velocity.shap...  40.7 us
    all_to_all x1, blocking collectives, local(): lax.all_to_all(jnp.broadcast_to(mine, parts.shape), EVERY, 0, 0, tiled=True)  17.7 us
    unnamed x33, local copies, waits for them, and re-layouts  6.55 us
    ppermute x1, starting transfers between devices, local(): xhi = lax.ppermute(velocity[:, :HALO], ROWS, down_row)  5.95 us
    ppermute x1, starting transfers between devices, local(): above = lax.ppermute(corners, ROWS, down_row)  4.78 us
    another operation x1, local copies, waits for them, and re-layouts, local(): jnp.stack([table_entry(t, my_row, my_col) for t in tables] + [my_row])  3.2 us
  transfers between devices with their start and end apart: 6, of which 0 were waited for; matrix products, arithmetic and copies ran while one was open for 9% of the time, Pallas kernels for 1%

profile of v1, /device:TPU:1, one launch (start us, length us, event | category | flops | bytes accessed | tf_op | source)
XLA Modules:
  0.0 146.4 jit_solution(12193369636951809509)
XLA Ops:
  0.6 0.0 copy-start.7
  0.6 0.0 copy-start.8
  0.7 0.0 copy-start.12
  0.7 0.0 copy-start.9
  0.7 0.0 copy-start.10
  0.7 0.0 copy-start.11
  0.7 0.0 copy-start.13
  0.7 2.4 %shard_map.144 = (f32[3,32,128]{2,1,0:T(8,128)}, f32[3,32,128]{2,1,0:T(8,128)}) custom-call(f32[3,20,32,128]{3,2,1,0:T(8,128)} %vel.3), custom_call_target="tpu_custom_call" | custom-call | tf_op jit(solution)/shard_map/pallas_call | solution.py:460
  3.1 2.7 %collective-permute-start.2 = (f32[3,32,128]{2,1,0:T(8,128)}, f32[3,32,128]{2,1,0:T(8,128)S(1)}, u32[]{:S(2)}, u32[]{:S(2)}) collective-permute-start(f32[3,32,128]{2,1,0:T(8,128)} %get-tuple-element.16), channel_id=1, source_target_pairs={{0,1},{1,2},{2,3},{3,4},{4,5},{5,6},{6,7},{7,0},{8,9},{9,10},{10,1... | collective-permute-start | bytes 147464 | tf_op jit(solution)/shard_map/ppermute | solution.py:463
  5.8 0.0 collective-permute-start.3
  5.8 1.8 %fusion.5 = (f32[3,5,32,128]{3,2,1,0:T(8,128)}, f32[3,5,32,128]{3,2,1,0:T(8,128)S(1)}) fusion(f32[3,20,32,128]{3,2,1,0:T(8,128)} %vel.3), kind=kLoop, calls=%fused_computation.14 | loop fusion | bytes 983040 | tf_op jit(solution)/shard_map/slice | solution.py:466
  7.6 6.0 %collective-permute-start.1 = (f32[3,5,32,128]{3,2,1,0:T(8,128)}, f32[3,5,32,128]{3,2,1,0:T(8,128)S(1)}, u32[]{:S(2)}, u32[]{:S(2)}) collective-permute-start(f32[3,5,32,128]{3,2,1,0:T(8,128)} %get-tuple-element.44), channel_id=1, source_target_pairs={{8,0},{16,8},{24,16},{32,24},{40,32},{48,40},{56,48},{64,56},{72,6... | collective-permute-start | bytes 737288 | tf_op jit(solution)/shard_map/ppermute | solution.py:466
  13.6 0.0 collective-permute-start
  13.6 0.0 copy-done.7
  13.6 0.4 copy.25
  14.0 0.2 reverse_bitcast_fusion
  14.2 0.0 copy-done.8
  14.2 0.0 copy-done.12
  14.2 0.0 copy-done.9
  14.3 0.0 copy-done.10
  14.3 0.0 copy-done.11
  14.3 0.8 fusion.4
  15.1 0.0 copy-done.13
  15.1 0.1 copy.26
  15.2 0.0 collective-permute-done.2.left
  15.2 0.0 copy-start.3
  15.2 0.0 collective-permute-done.3.right
  15.3 0.6 copy-done.3
  15.9 0.0 copy-start.5
  15.9 0.6 copy-done.5
  16.5 1.5 %shard_map.145 = f32[3,32,128]{2,1,0:T(8,128)} custom-call(f32[3,32,128]{2,1,0:T(8,128)} %copy-done.3, f32[3,32,128]{2,1,0:T(8,128)} %copy-done.5), custom_call_target="tpu_custom_call" | custom-call | tf_op jit(solution)/shard_map/pallas_call | solution.py:467
  18.0 4.8 %collective-permute-start.5 = (f32[3,32,128]{2,1,0:T(8,128)}, f32[3,32,128]{2,1,0:T(8,128)S(1)}, u32[]{:S(2)}, u32[]{:S(2)}) collective-permute-start(f32[3,32,128]{2,1,0:T(8,128)} %shard_map.145), channel_id=1, source_target_pairs={{8,0},{16,8},{24,16},{32,24},{40,32},{48,40},{56,48},{64,56},{72,6... | collective-permute-start | bytes 147464 | tf_op jit(solution)/shard_map/ppermute | solution.py:471
  22.8 0.0 collective-permute-start.4
  22.8 0.7 copy.33
  23.5 0.0 copy-start.4
  23.5 0.0 copy-start.6
  23.5 0.9 copy.24
  24.4 0.8 copy.22
  25.2 0.7 pad.9.clone.wl
  25.9 0.1 reshape.49
  26.0 0.1 copy.27.w1
  26.1 1.1 reshape.52
  27.2 1.1 copy.29.w2b
  28.3 0.4 reshape.51
  28.7 0.2 copy.28.w2
  28.9 3.2 %stack.27.where = s32[6]{0:T(128)S(1)} concatenate(s32[1]{0:T(128)} %bitcast, s32[1]{0:T(128)} %bitcast.1, s32[1]{0:T(128)} %bitcast.2, s32[1]{0:T(128)} %bitcast.3, s32[1]{0:T(128)} %bitcast.4, s32[1]{0:T(128)} %bitcast.5), dimensions={0} | concatenate | bytes 48 | tf_op jit(solution)/shard_map/stack | solution.py:490
  32.1 0.0 collective-permute-done.5.above
  32.1 0.0 collective-permute-done.4.below
  32.1 0.0 collective-permute-done.1.xhi
  32.1 0.0 collective-permute-done.xlo
  32.1 0.0 copy-done
  32.1 0.0 copy-done.4
  32.1 0.0 copy-done.6
  32.1 40.7 %shard_map.146 = (f32[3,20,32,128]{3,2,1,0:T(8,128)}, f32[3,20,32,128]{3,2,1,0:T(8,128)}, f32[6,20,32,128]{3,2,1,0:T(8,128)}) custom-call(f32[3,20,32,128]{3,2,1,0:T(8,128)S(1)} %copy-done, f32[3,5,32,128]{3,2,1,0:T(8,128)S(1)} %collective-permute-done.xlo, f32[3,5,32,128]{3,2,1,0:T(8,128)S(1)} %collective-permute-done.1.xhi, f32[3,32,128]{2,1,0:T(8,128)S(1)} %copy-done.4, ...), custom_call_target="tpu_custom_call" | custom-call | tf_op jit(solution)/shard_map/pallas_call | solution.py:473
  72.8 0.0 copy-start.1
  72.8 1.5 %copy-done.1 = f32[6,20,32,128]{3,2,1,0:T(8,128)S(1)} copy-done((f32[6,20,32,128]{3,2,1,0:T(8,128)S(1)}, f32[6,20,32,128]{3,2,1,0:T(8,128)}, u32[]{:S(2)}) %copy-start.1) | copy-done | bytes 1966104
  74.4 0.0 copy-start.2
  74.4 1.2 copy-done.2
  75.6 0.6 shard_map.147
  76.2 49.5 %all_to_all.10 = f32[128,8,128]{2,1,0:T(8,128)S(1)} all-to-all(f32[128,8,128]{2,1,0:T(8,128)S(1)} %shard_map.147), channel_id=1, replica_groups=mesh['group'=2,'dp'=8,'space'=8] {'group','dp','space'}, dimensions={0} | all-to-all | bytes 1048576 | tf_op jit(solution)/shard_map/all_to_all | solution.py:493
  125.7 0.1 reduce_sum.59
  125.9 17.7 %all_to_all.11.parts = f32[128,8,128]{2,1,0:T(8,128)S(1)} all-to-all(f32[128,8,128]{2,1,0:T(8,128)S(1)} %broadcast_in_dim.11), channel_id=1, replica_groups=mesh['group'=2,'dp'=8,'space'=8] {'group','dp','space'}, dimensions={0} | all-to-all | bytes 1048576 | tf_op jit(solution)/shard_map/all_to_all | solution.py:495
  143.6 1.9 %shard_map.148 = (f32[27,64,3]{2,1,0:T(8,128)S(1)}, f32[27,64,64]{2,1,0:T(8,128)}, f32[6,64]{1,0:T(8,128)}, f32[1]{0:T(128)}) custom-call(s32[6]{0:T(128)S(1)} %stack.27.where, f32[128,8,128]{2,1,0:T(8,128)S(1)} %all_to_all.11.parts), custom_call_target="tpu_custom_call" | custom-call | tf_op jit(solution)/shard_map/pallas_call | solution.py:496
  145.4 1.0 copy.31
  (7 shorter events, 0.1 us)
Async XLA Ops:
  0.6 13.0 %copy-start.7 = (bf16[27,64,64]{2,1,0:T(8,128)(2,1)S(1)}, bf16[27,64,64]{2,1,0:T(8,128)(2,1)}, u32[]{:S(2)}) copy-start(bf16[27,64,64]{2,1,0:T(8,128)(2,1)} %param.11) | copy-start | bytes 663556
  0.6 13.6 %copy-start.8 = (s32[16,8]{0,1:T(8,128)S(1)}, s32[16,8]{0,1:T(8,128)}, u32[]{:S(2)}) copy-start(s32[16,8]{0,1:T(8,128)} %param.17) | copy-start | bytes 1540
  0.7 13.6 %copy-start.12 = (s32[16,8]{0,1:T(8,128)S(1)}, s32[16,8]{0,1:T(8,128)}, u32[]{:S(2)}) copy-start(s32[16,8]{0,1:T(8,128)} %param.16) | copy-start | bytes 1540
  0.7 13.6 %copy-start.9 = (s32[16,8]{0,1:T(8,128)S(1)}, s32[16,8]{0,1:T(8,128)}, u32[]{:S(2)}) copy-start(s32[16,8]{0,1:T(8,128)} %param.15) | copy-start | bytes 1540
  0.7 13.6 %copy-start.10 = (s32[16,8]{0,1:T(8,128)S(1)}, s32[16,8]{0,1:T(8,128)}, u32[]{:S(2)}) copy-start(s32[16,8]{0,1:T(8,128)} %param.14) | copy-start | bytes 1540
  0.7 13.6 %copy-start.11 = (s32[16,8]{0,1:T(8,128)S(1)}, s32[16,8]{0,1:T(8,128)}, u32[]{:S(2)}) copy-start(s32[16,8]{0,1:T(8,128)} %param.13) | copy-start | bytes 1540
  0.7 14.4 %copy-start.13 = (bf16[6,64]{1,0:T(8,128)(2,1)S(1)}, bf16[6,64]{1,0:T(8,128)(2,1)}, u32[]{:S(2)}) copy-start(bf16[6,64]{1,0:T(8,128)(2,1)} %param.12) | copy-start | bytes 2308
  3.1 12.1 %collective-permute-start.2 = (f32[3,32,128]{2,1,0:T(8,128)}, f32[3,32,128]{2,1,0:T(8,128)S(1)}, u32[]{:S(2)}, u32[]{:S(2)}) collective-permute-start(f32[3,32,128]{2,1,0:T(8,128)} %get-tuple-element.16), channel_id=1, source_target_pairs={{0,1},{1,2},{2,3},{3,4},{4,5},{5,6},{6,7},{7,0},{8,9},{9,10},{10,1... | collective-permute-start | bytes 147464 | tf_op jit(solution)/shard_map/ppermute | solution.py:463
  5.8 9.4 %collective-permute-start.3 = (f32[3,32,128]{2,1,0:T(8,128)}, f32[3,32,128]{2,1,0:T(8,128)S(1)}, u32[]{:S(2)}, u32[]{:S(2)}) collective-permute-start(f32[3,32,128]{2,1,0:T(8,128)} %get-tuple-element.17), channel_id=1, source_target_pairs={{1,0},{2,1},{3,2},{4,3},{5,4},{6,5},{7,6},{0,7},{9,8},{10,9},{11,1... | collective-permute-start | bytes 147464 | tf_op jit(solution)/shard_map/ppermute | solution.py:464
  7.6 24.5 %collective-permute-start.1 = (f32[3,5,32,128]{3,2,1,0:T(8,128)}, f32[3,5,32,128]{3,2,1,0:T(8,128)S(1)}, u32[]{:S(2)}, u32[]{:S(2)}) collective-permute-start(f32[3,5,32,128]{3,2,1,0:T(8,128)} %get-tuple-element.44), channel_id=1, source_target_pairs={{8,0},{16,8},{24,16},{32,24},{40,32},{48,40},{56,48},{64,56},{72,6... | collective-permute-start | bytes 737288 | tf_op jit(solution)/shard_map/ppermute | solution.py:466
  13.6 18.5 %collective-permute-start = (f32[3,5,32,128]{3,2,1,0:T(8,128)S(1)}, f32[3,5,32,128]{3,2,1,0:T(8,128)S(1)}, u32[]{:S(2)}, u32[]{:S(2)}) collective-permute-start(f32[3,5,32,128]{3,2,1,0:T(8,128)S(1)} %get-tuple-element.45), channel_id=1, source_target_pairs={{0,8},{8,16},{16,24},{24,32},{32,40},{40,48},{48,56},{56,64},{64,7... | collective-permute-start | bytes 737288 | tf_op jit(solution)/shard_map/ppermute | solution.py:465
  15.2 0.6 copy-start.3
  15.9 0.6 copy-start.5
  18.0 14.1 %collective-permute-start.5 = (f32[3,32,128]{2,1,0:T(8,128)}, f32[3,32,128]{2,1,0:T(8,128)S(1)}, u32[]{:S(2)}, u32[]{:S(2)}) collective-permute-start(f32[3,32,128]{2,1,0:T(8,128)} %shard_map.145), channel_id=1, source_target_pairs={{8,0},{16,8},{24,16},{32,24},{40,32},{48,40},{56,48},{64,56},{72,6... | collective-permute-start | bytes 147464 | tf_op jit(solution)/shard_map/ppermute | solution.py:471
  22.8 9.3 %collective-permute-start.4 = (f32[3,32,128]{2,1,0:T(8,128)}, f32[3,32,128]{2,1,0:T(8,128)S(1)}, u32[]{:S(2)}, u32[]{:S(2)}) collective-permute-start(f32[3,32,128]{2,1,0:T(8,128)} %shard_map.145), channel_id=1, source_target_pairs={{0,8},{8,16},{16,24},{24,32},{32,40},{40,48},{48,56},{56,64},{64,7... | collective-permute-start | bytes 147464 | tf_op jit(solution)/shard_map/ppermute | solution.py:470
  23.5 8.6 %copy-start = (f32[3,20,32,128]{3,2,1,0:T(8,128)S(1)}, f32[3,20,32,128]{3,2,1,0:T(8,128)}, u32[]{:S(2)}) copy-start(f32[3,20,32,128]{3,2,1,0:T(8,128)} %vel.3) | copy-start | bytes 2949124
  23.5 8.7 %copy-start.4 = (f32[3,32,128]{2,1,0:T(8,128)S(1)}, f32[3,32,128]{2,1,0:T(8,128)}, u32[]{:S(2)}) copy-start(f32[3,32,128]{2,1,0:T(8,128)} %copy-done.3) | copy-start | bytes 147460
  23.5 8.7 %copy-start.6 = (f32[3,32,128]{2,1,0:T(8,128)S(1)}, f32[3,32,128]{2,1,0:T(8,128)}, u32[]{:S(2)}) copy-start(f32[3,32,128]{2,1,0:T(8,128)} %copy-done.5) | copy-start | bytes 147460
  72.8 1.5 %copy-start.1 = (f32[6,20,32,128]{3,2,1,0:T(8,128)S(1)}, f32[6,20,32,128]{3,2,1,0:T(8,128)}, u32[]{:S(2)}) copy-start(f32[6,20,32,128]{3,2,1,0:T(8,128)} %get-tuple-element.34) | copy-start | bytes 5898244
  74.4 1.2 copy-start.2

commit v2 on v1

v2 whole, which is shorter than its diff:
```python
import functools

import jax
import jax.numpy as jnp
from jax import lax
from jax.experimental import pallas as pl
from jax.experimental.pallas import tpu as pltpu
from jax.sharding import PartitionSpec as P

PE = 16
CELLS = PE * PE
LIVE_ROW = 2
HALO = 5
WINDOW = 32
PAIRS = [(0, 0), (1, 1), (2, 2), (0, 1), (0, 2), (1, 2)]
LANES = 128
ROWS = ("group", "dp")
EVERY = ("group", "dp", "space")
VIEWS = [(dz, dy) for dz in (-1, 0, 1) for dy in (-1, 0, 1)]
F32 = jnp.float32
BF16 = jnp.bfloat16


def lane_of(shape):
    return lax.broadcasted_iota(jnp.int32, shape, len(shape) - 1)


def roll(value, shift, axis=1):
    size = value.shape[axis]
    if isinstance(shift, int):
        shift = shift % size
        if shift == 0:
            return value
    return pltpu.roll(value, shift, axis)


def pack_kernel(vel, lo, hi):
    count = vel.shape[1]
    lane = lane_of((vel.shape[2], LANES))
    for c in range(3):
        first = jnp.zeros(lane.shape, F32)
        last = jnp.zeros(lane.shape, F32)
        for r in range(count):
            here = (lane >= HALO * r) & (lane < HALO * r + HALO)
            row = vel[c, r]
            first = jnp.where(here, roll(row, HALO * r), first)
            last = jnp.where(here, roll(row, HALO * r + HALO), last)
        lo[c] = first
        hi[c] = last


def faces(vel, left, right, up, down):
    count = vel.shape[1]
    lane = lane_of((left.shape[1], LANES))
    wide = HALO * HALO
    for c in range(3):
        lhs = left[c]
        rhs = right[c]
        up[c, 0:HALO] = vel[c, count - HALO :]
        down[c, 0:HALO] = vel[c, 0:HALO]
        at = HALO * (count - HALO)
        up[c, HALO] = jnp.where(lane < wide, roll(lhs, -at), roll(rhs, wide - at))
        down[c, HALO] = jnp.where(lane < wide, lhs, roll(rhs, wide))


def products(a, b, c):
    return [a * a, b * b, c * c, a * b, a * c, b * c]


def along_x(rows):
    return (
        20.0 * rows[3]
        + 15.0 * (rows[2] + rows[4])
        + 6.0 * (rows[1] + rows[5])
        + (rows[0] + rows[6])
    )


def solver_kernel(vel, xlo, xhi, left, right, nxt, wide_next, wa, wb):
    count = vel.shape[1]
    levels = vel.shape[2]
    lane = lane_of((levels, LANES))
    wide = HALO * HALO
    for c in range(3):
        for r in range(count + 2 * HALO):
            if r < HALO:
                main = xlo[c, r]
                lsrc, lat = xlo[c, HALO], HALO * r
                rsrc, rat = xlo[c, HALO], wide + HALO * r
            elif r < count + HALO:
                q = r - HALO
                main = vel[c, q]
                lsrc, lat = left[c], HALO * q
                rsrc, rat = right[c], HALO * q
            else:
                q = r - HALO - count
                main = xhi[c, q]
                lsrc, lat = xhi[c, HALO], HALO * q
                rsrc, rat = xhi[c, HALO], wide + HALO * q
            wa[c, r, :, 0:LANES] = main
            wa[c, r, :, LANES:] = jnp.where(
                lane < 64, roll(rsrc, -rat), roll(lsrc, LANES - HALO - lat)
            )
    level = lax.broadcasted_iota(jnp.int32, (levels, 2 * LANES), 0)

    def step(src, dst, n):
        def body(r, carry):
            mids = [src[c, r + 1] for c in range(3)]
            for c in range(3):
                mid = mids[c]
                xp = src[c, r + 2]
                xm = src[c, r]
                yp = roll(mid, -1)
                ym = roll(mid, 1)
                zp = jnp.where(level == levels - 1, 0.0, roll(mid, -1, 0))
                zm = jnp.where(level == 0, 0.0, roll(mid, 1, 0))
                adv = mids[0] * (xp - xm) + mids[1] * (yp - ym) + mids[2] * (zp - zm)
                lap = (xp + xm) + (yp + ym) + (zp + zm) - 6.0 * mid
                dst[c, r] = mid + (0.005 * lap - 0.025 * adv)
            return carry

        lax.fori_loop(0, n, body, 0)

    step(wa, wb, count + 2 * HALO - 2)
    step(wb, wide_next, count + 2 * HALO - 4)
    for c in range(3):
        nxt[c] = wide_next[c, 3 : 3 + count, :, 0:LANES]


def filter_kernel(wa, filt, stress):
    count = filt.shape[1]
    levels = filt.shape[2]
    tile = 8
    lanes = lane_of((tile, LANES))

    def along_y(f):
        m, e = f[:, :LANES], f[:, LANES:]

        def tap(k):
            outside = (lanes >= LANES - k) if k > 0 else (lanes < -k)
            return jnp.where(outside, roll(e, -k), roll(m, -k))

        near = 15.0 * (tap(1) + tap(-1)) + 6.0 * (tap(2) + tap(-2))
        return (20.0 * m + near + (tap(3) + tap(-3))) * (1.0 / 4096.0)

    def filter_row(r, carry):
        for t in range(levels // tile):
            zs = slice(t * tile, (t + 1) * tile)
            rows = [[wa[c, r + k, zs, :] for k in range(7)] for c in range(3)]
            done = [along_y(along_x(rows[c])) for c in range(3)]
            for c in range(3):
                filt[c, r, zs, :] = done[c]
            small = products(*done)
            for i, (a, b) in enumerate(PAIRS):
                big = along_y(along_x([rows[a][k] * rows[b][k] for k in range(7)]))
                stress[i, r, zs, :] = big - small[i]
        return carry

    lax.fori_loop(0, count, filter_row, 0)


def window_row(main, left, right, r, begin):
    lane = lane_of((8, LANES))
    col = (lane & (WINDOW - 1)) + (begin - HALO)
    out = jnp.zeros((8, LANES), F32)
    for t in range(4):
        zs = slice(8 * t, 8 * t + 8)
        base = 2 * LANES + WINDOW * t - begin
        a = roll(main[zs], lax.rem(base + HALO, LANES))
        b = roll(left[zs], lax.rem(base - HALO * r, LANES))
        c = roll(right[zs], lax.rem(base + LANES + HALO - HALO * r, LANES))
        value = jnp.where(col < 0, b, jnp.where(col >= LANES, c, a))
        out = jnp.where(lane // WINDOW == t, value, out)
    return out


def edge_kernel(rows, tables, vel, left, right, up, down):
    col = lax.axis_index("space")
    row = lax.axis_index("group") * lax.axis_size("dp") + lax.axis_index("dp")
    count = vel.shape[1]
    begin_up = tables[4, lax.rem(row + 1, rows), col]
    begin_down = tables[4, lax.rem(row + rows - 1, rows), col]
    for c in range(3):
        for k in range(HALO):
            r = count - HALO + k
            up[c, k] = window_row(vel[c, r], left[c], right[c], r, begin_up)
            down[c, k] = window_row(vel[c, k], left[c], right[c], k, begin_down)


def own_kernel(tables, vel, left, right, out, up, down):
    col = lax.axis_index("space")
    row = lax.axis_index("group") * lax.axis_size("dp") + lax.axis_index("dp")
    begin = tables[4, row, col]

    def body(r, carry):
        for c in range(3):
            out[c, r] = window_row(vel[c, r], left[c], right[c], r, begin)
        return carry

    lax.fori_loop(0, vel.shape[1], body, 0, unroll=4)
    faces(vel, left, right, up, down)


def window_fields(bx, own, wlo, whi, wa, wb, wc, fields):
    count = own.shape[1]
    wa[:, 0:HALO] = wlo[...]
    wa[:, HALO : HALO + count] = own[...]
    wa[:, HALO + count :] = whi[...]
    lane = lane_of((8, LANES))
    level = lax.broadcasted_iota(jnp.int32, (8, LANES), 0)

    def step(src, dst, base, n):
        for r in range(n):
            mids = [src[c, base + r + 1] for c in range(3)]
            for c in range(3):
                mid = mids[c]
                xp = src[c, base + r + 2]
                xm = src[c, base + r]
                yp = roll(mid, -1)
                ym = roll(mid, 1)
                zp = roll(mid, -1, 0)
                zp = jnp.where(
                    level == 7, jnp.where(lane >= 3 * WINDOW, 0.0, roll(zp, -WINDOW)), zp
                )
                zm = roll(mid, 1, 0)
                zm = jnp.where(level == 0, jnp.where(lane < WINDOW, 0.0, roll(zm, WINDOW)), zm)
                adv = mids[0] * (xp - xm) + mids[1] * (yp - ym) + mids[2] * (zp - zm)
                lap = (xp + xm) + (yp + ym) + (zp + zm) - 6.0 * mid
                dst[c, r] = mid + (0.005 * lap - 0.025 * adv)

    step(wa, wb, bx, PE + 8)
    step(wb, wc, 0, PE + 6)

    def along_y(f):
        near = 15.0 * (roll(f, -1) + roll(f, 1)) + 6.0 * (roll(f, -2) + roll(f, 2))
        return (20.0 * f + near + (roll(f, -3) + roll(f, 3))) * (1.0 / 4096.0)

    for r in range(PE):
        rows = [[wc[c, r + k] for k in range(7)] for c in range(3)]
        done = [along_y(along_x(rows[c])) for c in range(3)]
        at = slice(r * 8, r * 8 + 8)
        for c in range(3):
            fields[c, at] = done[c]
        small = products(*done)
        for i, (a, b) in enumerate(PAIRS):
            big = along_y(along_x([rows[a][k] * rows[b][k] for k in range(7)]))
            fields[3 + i, at] = big - small[i]


def views_of(even, odd):
    lane = lane_of(even.shape)
    column = lane & (PE - 1)
    none = jnp.zeros_like(even)
    by_y = {
        0: (even, odd),
        1: tuple(jnp.where(column == PE - 1, none, roll(h, -1)) for h in (even, odd)),
        -1: tuple(jnp.where(column == 0, none, roll(h, 1)) for h in (even, odd)),
    }
    by_z = {}
    for dy, (a, b) in by_y.items():
        by_z[0, dy] = (a, b)
        by_z[1, dy] = (b, jnp.where(lane >= LANES - PE, none, roll(a, -PE)))
        by_z[-1, dy] = (jnp.where(lane < PE, none, roll(b, PE)), a)
    return [by_z[view] for view in VIEWS]


def silu_parts(value):
    sigmoid = 0.5 * jnp.tanh(0.5 * value) + 0.5
    return value * sigmoid, sigmoid * (1.0 + value * (1.0 - sigmoid))


def dot_nn(a, b):
    return lax.dot_general(a, b, (((1,), (0,)), ((), ())), preferred_element_type=F32)


def dot_nt(a, b):
    return lax.dot_general(a, b, (((1,), (1,)), ((), ())), preferred_element_type=F32)


def cols(x, offset=0):
    return slice((x + offset) * CELLS, (x + offset + 1) * CELLS)


def half_cols(x, half):
    return slice(x * CELLS + half * LANES, x * CELLS + half * LANES + LANES)


def store_views(to, x, values, height):
    for k, pair in enumerate(views_of(values[:, :LANES], values[:, LANES:])):
        for half in range(2):
            to[height * k : height * (k + 1), half_cols(x, half)] = pair[half]


def train_kernel(
    grad_scale,
    tables,
    own,
    wlo,
    whi,
    w1,
    w2,
    w2b,
    wl,
    wlt,
    out,
    wa,
    wb,
    wc,
    fields,
    src,
    tgt,
    xv,
    vv,
    gv,
    ya,
    yb,
    s1,
    gs,
    acc,
):
    col = lax.axis_index("space")
    row = lax.axis_index("group") * lax.axis_size("dp") + lax.axis_index("dp")
    live = tables[0, row, col]

    @pl.when(live == 0)
    def _():
        out[...] = jnp.zeros(out.shape, F32)

    @pl.when(live != 0)
    def _():
        bx, bz, dest = tables[1, row, col], tables[2, row, col], tables[3, row, col]
        window_fields(bx, own, wlo, whi, wa, wb, wc, fields)
        src[...] = jnp.zeros(src.shape, F32)
        tgt[...] = jnp.zeros(tgt.shape, F32)
        lane16 = lane_of((PE, LANES)) // PE
        for f in range(9):
            halves = [jnp.zeros((PE, LANES), F32)] * 2
            for z in range(PE):
                deep = bz + z
                piece = fields[f, pl.ds(lax.rem(deep, 8), PE, stride=8), :]
                from_lane = HALO + WINDOW * (deep // 8)
                moved = roll(piece, lax.rem(PE * (z // 2) - from_lane + 2 * LANES, LANES))
                halves[z % 2] = jnp.where(lane16 == z // 2, moved, halves[z % 2])
            to, g = (src, f) if f < 3 else (tgt, f - 3)
            for half in range(2):
                to[half, PE * g : PE * g + PE] = halves[half].astype(BF16).astype(F32)

        def row_of(ref, x):
            return jnp.concatenate(
                [ref[half, pl.ds(x, 8, stride=PE), :] for half in range(2)], axis=1
            )

        for x in range(PE):
            store_views(xv, x, row_of(src, x), 8)
        xv[:, PE * CELLS :] = jnp.zeros((xv.shape[0], 2 * CELLS), F32)
        edge = jnp.zeros((192, CELLS), F32)
        ya[:, 0:CELLS] = edge
        yb[:, 0:CELLS] = edge
        yb[:, (PE + 1) * CELLS :] = edge
        none = jnp.zeros((64, CELLS), BF16)
        gs[0:64, PE * CELLS : (PE + 1) * CELLS] = none
        gs[128:192, CELLS : 2 * CELLS] = none

        def forward(yy, x):
            return yy[0:64, cols(x)] + yy[64:128, cols(x, 1)] + yy[128:192, cols(x, 2)]

        def backward(yy, x):
            return yy[0:64, cols(x, 2)] + yy[64:128, cols(x, 1)] + yy[128:192, cols(x)]

        def conv_a(x):
            ya[:, cols(x, 1)] = dot_nn(w1[...], xv[:, cols(x)].astype(BF16))

        def hidden_a(x):
            hidden, slope = silu_parts(forward(ya, x))
            s1[:, cols(x)] = slope
            store_views(vv, x, hidden.astype(BF16), 64)

        conv_a(0)
        conv_a(1)
        conv_a(2)
        hidden_a(0)

        def ahead(x):
            done = dot_nn(w2[...], vv[:, cols(x, -1)])
            conv_a(x + 2)
            hidden_a(x)
            yb[:, cols(x)] = done

        for x in range(1, PE):
            ahead(x)
        yb[:, cols(PE)] = dot_nn(w2[...], vv[:, cols(PE - 1)])

        def last(x, carry):
            total, grad_last = carry
            hidden, slope = silu_parts(forward(yb, x))
            hidden = hidden.astype(BF16)
            miss = dot_nn(wl[...], hidden) - row_of(tgt, x)
            total = total + miss * miss
            grad_pred = (miss * grad_scale).astype(BF16)
            grad_last = grad_last + dot_nt(grad_pred, hidden)
            grad = (dot_nn(wlt[...], grad_pred) * slope).astype(BF16)
            store_views(gv, x, grad, 64)
            gs[0:64, cols(x)] = grad
            gs[64:128, cols(x, 1)] = grad
            gs[128:192, cols(x, 2)] = grad
            return total, grad_last

        def back(x, carry):
            done = dot_nn(w2b[...], gv[:, cols(x, -1)])
            carry = last(x, carry)
            ya[:, cols(x)] = done
            return carry

        zero = (jnp.zeros((8, CELLS), F32), jnp.zeros((8, 64), F32))
        carry = last(0, zero)
        for x in range(1, PE):
            carry = back(x, carry)
        total, grad_last = carry
        ya[:, cols(PE)] = dot_nn(w2b[...], gv[:, cols(PE - 1)])
        ya[:, (PE + 1) * CELLS : (PE + 2) * CELLS] = edge

        acc[...] = jnp.zeros(acc.shape, F32)

        def weight_b(i):
            at = slice(2 * i * CELLS, 2 * (i + 1) * CELLS)
            at1 = slice((2 * i + 1) * CELLS, (2 * i + 3) * CELLS)
            more = dot_nt(gs[:, at1], vv[:, at])
            for k in range(2):
                x = 2 * i + k
                gv[0:64, cols(x)] = (backward(ya, x) * s1[:, cols(x)]).astype(BF16)
            acc[...] += more

        for i in range(PE // 2):
            weight_b(i)
        gs[0:64, PE * CELLS : (PE + 1) * CELLS] = none
        g1 = gv[0:64, 0 : PE * CELLS]
        shift = jnp.zeros((64, CELLS), BF16)
        whole = PE * CELLS
        stacked = jnp.concatenate(
            [
                jnp.concatenate([g1[:, CELLS:], shift], axis=1),
                g1,
                jnp.concatenate([shift, g1[:, : whole - CELLS]], axis=1),
            ],
            axis=0,
        )
        grad_first = dot_nt(xv[:, 0:whole].astype(BF16), stacked)

        for i in range(24):
            for j in range(4):
                out[4 * i + j] = acc[8 * i : 8 * i + 8, LANES * j : LANES * (j + 1)]
        for i in range(12):
            out[96 + i] = jnp.concatenate(
                [acc[8 * i : 8 * i + 8, 512:576], acc[8 * i + 96 : 8 * i + 104, 512:576]], axis=1
            )
        for i in range(9):
            out[108 + i] = grad_first[8 * i : 8 * i + 8, 0:LANES]
        for i in range(5):
            j = min(i + 5, 8)
            out[117 + i] = jnp.concatenate(
                [grad_first[8 * i : 8 * i + 8, 128:192], grad_first[8 * j : 8 * j + 8, 128:192]],
                axis=1,
            )
        loss = jnp.sum(total) * (1.0 / (PE**3 * LIVE_ROW))
        corner = lane_of((8, LANES))
        deep = lax.broadcasted_iota(jnp.int32, (8, LANES), 0)
        padded = jnp.concatenate([grad_last, jnp.zeros((8, 64), F32)], axis=1)
        out[122] = jnp.where((deep == 7) & (corner == 64 + dest), loss, padded)
        for i in range(123, 128):
            out[i] = jnp.zeros((8, LANES), F32)


def unpack_kernel(parts, first, mid, last, loss):
    for dx in range(3):
        for t in range(8):
            i = 8 * dx + t
            for k in range(9):
                if k < 8:
                    block, half = parts[4 * i + k // 2], k % 2
                else:
                    block, half = parts[96 + i % 12], i // 12
                mid[9 * dx + k, 8 * t : 8 * t + 8, :] = block[:, 64 * half : 64 * half + 64]
    for k in range(9):
        tail = parts[117 + k % 5]
        half = k // 5
        wide = jnp.concatenate([parts[108 + k], tail[:, 64 * half : 64 * half + 64]], axis=1)
        turned = wide.T
        for dx in range(3):
            first[9 * dx + k] = turned[64 * dx : 64 * dx + 64, 0:3]
    final = parts[122]
    last[...] = final[0:6, 0:64]
    corner = lane_of((8, LANES))
    deep = lax.broadcasted_iota(jnp.int32, (8, LANES), 0)
    row = lax.axis_index("group") * lax.axis_size("dp") + lax.axis_index("dp")
    mine = (deep == 7) & (corner == 64 + row)
    loss[0] = jnp.sum(jnp.where(mine, final, 0.0))


VMEM = pl.BlockSpec()
SMEM = pl.BlockSpec(memory_space=pltpu.SMEM)


def params(mib):
    return pltpu.CompilerParams(vmem_limit_bytes=mib * 1024 * 1024)


def train_call(tables, own, wlo, whi, weights, row_count):
    grad_scale = 2.0 / (PE**3 * row_count * LIVE_ROW)
    whole = PE * CELLS
    height = own.shape[1] + 2 * HALO
    return pl.pallas_call(
        functools.partial(train_kernel, grad_scale),
        out_shape=jax.ShapeDtypeStruct((128, 8, LANES), F32),
        in_specs=[SMEM] + [VMEM] * 8,
        out_specs=VMEM,
        scratch_shapes=[
            pltpu.VMEM((3, height, 8, LANES), F32),
            pltpu.VMEM((3, height, 8, LANES), F32),
            pltpu.VMEM((3, height, 8, LANES), F32),
            pltpu.VMEM((9, 8 * PE, LANES), F32),
            pltpu.VMEM((2, 8 * PE, LANES), F32),
            pltpu.VMEM((2, 8 * PE, LANES), F32),
            pltpu.VMEM((72, whole + 2 * CELLS), F32),
            pltpu.VMEM((576, whole), BF16),
            pltpu.VMEM((576, whole), BF16),
            pltpu.VMEM((192, whole + 3 * CELLS), F32),
            pltpu.VMEM((192, whole + 2 * CELLS), F32),
            pltpu.VMEM((64, whole), F32),
            pltpu.VMEM((192, whole + 2 * CELLS), BF16),
            pltpu.VMEM((192, 576), F32),
        ],
        compiler_params=params(60),
        cost_estimate=pl.CostEstimate(flops=10**7, bytes_accessed=6 * 10**7, transcendentals=0),
    )(tables, own, wlo, whi, *weights)


def weight_kernel(first, mid, last, w1, w2, w2b, wl, wlt):
    none = jnp.zeros((64, 5), F32)
    for dx in range(3):
        rows = slice(64 * dx, 64 * dx + 64)
        small = []
        for k in range(9):
            small += [first[9 * dx + k].astype(F32), none]
        w1[rows] = jnp.concatenate(small, axis=1).astype(BF16)
        blocks = [mid[9 * dx + k].astype(F32) for k in range(9)]
        w2[rows] = jnp.concatenate(blocks, axis=1).astype(BF16)
        w2b[rows] = jnp.concatenate(blocks[::-1], axis=0).T.astype(BF16)
    padded = jnp.concatenate([last[...].astype(F32), jnp.zeros((2, 64), F32)], axis=0)
    wl[...] = padded.astype(BF16)
    wlt[...] = padded.T.astype(BF16)


def layer_weights(conv_first, conv_mid, conv_last):
    shapes = ((192, 72), (192, 576), (192, 576), (8, 64), (64, 8))
    return pl.pallas_call(
        weight_kernel,
        out_shape=tuple(jax.ShapeDtypeStruct(s, BF16) for s in shapes),
        in_specs=[VMEM] * 3,
        out_specs=(VMEM,) * 5,
        compiler_params=params(60),
    )(conv_first, conv_mid, conv_last)


def local(
    velocity, conv_first, conv_mid, conv_last, corner_x, corner_z, corner_y, patch_live, patch_dest
):
    row_count = patch_live.shape[0]
    _, count, levels, _ = velocity.shape
    strip = jax.ShapeDtypeStruct((3, levels, LANES), F32)
    up_row = [(i, (i + 1) % row_count) for i in range(row_count)]
    down_row = [(j, i) for i, j in up_row]
    cols_n = lax.axis_size("space")
    up_col = [(i, (i + 1) % cols_n) for i in range(cols_n)]
    down_col = [(j, i) for i, j in up_col]

    tables = jnp.stack([patch_live, corner_x, corner_z, patch_dest, corner_y])
    lo, hi = pl.pallas_call(
        pack_kernel,
        out_shape=(strip, strip),
        in_specs=[VMEM],
        out_specs=(VMEM, VMEM),
        compiler_params=params(60),
    )(velocity)
    left = lax.ppermute(hi, "space", up_col)
    right = lax.ppermute(lo, "space", down_col)
    edge = jax.ShapeDtypeStruct((3, HALO, 8, LANES), F32)
    up, down = pl.pallas_call(
        functools.partial(edge_kernel, row_count),
        out_shape=(edge, edge),
        in_specs=[SMEM] + [VMEM] * 3,
        out_specs=(VMEM, VMEM),
        compiler_params=params(60),
    )(tables, velocity, left, right)
    wlo = lax.ppermute(up, ROWS, up_row)
    whi = lax.ppermute(down, ROWS, down_row)
    face = jax.ShapeDtypeStruct((3, HALO + 1, levels, LANES), F32)
    own, to_up, to_down = pl.pallas_call(
        own_kernel,
        out_shape=(jax.ShapeDtypeStruct((3, count, 8, LANES), F32), face, face),
        in_specs=[SMEM] + [VMEM] * 3,
        out_specs=(VMEM,) * 3,
        compiler_params=params(60),
    )(tables, velocity, left, right)
    weights = layer_weights(conv_first, conv_mid, conv_last)
    to_up, to_down, wlo, whi, weights = lax.optimization_barrier(
        (to_up, to_down, wlo, whi, weights)
    )
    xlo = lax.ppermute(to_up, ROWS, up_row)
    xhi = lax.ppermute(to_down, ROWS, down_row)
    parts = train_call(tables, own, wlo, whi, weights, row_count)

    parts, velocity, xlo, xhi = lax.optimization_barrier((parts, velocity, xlo, xhi))
    shares = lax.all_to_all(parts, EVERY, 0, 0, tiled=True)
    wide = 2 * LANES
    height = count + 2 * HALO
    nxt, wide_next = pl.pallas_call(
        solver_kernel,
        out_shape=(
            jax.ShapeDtypeStruct(velocity.shape, F32),
            jax.ShapeDtypeStruct((3, height - 4, levels, wide), F32),
        ),
        in_specs=[VMEM] * 5,
        out_specs=(VMEM, VMEM),
        scratch_shapes=[
            pltpu.VMEM((3, height, levels, wide), F32),
            pltpu.VMEM((3, height - 2, levels, wide), F32),
        ],
        compiler_params=params(60),
        cost_estimate=pl.CostEstimate(flops=10**7, bytes_accessed=4 * 10**7, transcendentals=0),
    )(velocity, xlo, xhi, left, right)
    shares, wide_next = lax.optimization_barrier((shares, wide_next))
    filt, stress = pl.pallas_call(
        filter_kernel,
        out_shape=(
            jax.ShapeDtypeStruct(velocity.shape, F32),
            jax.ShapeDtypeStruct((6,) + velocity.shape[1:], F32),
        ),
        in_specs=[VMEM],
        out_specs=(VMEM, VMEM),
        compiler_params=params(60),
        cost_estimate=pl.CostEstimate(flops=10**7, bytes_accessed=4 * 10**7, transcendentals=0),
    )(wide_next)
    mine = jnp.sum(shares, axis=0, keepdims=True)
    summed = lax.all_to_all(jnp.broadcast_to(mine, parts.shape), EVERY, 0, 0, tiled=True)
    grad_first, grad_mid, grad_last, loss = pl.pallas_call(
        unpack_kernel,
        out_shape=(
            jax.ShapeDtypeStruct((27, 64, 3), F32),
            jax.ShapeDtypeStruct((27, 64, 64), F32),
            jax.ShapeDtypeStruct((6, 64), F32),
            jax.ShapeDtypeStruct((1,), F32),
        ),
        in_specs=[VMEM],
        out_specs=(VMEM, VMEM, VMEM, SMEM),
        compiler_params=params(60),
    )(summed)
    return (nxt, filt, stress, grad_first, grad_mid, grad_last, loss)


def solution(mesh):
    block = P(None, ("group", "dp"), None, "space")
    in_specs = (block,) + (P(),) * 8
    out_specs = (block, block, block, P(), P(), P(), P(("group", "dp")))
    return jax.shard_map(local, mesh=mesh, in_specs=in_specs, out_specs=out_specs, check_vma=False)
```

time: 146 us -> 95.5 us (0.65)
  blocking collectives: 67.2 us -> 0 us
  starting transfers between devices: 13.4 us -> 34.4 us
  waiting for transfers between devices: 0.02 us -> 7.41 us
  local copies, waits for them, and re-layouts: 16.8 us -> 10.6 us
  Pallas kernels: 47.1 us -> 41.4 us
    all_to_all x2 -> x0, blocking collectives: 67.2 us -> none  [the longest x1 49.5 us: local(): shares = lax.all_to_all(parts, EVERY, 0, 0, tiled=True)]
    all_to_all x0 -> x2, starting transfers between devices: none -> 20.9 us  [the longest x1 13.2 us: local(): shares = lax.all_to_all(parts, EVERY, 0, 0, tiled=True)]
    pallas_call x2 -> x5, Pallas kernels: 42.2 us -> 33.9 us  [the longest x1 13.9 us: local(): pl.pallas_call(filter_kernel, out_shape=(jax.ShapeDtypeStruct(velocity.sh...]
    ppermute x4, waiting for transfers between devices: 0.01 us -> 5.33 us  [the longest x1 5.32 us: local(): xlo = lax.ppermute(to_up, ROWS, up_row)]
    reshape x8 -> x0, local copies, waits for them, and re-layouts: 4.27 us -> none  [the longest x2 2.22 us: train_call(): w2b = by_k[:, ::-1].transpose(0, 3, 1, 2).reshape(192, 576)]
    all_to_all x0 -> x2, waiting for transfers between devices: none -> 2.07 us  [the longest x1 2.07 us: local(): shares = lax.all_to_all(parts, EVERY, 0, 0, tiled=True)]
    pallas_call x1, Pallas kernels: 0.58 us -> 2.51 us  [train_call(): pl.pallas_call(functools.partial(train_kernel, grad_scale), out_shape=jax...]
    slice x1 -> x0, local copies, waits for them, and re-layouts: 1.79 us -> none  [local(): xhi = lax.ppermute(velocity[:, :HALO], ROWS, down_row)]
  transfers between devices with their start and end apart: 6 -> 8, of which waited for: 0 -> 2; matrix products, arithmetic and copies ran while one was open for 9% -> 6% of each run, Pallas kernels for 1% -> 36%
where the time goes in v2:
time: 95.5 us; the launch traced here: 94.7 us
  Pallas kernels  41.4 us (43%)
  starting transfers between devices  34.4 us (36%)
  local copies, waits for them, and re-layouts  10.6 us (11%)
  waiting for transfers between devices  7.41 us (8%)
    pallas_call x1, Pallas kernels, local(): pl.pallas_call(filter_kernel, out_shape=(jax.ShapeDtypeStruct(velocity.sh...  13.9 us
    all_to_all x1, starting transfers between devices, local(): shares = lax.all_to_all(parts, EVERY, 0, 0, tiled=True)  13.2 us
    pallas_call x1, Pallas kernels, local(): pl.pallas_call(solver_kernel, out_shape=(jax.ShapeDtypeStruct(velocity.sh...  11.5 us
    all_to_all x1, starting transfers between devices, local(): lax.all_to_all(jnp.broadcast_to(mine, parts.shape), EVERY, 0, 0, tiled=True)  7.69 us
    unnamed x22, local copies, waits for them, and re-layouts  5.97 us
    ppermute x1, waiting for transfers between devices, local(): xlo = lax.ppermute(to_up, ROWS, up_row)  5.32 us
    ppermute x1, starting transfers between devices, local(): xhi = lax.ppermute(to_down, ROWS, down_row)  4.18 us
    another operation x6, local copies, waits for them, and re-layouts, local(): tables = jnp.stack([patch_live, corner_x, corner_z, patch_dest, corner_y])  3.79 us
  transfers between devices with their start and end apart: 8, of which 2 were waited for; matrix products, arithmetic and copies ran while one was open for 6% of the time, Pallas kernels for 36%

profile of v2, /device:TPU:1, one launch (start us, length us, event | category | flops | bytes accessed | tf_op | source)
XLA Modules:
  0.0 94.7 jit_solution(3023986733289174337)
XLA Ops:
  0.6 2.4 %shard_map.144 = (f32[3,32,128]{2,1,0:T(8,128)}, f32[3,32,128]{2,1,0:T(8,128)}) custom-call(f32[3,20,32,128]{3,2,1,0:T(8,128)} %vel.6), custom_call_target="tpu_custom_call" | custom-call | tf_op jit(solution)/shard_map/pallas_call | solution.py:577
  3.0 2.7 %collective-permute-start = (f32[3,32,128]{2,1,0:T(8,128)}, f32[3,32,128]{2,1,0:T(8,128)S(1)}, u32[]{:S(2)}, u32[]{:S(2)}) collective-permute-start(f32[3,32,128]{2,1,0:T(8,128)} %get-tuple-element.42), channel_id=1, source_target_pairs={{0,1},{1,2},{2,3},{3,4},{4,5},{5,6},{6,7},{7,0},{8,9},{9,10},{10,1... | collective-permute-start | bytes 147464 | tf_op jit(solution)/shard_map/ppermute | solution.py:584
  5.7 0.0 collective-permute-start.1
  5.7 0.8 copy.17
  6.5 0.8 copy.18
  7.2 0.8 copy.20
  8.0 0.8 copy.16
  8.8 0.8 copy.19
  9.5 0.0 copy-start.3
  9.5 0.0 collective-permute-done.left
  9.6 0.0 copy-start.1
  9.6 0.0 collective-permute-done.1.right
  9.6 0.6 copy-done.3
  10.1 0.0 copy-done.1
  10.2 0.0 copy-start.2
  10.2 0.6 copy-done.2
  10.8 2.7 %shard_map.146 = (f32[3,5,8,128]{3,2,1,0:T(8,128)}, f32[3,5,8,128]{3,2,1,0:T(8,128)}) custom-call(s32[5,16,8]{2,1,0:T(8,128)} %copy-done.3, f32[3,20,32,128]{3,2,1,0:T(8,128)} %vel.6, f32[3,32,128]{2,1,0:T(8,128)} %copy-done.1, f32[3,32,128]{2,1,0:T(8,128)} %copy-done.2), custom_call_target="tpu_custom_call" | custom-call | tf_op jit(solution)/shard_map/pallas_call | solution.py:587
  13.4 3.6 %collective-permute-start.2 = (f32[3,5,8,128]{3,2,1,0:T(8,128)}, f32[3,5,8,128]{3,2,1,0:T(8,128)S(1)}, u32[]{:S(2)}, u32[]{:S(2)}) collective-permute-start(f32[3,5,8,128]{3,2,1,0:T(8,128)} %get-tuple-element.47), channel_id=1, source_target_pairs={{0,8},{8,16},{16,24},{24,32},{32,40},{40,48},{48,56},{56,64},{64,7... | collective-permute-start | bytes 184328 | tf_op jit(solution)/shard_map/ppermute | solution.py:594
  17.0 2.4 %collective-permute-start.3 = (f32[3,5,8,128]{3,2,1,0:T(8,128)}, f32[3,5,8,128]{3,2,1,0:T(8,128)S(1)}, u32[]{:S(2)}, u32[]{:S(2)}) collective-permute-start(f32[3,5,8,128]{3,2,1,0:T(8,128)} %get-tuple-element.48), channel_id=1, source_target_pairs={{8,0},{16,8},{24,16},{32,24},{40,32},{48,40},{56,48},{64,56},{72,6... | collective-permute-start | bytes 184328 | tf_op jit(solution)/shard_map/ppermute | solution.py:595
  19.4 1.8 %copy.21.first = bf16[27,64,3]{2,1,0:T(8,128)(2,1)} copy(bf16[27,64,3]{1,0,2:T(8,128)(2,1)} %param.10) | data formatting | bytes 20736 | tf_op args[1]
  21.2 2.2 %shard_map.147 = (bf16[192,72]{1,0:T(8,128)(2,1)}, bf16[192,576]{1,0:T(8,128)(2,1)}, bf16[192,576]{1,0:T(8,128)(2,1)}, bf16[8,64]{1,0:T(8,128)(2,1)}, bf16[64,8]{1,0:T(8,128)(2,1)}) custom-call(bf16[27,64,3]{2,1,0:T(8,128)(2,1)} %copy.21.first, bf16[27,64,64]{2,1,0:T(8,128)(2,1)} %mid.1, bf16[6,64]{1,0:T(8,128)(2,1)} %last.1), custom_call_target="tpu_custom_call" | custom-call | tf_op jit(solution)/shard_map/pallas_call | solution.py:555
  23.4 3.6 %shard_map.145 = (f32[3,20,8,128]{3,2,1,0:T(8,128)}, f32[3,6,32,128]{3,2,1,0:T(8,128)}, f32[3,6,32,128]{3,2,1,0:T(8,128)}) custom-call(s32[5,16,8]{2,1,0:T(8,128)} %copy-done.3, f32[3,20,32,128]{3,2,1,0:T(8,128)} %vel.6, f32[3,32,128]{2,1,0:T(8,128)} %copy-done.1, f32[3,32,128]{2,1,0:T(8,128)} %copy-done.2), custom_call_target="tpu_custom_call" | custom-call | tf_op jit(solution)/shard_map/pallas_call | solution.py:597
  27.0 0.0 collective-permute-done.2.wlo
  27.0 0.0 copy-start.6
  27.0 0.0 collective-permute-done.3.whi
  27.0 0.0 copy-start.7
  27.0 0.7 collective-permute-start.4
  27.7 4.2 %collective-permute-start.5 = (f32[3,6,32,128]{3,2,1,0:T(8,128)}, f32[3,6,32,128]{3,2,1,0:T(8,128)S(1)}, u32[]{:S(2)}, u32[]{:S(2)}) collective-permute-start(f32[3,6,32,128]{3,2,1,0:T(8,128)} %get-tuple-element.62), channel_id=1, source_target_pairs={{8,0},{16,8},{24,16},{32,24},{40,32},{48,40},{56,48},{64,56},{72,6... | collective-permute-start | bytes 884744 | tf_op jit(solution)/shard_map/ppermute | solution.py:609
  31.9 0.0 copy-done.6
  31.9 0.0 copy-done.7
  31.9 2.5 %shard_map.148 = f32[128,8,128]{2,1,0:T(8,128)} custom-call(s32[5,16,8]{2,1,0:T(8,128)} %copy-done.3, f32[3,20,8,128]{3,2,1,0:T(8,128)} %get-tuple-element.44.own, f32[3,5,8,128]{3,2,1,0:T(8,128)} %copy-done.6, f32[3,5,8,128]{3,2,1,0:T(8,128)} %copy-done.7, bf16[192,72]{1,0:T(8,128)(2,1)} %get-tuple-element.56.w1, bf16[192,576]{1,0:T(8,128)(2,1)} %get-tuple-element.57.w2, ...), custom_call_target="tpu_custom_call" | custom-call | flops 10000000 | bytes 60000000 | tf_op jit(solution)/shard_map/pallas_call | solution.py:511
  34.4 5.3 %collective-permute-done.4.xlo = f32[3,6,32,128]{3,2,1,0:T(8,128)S(1)} collective-permute-done((f32[3,6,32,128]{3,2,1,0:T(8,128)}, f32[3,6,32,128]{3,2,1,0:T(8,128)S(1)}, u32[]{:S(2)}, u32[]{:S(2)}) %collective-permute-start.4) | collective-permute-done | bytes 294944 | tf_op jit(solution)/shard_map/ppermute | solution.py:608
  39.7 0.0 copy-start.4
  39.7 0.0 collective-permute-done.5.xhi
  39.7 0.0 copy-start.5
  39.7 13.2 %all-to-all-start = ((f32[128,8,128]{2,1,0:T(8,128)}), f32[128,8,128]{2,1,0:T(8,128)S(1)}, u32[]{:S(2)}, u32[]{:S(2)}) async-start(f32[128,8,128]{2,1,0:T(8,128)} %shard_map.148), calls=%async_computation | async-start | bytes 1048576 | tf_op jit(solution)/shard_map/all_to_all | solution.py:613
  52.9 0.0 copy-done.4
  52.9 0.0 copy-done.5
  52.9 11.5 %shard_map.149 = (f32[3,20,32,128]{3,2,1,0:T(8,128)}, f32[3,26,32,256]{3,2,1,0:T(8,128)}) custom-call(f32[3,20,32,128]{3,2,1,0:T(8,128)} %vel.6, f32[3,6,32,128]{3,2,1,0:T(8,128)} %copy-done.4, f32[3,6,32,128]{3,2,1,0:T(8,128)} %copy-done.5, f32[3,32,128]{2,1,0:T(8,128)} %copy-done.1, f32[3,32,128]{2,1,0:T(8,128)} %copy-done.2), custom_call_target="tpu_custom_call" | custom-call | flops 10000000 | bytes 40000000 | tf_op jit(solution)/shard_map/pallas_call | solution.py:616
  64.4 2.1 %all-to-all-done = f32[128,8,128]{2,1,0:T(8,128)S(1)} async-done(((f32[128,8,128]{2,1,0:T(8,128)}), f32[128,8,128]{2,1,0:T(8,128)S(1)}, u32[]{:S(2)}, u32[]{:S(2)}) %all-to-all-start) | async-done | bytes 524320 | tf_op jit(solution)/shard_map/all_to_all | solution.py:613
  66.5 0.1 reduce_sum.9
  66.6 0.8 broadcast_in_dim.2
  67.5 7.7 %all-to-all-start.1 = ((f32[128,8,128]{2,1,0:T(8,128)}), f32[128,8,128]{2,1,0:T(8,128)S(1)}, u32[]{:S(2)}, u32[]{:S(2)}) async-start(f32[128,8,128]{2,1,0:T(8,128)} %broadcast_in_dim.2), calls=%async_computation.1 | async-start | bytes 1048576 | tf_op jit(solution)/shard_map/all_to_all | solution.py:644
  75.2 13.9 %shard_map.150 = (f32[3,20,32,128]{3,2,1,0:T(8,128)}, f32[6,20,32,128]{3,2,1,0:T(8,128)}) custom-call(f32[3,26,32,256]{3,2,1,0:T(8,128)} %get-tuple-element.69.wa), custom_call_target="tpu_custom_call" | custom-call | flops 10000000 | bytes 40000000 | tf_op jit(solution)/shard_map/pallas_call | solution.py:632
  89.1 0.0 all-to-all-done.1.parts
  89.1 0.0 copy-start
  89.1 0.8 copy-done
  89.9 2.7 %shard_map.151 = (f32[27,64,3]{2,1,0:T(8,128)}, f32[27,64,64]{2,1,0:T(8,128)}, f32[6,64]{1,0:T(8,128)}, f32[1]{0:T(128)}) custom-call(f32[128,8,128]{2,1,0:T(8,128)} %copy-done), custom_call_target="tpu_custom_call" | custom-call | tf_op jit(solution)/shard_map/pallas_call | solution.py:645
  92.6 2.2 %copy.22 = f32[27,64,3]{1,0,2:T(8,128)} copy(f32[27,64,3]{2,1,0:T(8,128)} %get-tuple-element.80) | data formatting | bytes 41472
  (5 shorter events, 0.0 us)
Async XLA Ops:
  3.0 6.5 %collective-permute-start = (f32[3,32,128]{2,1,0:T(8,128)}, f32[3,32,128]{2,1,0:T(8,128)S(1)}, u32[]{:S(2)}, u32[]{:S(2)}) collective-permute-start(f32[3,32,128]{2,1,0:T(8,128)} %get-tuple-element.42), channel_id=1, source_target_pairs={{0,1},{1,2},{2,3},{3,4},{4,5},{5,6},{6,7},{7,0},{8,9},{9,10},{10,1... | collective-permute-start | bytes 147464 | tf_op jit(solution)/shard_map/ppermute | solution.py:584
  5.7 3.8 %collective-permute-start.1 = (f32[3,32,128]{2,1,0:T(8,128)}, f32[3,32,128]{2,1,0:T(8,128)S(1)}, u32[]{:S(2)}, u32[]{:S(2)}) collective-permute-start(f32[3,32,128]{2,1,0:T(8,128)} %get-tuple-element.43), channel_id=1, source_target_pairs={{1,0},{2,1},{3,2},{4,3},{5,4},{6,5},{7,6},{0,7},{9,8},{10,9},{11,1... | collective-permute-start | bytes 147464 | tf_op jit(solution)/shard_map/ppermute | solution.py:585
  9.5 0.6 copy-start.3
  9.6 0.6 copy-start.1
  10.2 0.6 copy-start.2
  13.4 13.5 %collective-permute-start.2 = (f32[3,5,8,128]{3,2,1,0:T(8,128)}, f32[3,5,8,128]{3,2,1,0:T(8,128)S(1)}, u32[]{:S(2)}, u32[]{:S(2)}) collective-permute-start(f32[3,5,8,128]{3,2,1,0:T(8,128)} %get-tuple-element.47), channel_id=1, source_target_pairs={{0,8},{8,16},{16,24},{24,32},{32,40},{40,48},{48,56},{56,64},{64,7... | collective-permute-start | bytes 184328 | tf_op jit(solution)/shard_map/ppermute | solution.py:594
  17.0 9.9 %collective-permute-start.3 = (f32[3,5,8,128]{3,2,1,0:T(8,128)}, f32[3,5,8,128]{3,2,1,0:T(8,128)S(1)}, u32[]{:S(2)}, u32[]{:S(2)}) collective-permute-start(f32[3,5,8,128]{3,2,1,0:T(8,128)} %get-tuple-element.48), channel_id=1, source_target_pairs={{8,0},{16,8},{24,16},{32,24},{40,32},{48,40},{56,48},{64,56},{72,6... | collective-permute-start | bytes 184328 | tf_op jit(solution)/shard_map/ppermute | solution.py:595
  27.0 4.9 %copy-start.6 = (f32[3,5,8,128]{3,2,1,0:T(8,128)}, f32[3,5,8,128]{3,2,1,0:T(8,128)S(1)}, u32[]{:S(2)}) copy-start(f32[3,5,8,128]{3,2,1,0:T(8,128)S(1)} %collective-permute-done.2.wlo) | copy-start | bytes 184324
  27.0 4.9 %copy-start.7 = (f32[3,5,8,128]{3,2,1,0:T(8,128)}, f32[3,5,8,128]{3,2,1,0:T(8,128)S(1)}, u32[]{:S(2)}) copy-start(f32[3,5,8,128]{3,2,1,0:T(8,128)S(1)} %collective-permute-done.3.whi) | copy-start | bytes 184324
  27.0 12.7 %collective-permute-start.4 = (f32[3,6,32,128]{3,2,1,0:T(8,128)}, f32[3,6,32,128]{3,2,1,0:T(8,128)S(1)}, u32[]{:S(2)}, u32[]{:S(2)}) collective-permute-start(f32[3,6,32,128]{3,2,1,0:T(8,128)} %get-tuple-element.61), channel_id=1, source_target_pairs={{0,8},{8,16},{16,24},{24,32},{32,40},{40,48},{48,56},{56,64},{64,7... | collective-permute-start | bytes 884744 | tf_op jit(solution)/shard_map/ppermute | solution.py:608
  27.7 12.0 %collective-permute-start.5 = (f32[3,6,32,128]{3,2,1,0:T(8,128)}, f32[3,6,32,128]{3,2,1,0:T(8,128)S(1)}, u32[]{:S(2)}, u32[]{:S(2)}) collective-permute-start(f32[3,6,32,128]{3,2,1,0:T(8,128)} %get-tuple-element.62), channel_id=1, source_target_pairs={{8,0},{16,8},{24,16},{32,24},{40,32},{48,40},{56,48},{64,56},{72,6... | collective-permute-start | bytes 884744 | tf_op jit(solution)/shard_map/ppermute | solution.py:609
  39.7 13.2 %copy-start.4 = (f32[3,6,32,128]{3,2,1,0:T(8,128)}, f32[3,6,32,128]{3,2,1,0:T(8,128)S(1)}, u32[]{:S(2)}) copy-start(f32[3,6,32,128]{3,2,1,0:T(8,128)S(1)} %collective-permute-done.4.xlo) | copy-start | bytes 884740
  39.7 13.2 %copy-start.5 = (f32[3,6,32,128]{3,2,1,0:T(8,128)}, f32[3,6,32,128]{3,2,1,0:T(8,128)S(1)}, u32[]{:S(2)}) copy-start(f32[3,6,32,128]{3,2,1,0:T(8,128)S(1)} %collective-permute-done.5.xhi) | copy-start | bytes 884740
  39.7 26.8 %all-to-all-start = ((f32[128,8,128]{2,1,0:T(8,128)}), f32[128,8,128]{2,1,0:T(8,128)S(1)}, u32[]{:S(2)}, u32[]{:S(2)}) async-start(f32[128,8,128]{2,1,0:T(8,128)} %shard_map.148), calls=%async_computation | async-start | bytes 1048576 | tf_op jit(solution)/shard_map/all_to_all | solution.py:613
  67.5 21.6 %all-to-all-start.1 = ((f32[128,8,128]{2,1,0:T(8,128)}), f32[128,8,128]{2,1,0:T(8,128)S(1)}, u32[]{:S(2)}, u32[]{:S(2)}) async-start(f32[128,8,128]{2,1,0:T(8,128)} %broadcast_in_dim.2), calls=%async_computation.1 | async-start | bytes 1048576 | tf_op jit(solution)/shard_map/all_to_all | solution.py:644
  89.1 0.8 copy-start

commit v3 on v2

--- a/solution.py
+++ b/solution.py
@@ -76,7 +76,19 @@
     )
 
 
-def solver_kernel(vel, xlo, xhi, left, right, nxt, wide_next, wa, wb):
+def fetch(sources, targets, sems):
+    copies = [
+        pltpu.make_async_copy(source, target, sems.at[i])
+        for i, (source, target) in enumerate(zip(sources, targets))
+    ]
+    for copy in copies:
+        copy.start()
+    for copy in copies:
+        copy.wait()
+
+
+def solver_kernel(vel, xlo_h, xhi_h, left_h, right_h, nxt, wide_next, wa, wb, xlo, xhi, left, right, sems):
+    fetch((xlo_h, xhi_h, left_h, right_h), (xlo, xhi, left, right), sems)
     count = vel.shape[1]
     levels = vel.shape[2]
     lane = lane_of((levels, LANES))
@@ -104,7 +116,7 @@
     level = lax.broadcasted_iota(jnp.int32, (levels, 2 * LANES), 0)
 
     def step(src, dst, n):
-        def body(r, carry):
+        for r in range(n):
             mids = [src[c, r + 1] for c in range(3)]
             for c in range(3):
                 mid = mids[c]
@@ -117,9 +129,6 @@
                 adv = mids[0] * (xp - xm) + mids[1] * (yp - ym) + mids[2] * (zp - zm)
                 lap = (xp + xm) + (yp + ym) + (zp + zm) - 6.0 * mid
                 dst[c, r] = mid + (0.005 * lap - 0.025 * adv)
-            return carry
-
-        lax.fori_loop(0, n, body, 0)
 
     step(wa, wb, count + 2 * HALO - 2)
     step(wb, wide_next, count + 2 * HALO - 4)
@@ -127,36 +136,49 @@
         nxt[c] = wide_next[c, 3 : 3 + count, :, 0:LANES]
 
 
-def filter_kernel(wa, filt, stress):
+def filter_kernel(wa, filt, stress, parts):
     count = filt.shape[1]
     levels = filt.shape[2]
-    tile = 8
-    lanes = lane_of((tile, LANES))
-
-    def along_y(f):
-        m, e = f[:, :LANES], f[:, LANES:]
-
-        def tap(k):
-            outside = (lanes >= LANES - k) if k > 0 else (lanes < -k)
-            return jnp.where(outside, roll(e, -k), roll(m, -k))
-
-        near = 15.0 * (tap(1) + tap(-1)) + 6.0 * (tap(2) + tap(-2))
-        return (20.0 * m + near + (tap(3) + tap(-3))) * (1.0 / 4096.0)
-
-    def filter_row(r, carry):
+    wide = 2 * LANES
+    source = lax.broadcasted_iota(jnp.int32, (wide, LANES), 0)
+    source = jnp.where(source < LANES + 64, source, source - wide)
+    apart = jnp.abs(source - lax.broadcasted_iota(jnp.int32, (wide, LANES), 1))
+    band = jnp.zeros((wide, LANES), F32)
+    for k, weight in enumerate((20.0, 15.0, 6.0, 1.0)):
+        band = jnp.where(apart == k, weight, band)
+    band = jnp.concatenate([band] * 3, axis=0).astype(BF16)
+    tile = 16
+    for f in range(9):
         for t in range(levels // tile):
             zs = slice(t * tile, (t + 1) * tile)
-            rows = [[wa[c, r + k, zs, :] for k in range(7)] for c in range(3)]
-            done = [along_y(along_x(rows[c])) for c in range(3)]
-            for c in range(3):
-                filt[c, r, zs, :] = done[c]
-            small = products(*done)
-            for i, (a, b) in enumerate(PAIRS):
-                big = along_y(along_x([rows[a][k] * rows[b][k] for k in range(7)]))
-                stress[i, r, zs, :] = big - small[i]
-        return carry
-
-    lax.fori_loop(0, count, filter_row, 0)
+            before = [None] * 6
+            for r in range(count + 6):
+                if f < 3:
+                    value = wa[f, r, zs, :]
+                else:
+                    a, b = PAIRS[f - 3]
+                    value = wa[a, r, zs, :] * wa[b, r, zs, :]
+                for k in range(6):
+                    old, before[k] = before[k], value
+                    if old is None:
+                        value = None
+                        break
+                    value = old + value
+                if value is None:
+                    continue
+                at = slice((r - 6) * levels + t * tile, (r - 6) * levels + (t + 1) * tile)
+                for k in range(3):
+                    part = value.astype(BF16)
+                    parts[f % 2, at, k * wide : (k + 1) * wide] = part
+                    if k < 2:
+                        value = value - part.astype(F32)
+        done = dot_nn(parts[f % 2], band) * (1.0 / 4096.0)
+        done = done.reshape(count, levels, LANES)
+        if f < 3:
+            filt[f] = done
+        else:
+            a, b = PAIRS[f - 3]
+            stress[f - 3] = done - filt[a] * filt[b]
 
 
 def window_row(main, left, right, r, begin):
@@ -174,12 +196,13 @@
     return out
 
 
-def edge_kernel(rows, tables, vel, left, right, up, down):
+def edge_kernel(rows, corner_h, vel, left, right, up, down, corner_y, sems):
     col = lax.axis_index("space")
     row = lax.axis_index("group") * lax.axis_size("dp") + lax.axis_index("dp")
+    fetch((corner_h,), (corner_y,), sems)
     count = vel.shape[1]
-    begin_up = tables[4, lax.rem(row + 1, rows), col]
-    begin_down = tables[4, lax.rem(row + rows - 1, rows), col]
+    begin_up = corner_y[col, lax.rem(row + 1, rows)]
+    begin_down = corner_y[col, lax.rem(row + rows - 1, rows)]
     for c in range(3):
         for k in range(HALO):
             r = count - HALO + k
@@ -187,10 +210,11 @@
             down[c, k] = window_row(vel[c, k], left[c], right[c], k, begin_down)
 
 
-def own_kernel(tables, vel, left, right, out, up, down):
+def own_kernel(corner_h, vel, left, right, out, up, down, corner_y, sems):
+    fetch((corner_h,), (corner_y,), sems)
     col = lax.axis_index("space")
     row = lax.axis_index("group") * lax.axis_size("dp") + lax.axis_index("dp")
-    begin = tables[4, row, col]
+    begin = corner_y[col, row]
 
     def body(r, carry):
         for c in range(3):
@@ -293,7 +317,10 @@
 
 def train_kernel(
     grad_scale,
-    tables,
+    patch_live,
+    corner_x,
+    corner_z,
+    patch_dest,
     own,
     wlo,
     whi,
@@ -320,7 +347,7 @@
 ):
     col = lax.axis_index("space")
     row = lax.axis_index("group") * lax.axis_size("dp") + lax.axis_index("dp")
-    live = tables[0, row, col]
+    live = patch_live[col, row]
 
     @pl.when(live == 0)
     def _():
@@ -328,7 +355,7 @@
 
     @pl.when(live != 0)
     def _():
-        bx, bz, dest = tables[1, row, col], tables[2, row, col], tables[3, row, col]
+        bx, bz, dest = corner_x[col, row], corner_z[col, row], patch_dest[col, row]
         window_fields(bx, own, wlo, whi, wa, wb, wc, fields)
         src[...] = jnp.zeros(src.shape, F32)
         tgt[...] = jnp.zeros(tgt.shape, F32)
@@ -483,10 +510,11 @@
     for k in range(9):
         tail = parts[117 + k % 5]
         half = k // 5
-        wide = jnp.concatenate([parts[108 + k], tail[:, 64 * half : 64 * half + 64]], axis=1)
-        turned = wide.T
+        head = parts[108 + k]
+        by_dx = (head[:, 0:64], head[:, 64:128], tail[:, 64 * half : 64 * half + 64])
         for dx in range(3):
-            first[9 * dx + k] = turned[64 * dx : 64 * dx + 64, 0:3]
+            for c in range(3):
+                first[c, 9 * dx + k : 9 * dx + k + 1, :] = by_dx[dx][c : c + 1]
     final = parts[122]
     last[...] = final[0:6, 0:64]
     corner = lane_of((8, LANES))
@@ -497,6 +525,8 @@
 
 
 VMEM = pl.BlockSpec()
+HERE = pl.BlockSpec(memory_space=pltpu.VMEM)
+AWAY = pl.BlockSpec(memory_space=pltpu.HBM)
 SMEM = pl.BlockSpec(memory_space=pltpu.SMEM)
 
 
@@ -511,8 +541,8 @@
     return pl.pallas_call(
         functools.partial(train_kernel, grad_scale),
         out_shape=jax.ShapeDtypeStruct((128, 8, LANES), F32),
-        in_specs=[SMEM] + [VMEM] * 8,
-        out_specs=VMEM,
+        in_specs=[SMEM] * 4 + [HERE] * 3 + [VMEM] * 5,
+        out_specs=HERE,
         scratch_shapes=[
             pltpu.VMEM((3, height, 8, LANES), F32),
             pltpu.VMEM((3, height, 8, LANES), F32),
@@ -529,19 +559,21 @@
             pltpu.VMEM((192, whole + 2 * CELLS), BF16),
             pltpu.VMEM((192, 576), F32),
         ],
-        compiler_params=params(60),
+        compiler_params=params(40),
         cost_estimate=pl.CostEstimate(flops=10**7, bytes_accessed=6 * 10**7, transcendentals=0),
-    )(tables, own, wlo, whi, *weights)
-
-
-def weight_kernel(first, mid, last, w1, w2, w2b, wl, wlt):
-    none = jnp.zeros((64, 5), F32)
+    )(*tables, own, wlo, whi, *weights)
+
+
+def weight_kernel(first_h, mid_h, last_h, w1, w2, w2b, wl, wlt, small, first, mid, last, sems):
+    fetch((first_h, mid_h, last_h), (first, mid, last), sems)
+    small[...] = jnp.zeros(small.shape, F32)
+    for c in range(3):
+        value = first[c].astype(F32)
+        for dx in range(3):
+            small[dx, pl.ds(c, 9, stride=8), :] = value[9 * dx : 9 * dx + 9]
     for dx in range(3):
         rows = slice(64 * dx, 64 * dx + 64)
-        small = []
-        for k in range(9):
-            small += [first[9 * dx + k].astype(F32), none]
-        w1[rows] = jnp.concatenate(small, axis=1).astype(BF16)
+        w1[rows] = small[dx].T.astype(BF16)
         blocks = [mid[9 * dx + k].astype(F32) for k in range(9)]
         w2[rows] = jnp.concatenate(blocks, axis=1).astype(BF16)
         w2b[rows] = jnp.concatenate(blocks[::-1], axis=0).T.astype(BF16)
@@ -555,10 +587,17 @@
     return pl.pallas_call(
         weight_kernel,
         out_shape=tuple(jax.ShapeDtypeStruct(s, BF16) for s in shapes),
-        in_specs=[VMEM] * 3,
-        out_specs=(VMEM,) * 5,
-        compiler_params=params(60),
-    )(conv_first, conv_mid, conv_last)
+        in_specs=[AWAY] * 3,
+        out_specs=(HERE,) * 5,
+        scratch_shapes=[
+            pltpu.VMEM((3, 72, 64), F32),
+            pltpu.VMEM((3, 27, 64), BF16),
+            pltpu.VMEM((27, 64, 64), BF16),
+            pltpu.VMEM((6, 64), BF16),
+            pltpu.SemaphoreType.DMA((3,)),
+        ],
+        compiler_params=params(8),
+    )(conv_first.transpose(2, 0, 1), conv_mid, conv_last)
 
 
 def local(
@@ -573,13 +612,15 @@
     up_col = [(i, (i + 1) % cols_n) for i in range(cols_n)]
     down_col = [(j, i) for i, j in up_col]
 
-    tables = jnp.stack([patch_live, corner_x, corner_z, patch_dest, corner_y])
+    tables = (patch_live.T, corner_x.T, corner_z.T, patch_dest.T)
+    corner_y = corner_y.T
+    corner_scratch = [pltpu.SMEM(corner_y.shape, jnp.int32), pltpu.SemaphoreType.DMA((1,))]
     lo, hi = pl.pallas_call(
         pack_kernel,
         out_shape=(strip, strip),
         in_specs=[VMEM],
-        out_specs=(VMEM, VMEM),
-        compiler_params=params(60),
+        out_specs=(HERE, HERE),
+        compiler_params=params(8),
     )(velocity)
     left = lax.ppermute(hi, "space", up_col)
     right = lax.ppermute(lo, "space", down_col)
@@ -587,20 +628,22 @@
     up, down = pl.pallas_call(
         functools.partial(edge_kernel, row_count),
         out_shape=(edge, edge),
-        in_specs=[SMEM] + [VMEM] * 3,
-        out_specs=(VMEM, VMEM),
-        compiler_params=params(60),
-    )(tables, velocity, left, right)
+        in_specs=[AWAY, VMEM, HERE, HERE],
+        out_specs=(HERE, HERE),
+        scratch_shapes=corner_scratch,
+        compiler_params=params(8),
+    )(corner_y, velocity, left, right)
     wlo = lax.ppermute(up, ROWS, up_row)
     whi = lax.ppermute(down, ROWS, down_row)
     face = jax.ShapeDtypeStruct((3, HALO + 1, levels, LANES), F32)
     own, to_up, to_down = pl.pallas_call(
         own_kernel,
         out_shape=(jax.ShapeDtypeStruct((3, count, 8, LANES), F32), face, face),
-        in_specs=[SMEM] + [VMEM] * 3,
-        out_specs=(VMEM,) * 3,
-        compiler_params=params(60),
-    )(tables, velocity, left, right)
+        in_specs=[AWAY, VMEM, HERE, HERE],
+        out_specs=(HERE,) * 3,
+        scratch_shapes=corner_scratch,
+        compiler_params=params(12),
+    )(corner_y, velocity, left, right)
     weights = layer_weights(conv_first, conv_mid, conv_last)
     to_up, to_down, wlo, whi, weights = lax.optimization_barrier(
         (to_up, to_down, wlo, whi, weights)
@@ -619,13 +662,18 @@
             jax.ShapeDtypeStruct(velocity.shape, F32),
             jax.ShapeDtypeStruct((3, height - 4, levels, wide), F32),
         ),
-        in_specs=[VMEM] * 5,
+        in_specs=[VMEM] + [AWAY] * 4,
         out_specs=(VMEM, VMEM),
         scratch_shapes=[
             pltpu.VMEM((3, height, levels, wide), F32),
             pltpu.VMEM((3, height - 2, levels, wide), F32),
+            pltpu.VMEM(xlo.shape, F32),
+            pltpu.VMEM(xhi.shape, F32),
+            pltpu.VMEM(left.shape, F32),
+            pltpu.VMEM(right.shape, F32),
+            pltpu.SemaphoreType.DMA((4,)),
         ],
-        compiler_params=params(60),
+        compiler_params=params(24),
         cost_estimate=pl.CostEstimate(flops=10**7, bytes_accessed=4 * 10**7, transcendentals=0),
     )(velocity, xlo, xhi, left, right)
     shares, wide_next = lax.optimization_barrier((shares, wide_next))
@@ -637,7 +685,8 @@
         ),
         in_specs=[VMEM],
         out_specs=(VMEM, VMEM),
-        compiler_params=params(60),
+        scratch_shapes=[pltpu.VMEM((2, count * levels, 6 * LANES), BF16)],
+        compiler_params=params(24),
         cost_estimate=pl.CostEstimate(flops=10**7, bytes_accessed=4 * 10**7, transcendentals=0),
     )(wide_next)
     mine = jnp.sum(shares, axis=0, keepdims=True)
@@ -645,16 +694,16 @@
     grad_first, grad_mid, grad_last, loss = pl.pallas_call(
         unpack_kernel,
         out_shape=(
-            jax.ShapeDtypeStruct((27, 64, 3), F32),
+            jax.ShapeDtypeStruct((3, 27, 64), F32),
             jax.ShapeDtypeStruct((27, 64, 64), F32),
             jax.ShapeDtypeStruct((6, 64), F32),
             jax.ShapeDtypeStruct((1,), F32),
         ),
-        in_specs=[VMEM],
+        in_specs=[HERE],
         out_specs=(VMEM, VMEM, VMEM, SMEM),
-        compiler_params=params(60),
+        compiler_params=params(8),
     )(summed)
-    return (nxt, filt, stress, grad_first, grad_mid, grad_last, loss)
+    return (nxt, filt, stress, grad_first.transpose(1, 2, 0), grad_mid, grad_last, loss)
 
 
 def solution(mesh):

time: 95.5 us -> 85.3 us (0.89)
  Pallas kernels: 41.4 us -> 18.6 us
  waiting for transfers between devices: 7.41 us -> 23.9 us
  starting transfers between devices: 34.4 us -> 29.1 us
  other arithmetic: 0.14 us -> 1.18 us
    pallas_call x1, Pallas kernels: 13.9 us -> 5.18 us  [local(): pl.pallas_call(filter_kernel, out_shape=(jax.ShapeDtypeStruct(velocity.sh...]
    all_to_all x1, waiting for transfers between devices: 0.01 us -> 8.4 us  [local(): lax.all_to_all(jnp.broadcast_to(mine, parts.shape), EVERY, 0, 0, tiled=True)]
    pallas_call x1, Pallas kernels: 11.5 us -> 6.23 us  [local(): pl.pallas_call(solver_kernel, out_shape=(jax.ShapeDtypeStruct(velocity.sh...]
    all_to_all x1, starting transfers between devices: 13.2 us -> 9.13 us  [local(): shares = lax.all_to_all(parts, EVERY, 0, 0, tiled=True)]
    unnamed x22 -> x38, local copies, waits for them, and re-layouts: 5.97 us -> 9.98 us
    another operation x6 -> x0, local copies, waits for them, and re-layouts: 3.79 us -> none  [local(): tables = jnp.stack([patch_live, corner_x, corner_z, patch_dest, corner_y])]
    ppermute x1, waiting for transfers between devices: 5.32 us -> 8.58 us  [local(): xlo = lax.ppermute(to_up, ROWS, up_row)]
    ppermute x1, waiting for transfers between devices: 0.01 us -> 2.33 us  [local(): right = lax.ppermute(lo, 'space', down_col)]
  transfers between devices with their start and end apart: 8 -> 8, of which waited for: 2 -> 5; matrix products, arithmetic and copies ran while one was open for 6% -> 0% of each run, Pallas kernels for 36% -> 19%
where the time goes in v3:
time: 85.3 us; the launch traced here: 84.6 us
  starting transfers between devices  29.1 us (34%)
  waiting for transfers between devices  23.9 us (28%)
  Pallas kernels  18.6 us (22%)
  local copies, waits for them, and re-layouts  10.8 us (13%)
  other arithmetic  1.18 us (1%)
  between operations  0.96 us (1%)
    unnamed x38, local copies, waits for them, and re-layouts  9.98 us
    all_to_all x1, starting transfers between devices, local(): shares = lax.all_to_all(parts, EVERY, 0, 0, tiled=True)  9.13 us
    ppermute x1, waiting for transfers between devices, local(): xlo = lax.ppermute(to_up, ROWS, up_row)  8.58 us
    all_to_all x1, waiting for transfers between devices, local(): lax.all_to_all(jnp.broadcast_to(mine, parts.shape), EVERY, 0, 0, tiled=True)  8.4 us
    all_to_all x1, starting transfers between devices, local(): lax.all_to_all(jnp.broadcast_to(mine, parts.shape), EVERY, 0, 0, tiled=True)  6.32 us
    pallas_call x1, Pallas kernels, local(): pl.pallas_call(solver_kernel, out_shape=(jax.ShapeDtypeStruct(velocity.sh...  6.23 us
    pallas_call x1, Pallas kernels, local(): pl.pallas_call(filter_kernel, out_shape=(jax.ShapeDtypeStruct(velocity.sh...  5.18 us
    ppermute x1, starting transfers between devices, local(): xhi = lax.ppermute(to_down, ROWS, down_row)  4.25 us
  transfers between devices with their start and end apart: 8, of which 5 were waited for; matrix products, arithmetic and copies ran while one was open for 0% of the time, Pallas kernels for 19%

profile of v3, /device:TPU:1, one launch (start us, length us, event | category | flops | bytes accessed | tf_op | source)
XLA Modules:
  0.0 84.6 jit_solution(7147370237688208354)
XLA Ops:
  0.6 0.0 copy-start
  0.6 1.2 %copy-done = f32[3,20,32,128]{3,2,1,0:T(8,128)S(1)} copy-done((f32[3,20,32,128]{3,2,1,0:T(8,128)S(1)}, f32[3,20,32,128]{3,2,1,0:T(8,128)}, u32[]{:S(2)}) %copy-start) | copy-done | bytes 983064
  1.8 0.0 copy-start.1
  1.8 0.0 copy-start.14
  1.8 0.6 shard_map.144
  2.4 2.7 %collective-permute-start = (f32[3,32,128]{2,1,0:T(8,128)S(1)}, f32[3,32,128]{2,1,0:T(8,128)S(1)}, u32[]{:S(2)}, u32[]{:S(2)}) collective-permute-start(f32[3,32,128]{2,1,0:T(8,128)S(1)} %get-tuple-element.42), channel_id=1, source_target_pairs={{0,1},{1,2},{2,3},{3,4},{4,5},{5,6},{6,7},{7,0},{8,9},{9,10},{10,1... | collective-permute-start | bytes 147464 | tf_op jit(solution)/shard_map/ppermute | solution.py:625
  5.1 0.0 collective-permute-start.1
  5.1 1.2 %collective-permute-done.left.left_h = f32[3,32,128]{2,1,0:T(8,128)S(1)} collective-permute-done((f32[3,32,128]{2,1,0:T(8,128)S(1)}, f32[3,32,128]{2,1,0:T(8,128)S(1)}, u32[]{:S(2)}, u32[]{:S(2)}) %collective-permute-start) | collective-permute-done | bytes 49184 | tf_op jit(solution)/shard_map/ppermute | solution.py:625
  6.3 0.0 copy-start.2
  6.3 2.3 %collective-permute-done.1.right.right_h = f32[3,32,128]{2,1,0:T(8,128)S(1)} collective-permute-done((f32[3,32,128]{2,1,0:T(8,128)S(1)}, f32[3,32,128]{2,1,0:T(8,128)S(1)}, u32[]{:S(2)}, u32[]{:S(2)}) %collective-permute-start.1) | collective-permute-done | bytes 49184 | tf_op jit(solution)/shard_map/ppermute | solution.py:626
  8.6 0.0 copy-start.4
  8.6 0.0 copy-start.12
  8.6 0.7 copy-done.12
  9.3 0.0 copy-start.15
  9.3 0.0 copy-start.16
  9.3 0.0 copy-start.17
  9.3 1.1 %shard_map.146 = (f32[3,5,8,128]{3,2,1,0:T(8,128)S(1)}, f32[3,5,8,128]{3,2,1,0:T(8,128)S(1)}) custom-call(s32[8,16]{1,0:T(8,128)S(1)} %bitcast.8, f32[3,20,32,128]{3,2,1,0:T(8,128)S(1)} %copy-done, f32[3,32,128]{2,1,0:T(8,128)S(1)} %collective-permute-done.left.left_h, f32[3,32,128]{2,1,0:T(8,128)S(1)} %collective-permute-done.1.right.right_h), custom_call_target="tpu_custom_call" | custom-call | tf_op jit(solution)/shard_map/pallas_call | solution.py:628
  10.5 3.7 %collective-permute-start.2 = (f32[3,5,8,128]{3,2,1,0:T(8,128)S(1)}, f32[3,5,8,128]{3,2,1,0:T(8,128)S(1)}, u32[]{:S(2)}, u32[]{:S(2)}) collective-permute-start(f32[3,5,8,128]{3,2,1,0:T(8,128)S(1)} %get-tuple-element.47), channel_id=1, source_target_pairs={{0,8},{8,16},{16,24},{24,32},{32,40},{40,48},{48,56},{56,64},{64,7... | collective-permute-start | bytes 184328 | tf_op jit(solution)/shard_map/ppermute | solution.py:636
  14.2 2.4 %collective-permute-start.3 = (f32[3,5,8,128]{3,2,1,0:T(8,128)S(1)}, f32[3,5,8,128]{3,2,1,0:T(8,128)S(1)}, u32[]{:S(2)}, u32[]{:S(2)}) collective-permute-start(f32[3,5,8,128]{3,2,1,0:T(8,128)S(1)} %get-tuple-element.48), channel_id=1, source_target_pairs={{8,0},{16,8},{24,16},{32,24},{40,32},{48,40},{56,48},{64,56},{72,6... | collective-permute-start | bytes 184328 | tf_op jit(solution)/shard_map/ppermute | solution.py:637
  16.6 0.0 copy-start.6
  16.6 1.0 %copy-done.6 = bf16[27,64,64]{2,1,0:T(8,128)(2,1)S(1)} copy-done((bf16[27,64,64]{2,1,0:T(8,128)(2,1)S(1)}, bf16[27,64,64]{2,1,0:T(8,128)(2,1)}, u32[]{:S(2)}) %copy-start.6) | copy-done | bytes 221208
  17.6 0.0 copy-start.11
  17.6 0.7 copy-done.11
  18.3 0.0 copy-start.18
  18.3 0.7 copy-done.18
  19.0 0.6 shard_map.147
  19.6 0.0 copy-done.2
  19.6 0.0 copy-done.1
  19.7 0.0 copy-start.13
  19.7 0.7 copy-done.13
  20.3 1.9 %shard_map.145 = (f32[3,20,8,128]{3,2,1,0:T(8,128)S(1)}, f32[3,6,32,128]{3,2,1,0:T(8,128)S(1)}, f32[3,6,32,128]{3,2,1,0:T(8,128)S(1)}) custom-call(s32[8,16]{1,0:T(8,128)S(1)} %bitcast.9, f32[3,20,32,128]{3,2,1,0:T(8,128)S(1)} %copy-done.1, f32[3,32,128]{2,1,0:T(8,128)S(1)} %collective-permute-done.left.left_h, ...), custom_call_target="tpu_custom_call" | custom-call | tf_op jit(solution)/shard_map/pallas_call | solution.py:639
  22.3 0.0 copy-done.4
  22.3 0.0 collective-permute-done.2.wlo
  22.3 0.0 collective-permute-done.3.whi
  22.3 0.6 collective-permute-start.4
  22.9 4.3 %collective-permute-start.5 = (f32[3,6,32,128]{3,2,1,0:T(8,128)S(1)}, f32[3,6,32,128]{3,2,1,0:T(8,128)S(1)}, u32[]{:S(2)}, u32[]{:S(2)}) collective-permute-start(f32[3,6,32,128]{3,2,1,0:T(8,128)S(1)} %get-tuple-element.62), channel_id=1, source_target_pairs={{8,0},{16,8},{24,16},{32,24},{40,32},{48,40},{56,48},{64,56},{72,6... | collective-permute-start | bytes 884744 | tf_op jit(solution)/shard_map/ppermute | solution.py:652
  27.2 0.0 copy-done.14
  27.2 0.0 copy-done.15
  27.2 0.0 copy-done.16
  27.2 0.0 copy-done.17
  27.2 1.8 %shard_map.148 = f32[128,8,128]{2,1,0:T(8,128)} custom-call(s32[8,16]{1,0:T(8,128)S(1)} %bitcast.10, s32[8,16]{1,0:T(8,128)S(1)} %bitcast.11, s32[8,16]{1,0:T(8,128)S(1)} %bitcast.12, s32[8,16]{1,0:T(8,128)S(1)} %bitcast.13, f32[3,20,8,128]{3,2,1,0:T(8,128)S(1)} %get-tuple-element.44.own, f32[3,5,8,128]{3,2,1,0:T(8,128)S(1)} %collective-permute-done.2.wlo, ...), custom_call_target="tpu_custom_call" | custom-call | flops 10000000 | bytes 60000000 | tf_op jit(solution)/shard_map/pallas_call | solution.py:541
  29.0 8.6 %collective-permute-done.4.xlo_h = f32[3,6,32,128]{3,2,1,0:T(8,128)S(1)} collective-permute-done((f32[3,6,32,128]{3,2,1,0:T(8,128)S(1)}, f32[3,6,32,128]{3,2,1,0:T(8,128)S(1)}, u32[]{:S(2)}, u32[]{:S(2)}) %collective-permute-start.4) | collective-permute-done | bytes 294944 | tf_op jit(solution)/shard_map/ppermute | solution.py:651
  37.6 0.0 copy-start.7
  37.6 0.7 copy-done.7
  38.3 0.0 collective-permute-done.5.xhi_h
  38.3 0.0 copy-start.9
  38.3 0.7 copy-done.9
  39.0 9.1 %all-to-all-start = ((f32[128,8,128]{2,1,0:T(8,128)}), f32[128,8,128]{2,1,0:T(8,128)}, u32[]{:S(2)}, u32[]{:S(2)}) async-start(f32[128,8,128]{2,1,0:T(8,128)} %shard_map.148), calls=%async_computation | async-start | bytes 1048576 | tf_op jit(solution)/shard_map/all_to_all | solution.py:656
  48.2 0.0 copy-start.3
  48.2 0.8 copy-done.3
  49.0 0.0 copy-start.5
  49.0 0.8 copy-done.5
  49.8 0.0 copy-start.8
  49.8 1.0 %copy-done.8 = f32[3,6,32,128]{3,2,1,0:T(8,128)S(1)} copy-done((f32[3,6,32,128]{3,2,1,0:T(8,128)S(1)}, f32[3,6,32,128]{3,2,1,0:T(8,128)}, u32[]{:S(2)}) %copy-start.8) | copy-done | bytes 294936
  50.7 0.0 copy-start.10
  50.7 1.0 %copy-done.10 = f32[3,6,32,128]{3,2,1,0:T(8,128)S(1)} copy-done((f32[3,6,32,128]{3,2,1,0:T(8,128)S(1)}, f32[3,6,32,128]{3,2,1,0:T(8,128)}, u32[]{:S(2)}) %copy-start.10) | copy-done | bytes 294936
  51.7 6.2 %shard_map.149 = (f32[3,20,32,128]{3,2,1,0:T(8,128)}, f32[3,26,32,256]{3,2,1,0:T(8,128)S(1)}) custom-call(f32[3,20,32,128]{3,2,1,0:T(8,128)S(1)} %copy-done.1, f32[3,6,32,128]{3,2,1,0:T(8,128)S(1)} %copy-done.8, f32[3,6,32,128]{3,2,1,0:T(8,128)S(1)} %copy-done.10, f32[3,32,128]{2,1,0:T(8,128)S(1)} %copy-done.3, f32[3,32,128]{2,1,0:T(8,128)S(1)} %copy-done.5), custom_call_target="tpu_custom_call" | custom-call | flops 10000000 | bytes 40000000 | tf_op jit(solution)/shard_map/pallas_call | solution.py:659
  57.9 3.4 %all-to-all-done = f32[128,8,128]{2,1,0:T(8,128)} async-done(((f32[128,8,128]{2,1,0:T(8,128)}), f32[128,8,128]{2,1,0:T(8,128)}, u32[]{:S(2)}, u32[]{:S(2)}) %all-to-all-start) | async-done | bytes 524320 | tf_op jit(solution)/shard_map/all_to_all | solution.py:656
  61.4 1.2 %reduce_sum.9 = f32[8,128]{1,0:T(8,128)S(1)} reduce(f32[128,8,128]{2,1,0:T(8,128)} %all-to-all-done, f32[]{:T(128)} %constant.0.clone.1), dimensions={0}, to_apply=%region_0.0 | reduce | flops 130048 | bytes 528388 | tf_op jit(solution)/shard_map/reduce_sum | solution.py:692
  62.6 0.8 broadcast_in_dim.2
  63.4 6.3 %all-to-all-start.1 = ((f32[128,8,128]{2,1,0:T(8,128)}), f32[128,8,128]{2,1,0:T(8,128)S(1)}, u32[]{:S(2)}, u32[]{:S(2)}) async-start(f32[128,8,128]{2,1,0:T(8,128)} %broadcast_in_dim.2), calls=%async_computation.1 | async-start | bytes 1048576 | tf_op jit(solution)/shard_map/all_to_all | solution.py:693
  69.7 5.2 %shard_map.150 = (f32[3,20,32,128]{3,2,1,0:T(8,128)}, f32[6,20,32,128]{3,2,1,0:T(8,128)}) custom-call(f32[3,26,32,256]{3,2,1,0:T(8,128)S(1)} %get-tuple-element.69.wa), custom_call_target="tpu_custom_call" | custom-call | flops 10000000 | bytes 40000000 | tf_op jit(solution)/shard_map/pallas_call | solution.py:680
  74.9 8.4 %all-to-all-done.1.parts = f32[128,8,128]{2,1,0:T(8,128)S(1)} async-done(((f32[128,8,128]{2,1,0:T(8,128)}), f32[128,8,128]{2,1,0:T(8,128)S(1)}, u32[]{:S(2)}, u32[]{:S(2)}) %all-to-all-start.1) | async-done | bytes 524320 | tf_op jit(solution)/shard_map/all_to_all | solution.py:693
  83.3 1.1 %shard_map.151 = (f32[3,27,64]{2,1,0:T(8,128)}, f32[27,64,64]{2,1,0:T(8,128)}, f32[6,64]{1,0:T(8,128)}, f32[1]{0:T(128)}) custom-call(f32[128,8,128]{2,1,0:T(8,128)S(1)} %all-to-all-done.1.parts), custom_call_target="tpu_custom_call" | custom-call | tf_op jit(solution)/shard_map/pallas_call | solution.py:694
Async XLA Ops:
  0.6 1.2 %copy-start = (f32[3,20,32,128]{3,2,1,0:T(8,128)S(1)}, f32[3,20,32,128]{3,2,1,0:T(8,128)}, u32[]{:S(2)}) copy-start(f32[3,20,32,128]{3,2,1,0:T(8,128)} %vel.6) | copy-start | bytes 2949124
  1.8 17.8 %copy-start.1 = (f32[3,20,32,128]{3,2,1,0:T(8,128)S(1)}, f32[3,20,32,128]{3,2,1,0:T(8,128)}, u32[]{:S(2)}) copy-start(f32[3,20,32,128]{3,2,1,0:T(8,128)} %vel.6) | copy-start | bytes 2949124
  1.8 25.3 %copy-start.14 = (s32[16,8]{0,1:T(8,128)S(1)}, s32[16,8]{0,1:T(8,128)}, u32[]{:S(2)}) copy-start(s32[16,8]{0,1:T(8,128)} %param.16) | copy-start | bytes 1540
  2.4 3.9 %collective-permute-start = (f32[3,32,128]{2,1,0:T(8,128)S(1)}, f32[3,32,128]{2,1,0:T(8,128)S(1)}, u32[]{:S(2)}, u32[]{:S(2)}) collective-permute-start(f32[3,32,128]{2,1,0:T(8,128)S(1)} %get-tuple-element.42), channel_id=1, source_target_pairs={{0,1},{1,2},{2,3},{3,4},{4,5},{5,6},{6,7},{7,0},{8,9},{9,10},{10,1... | collective-permute-start | bytes 147464 | tf_op jit(solution)/shard_map/ppermute | solution.py:625
  5.1 3.5 %collective-permute-start.1 = (f32[3,32,128]{2,1,0:T(8,128)S(1)}, f32[3,32,128]{2,1,0:T(8,128)S(1)}, u32[]{:S(2)}, u32[]{:S(2)}) collective-permute-start(f32[3,32,128]{2,1,0:T(8,128)S(1)} %get-tuple-element.43), channel_id=1, source_target_pairs={{1,0},{2,1},{3,2},{4,3},{5,4},{6,5},{7,6},{0,7},{9,8},{10,9},{11,1... | collective-permute-start | bytes 147464 | tf_op jit(solution)/shard_map/ppermute | solution.py:626
  6.3 13.4 %copy-start.2 = (f32[3,32,128]{2,1,0:T(8,128)}, f32[3,32,128]{2,1,0:T(8,128)S(1)}, u32[]{:S(2)}) copy-start(f32[3,32,128]{2,1,0:T(8,128)S(1)} %collective-permute-done.left.left_h) | copy-start | bytes 147460
  8.6 13.7 %copy-start.4 = (f32[3,32,128]{2,1,0:T(8,128)}, f32[3,32,128]{2,1,0:T(8,128)S(1)}, u32[]{:S(2)}) copy-start(f32[3,32,128]{2,1,0:T(8,128)S(1)} %collective-permute-done.1.right.right_h) | copy-start | bytes 147460
  8.6 0.7 copy-start.12
  9.3 17.8 %copy-start.15 = (s32[16,8]{0,1:T(8,128)S(1)}, s32[16,8]{0,1:T(8,128)}, u32[]{:S(2)}) copy-start(s32[16,8]{0,1:T(8,128)} %param.13) | copy-start | bytes 1540
  9.3 17.8 %copy-start.16 = (s32[16,8]{0,1:T(8,128)S(1)}, s32[16,8]{0,1:T(8,128)}, u32[]{:S(2)}) copy-start(s32[16,8]{0,1:T(8,128)} %param.14) | copy-start | bytes 1540
  9.3 17.8 %copy-start.17 = (s32[16,8]{0,1:T(8,128)S(1)}, s32[16,8]{0,1:T(8,128)}, u32[]{:S(2)}) copy-start(s32[16,8]{0,1:T(8,128)} %param.17) | copy-start | bytes 1540
  10.5 11.8 %collective-permute-start.2 = (f32[3,5,8,128]{3,2,1,0:T(8,128)S(1)}, f32[3,5,8,128]{3,2,1,0:T(8,128)S(1)}, u32[]{:S(2)}, u32[]{:S(2)}) collective-permute-start(f32[3,5,8,128]{3,2,1,0:T(8,128)S(1)} %get-tuple-element.47), channel_id=1, source_target_pairs={{0,8},{8,16},{16,24},{24,32},{32,40},{40,48},{48,56},{56,64},{64,7... | collective-permute-start | bytes 184328 | tf_op jit(solution)/shard_map/ppermute | solution.py:636
  14.2 8.1 %collective-permute-start.3 = (f32[3,5,8,128]{3,2,1,0:T(8,128)S(1)}, f32[3,5,8,128]{3,2,1,0:T(8,128)S(1)}, u32[]{:S(2)}, u32[]{:S(2)}) collective-permute-start(f32[3,5,8,128]{3,2,1,0:T(8,128)S(1)} %get-tuple-element.48), channel_id=1, source_target_pairs={{8,0},{16,8},{24,16},{32,24},{40,32},{48,40},{56,48},{64,56},{72,6... | collective-permute-start | bytes 184328 | tf_op jit(solution)/shard_map/ppermute | solution.py:637
  16.6 1.0 %copy-start.6 = (bf16[27,64,64]{2,1,0:T(8,128)(2,1)S(1)}, bf16[27,64,64]{2,1,0:T(8,128)(2,1)}, u32[]{:S(2)}) copy-start(bf16[27,64,64]{2,1,0:T(8,128)(2,1)} %mid_h.1) | copy-start | bytes 663556
  17.6 0.7 copy-start.11
  18.3 0.7 copy-start.18
  19.7 0.7 copy-start.13
  22.3 15.3 %collective-permute-start.4 = (f32[3,6,32,128]{3,2,1,0:T(8,128)S(1)}, f32[3,6,32,128]{3,2,1,0:T(8,128)S(1)}, u32[]{:S(2)}, u32[]{:S(2)}) collective-permute-start(f32[3,6,32,128]{3,2,1,0:T(8,128)S(1)} %get-tuple-element.61), channel_id=1, source_target_pairs={{0,8},{8,16},{16,24},{24,32},{32,40},{40,48},{48,56},{56,64},{64,7... | collective-permute-start | bytes 884744 | tf_op jit(solution)/shard_map/ppermute | solution.py:651
  22.9 15.4 %collective-permute-start.5 = (f32[3,6,32,128]{3,2,1,0:T(8,128)S(1)}, f32[3,6,32,128]{3,2,1,0:T(8,128)S(1)}, u32[]{:S(2)}, u32[]{:S(2)}) collective-permute-start(f32[3,6,32,128]{3,2,1,0:T(8,128)S(1)} %get-tuple-element.62), channel_id=1, source_target_pairs={{8,0},{16,8},{24,16},{32,24},{40,32},{48,40},{56,48},{64,56},{72,6... | collective-permute-start | bytes 884744 | tf_op jit(solution)/shard_map/ppermute | solution.py:652
  37.6 0.7 copy-start.7
  38.3 0.7 copy-start.9
  39.0 22.4 %all-to-all-start = ((f32[128,8,128]{2,1,0:T(8,128)}), f32[128,8,128]{2,1,0:T(8,128)}, u32[]{:S(2)}, u32[]{:S(2)}) async-start(f32[128,8,128]{2,1,0:T(8,128)} %shard_map.148), calls=%async_computation | async-start | bytes 1048576 | tf_op jit(solution)/shard_map/all_to_all | solution.py:656
  48.2 0.8 copy-start.3
  49.0 0.8 copy-start.5
  49.8 1.0 %copy-start.8 = (f32[3,6,32,128]{3,2,1,0:T(8,128)S(1)}, f32[3,6,32,128]{3,2,1,0:T(8,128)}, u32[]{:S(2)}) copy-start(f32[3,6,32,128]{3,2,1,0:T(8,128)} %copy-done.7) | copy-start | bytes 884740
  50.7 1.0 %copy-start.10 = (f32[3,6,32,128]{3,2,1,0:T(8,128)S(1)}, f32[3,6,32,128]{3,2,1,0:T(8,128)}, u32[]{:S(2)}) copy-start(f32[3,6,32,128]{3,2,1,0:T(8,128)} %copy-done.9) | copy-start | bytes 884740
  63.4 19.9 %all-to-all-start.1 = ((f32[128,8,128]{2,1,0:T(8,128)}), f32[128,8,128]{2,1,0:T(8,128)S(1)}, u32[]{:S(2)}, u32[]{:S(2)}) async-start(f32[128,8,128]{2,1,0:T(8,128)} %broadcast_in_dim.2), calls=%async_computation.1 | async-start | bytes 1048576 | tf_op jit(solution)/shard_map/all_to_all | solution.py:693

commit v4 on v3

--- a/solution.py
+++ b/solution.py
@@ -34,7 +34,7 @@
     return pltpu.roll(value, shift, axis)
 
 
-def pack_kernel(vel, lo, hi):
+def pack_kernel(vel, lo, hi, low_rows, high_rows):
     count = vel.shape[1]
     lane = lane_of((vel.shape[2], LANES))
     for c in range(3):
@@ -47,6 +47,8 @@
             last = jnp.where(here, roll(row, HALO * r + HALO), last)
         lo[c] = first
         hi[c] = last
+        low_rows[c] = vel[c, 0:HALO]
+        high_rows[c] = vel[c, count - HALO :]
 
 
 def faces(vel, left, right, up, down):
@@ -196,25 +198,26 @@
     return out
 
 
-def edge_kernel(rows, corner_h, vel, left, right, up, down, corner_y, sems):
+def entries(word):
+    return word & 1, (word >> 1) & 7, (word >> 4) & 63, (word >> 10) & 255, word >> 18
+
+
+def edge_kernel(rows, count, table, low_rows, high_rows, left, right, up, down):
     col = lax.axis_index("space")
     row = lax.axis_index("group") * lax.axis_size("dp") + lax.axis_index("dp")
-    fetch((corner_h,), (corner_y,), sems)
-    count = vel.shape[1]
-    begin_up = corner_y[col, lax.rem(row + 1, rows)]
-    begin_down = corner_y[col, lax.rem(row + rows - 1, rows)]
+    begin_up = entries(table[col, lax.rem(row + 1, rows)])[3]
+    begin_down = entries(table[col, lax.rem(row + rows - 1, rows)])[3]
     for c in range(3):
         for k in range(HALO):
             r = count - HALO + k
-            up[c, k] = window_row(vel[c, r], left[c], right[c], r, begin_up)
-            down[c, k] = window_row(vel[c, k], left[c], right[c], k, begin_down)
-
-
-def own_kernel(corner_h, vel, left, right, out, up, down, corner_y, sems):
-    fetch((corner_h,), (corner_y,), sems)
+            up[c, k] = window_row(high_rows[c, k], left[c], right[c], r, begin_up)
+            down[c, k] = window_row(low_rows[c, k], left[c], right[c], k, begin_down)
+
+
+def own_kernel(table, vel, left, right, out, up, down):
     col = lax.axis_index("space")
     row = lax.axis_index("group") * lax.axis_size("dp") + lax.axis_index("dp")
-    begin = corner_y[col, row]
+    begin = entries(table[col, row])[3]
 
     def body(r, carry):
         for c in range(3):
@@ -225,7 +228,7 @@
     faces(vel, left, right, up, down)
 
 
-def window_fields(bx, own, wlo, whi, wa, wb, wc, fields):
+def window_steps(bx, own, wlo, whi, wa, wb, wc):
     count = own.shape[1]
     wa[:, 0:HALO] = wlo[...]
     wa[:, HALO : HALO + count] = own[...]
@@ -259,16 +262,18 @@
         near = 15.0 * (roll(f, -1) + roll(f, 1)) + 6.0 * (roll(f, -2) + roll(f, 2))
         return (20.0 * f + near + (roll(f, -3) + roll(f, 3))) * (1.0 / 4096.0)
 
+    return along_y
+
+
+def window_field(f, along_y, wc, fields):
     for r in range(PE):
-        rows = [[wc[c, r + k] for k in range(7)] for c in range(3)]
-        done = [along_y(along_x(rows[c])) for c in range(3)]
         at = slice(r * 8, r * 8 + 8)
-        for c in range(3):
-            fields[c, at] = done[c]
-        small = products(*done)
-        for i, (a, b) in enumerate(PAIRS):
-            big = along_y(along_x([rows[a][k] * rows[b][k] for k in range(7)]))
-            fields[3 + i, at] = big - small[i]
+        if f < 3:
+            fields[f, at] = along_y(along_x([wc[f, r + k] for k in range(7)]))
+        else:
+            a, b = PAIRS[f - 3]
+            big = along_y(along_x([wc[a, r + k] * wc[b, r + k] for k in range(7)]))
+            fields[f, at] = big - fields[a, at] * fields[b, at]
 
 
 def views_of(even, odd):
@@ -315,21 +320,43 @@
             to[height * k : height * (k + 1), half_cols(x, half)] = pair[half]
 
 
+def layer_weights(first, mid, last, w1, w2, wl, wlt, small):
+    small[...] = jnp.zeros(small.shape, F32)
+    for c in range(3):
+        value = first[c].astype(F32)
+        for dx in range(3):
+            small[dx, pl.ds(c, 9, stride=8), :] = value[9 * dx : 9 * dx + 9]
+    for dx in range(3):
+        rows = slice(64 * dx, 64 * dx + 64)
+        w1[rows] = small[dx].T.astype(BF16)
+        blocks = [mid[9 * dx + k].astype(F32) for k in range(9)]
+        w2[rows] = jnp.concatenate(blocks, axis=1).astype(BF16)
+    padded = jnp.concatenate([last[...].astype(F32), jnp.zeros((2, 64), F32)], axis=0)
+    wl[...] = padded.astype(BF16)
+    wlt[...] = padded.T.astype(BF16)
+
+
+def backward_weights(dx, mid, w2b):
+    blocks = [mid[9 * dx + k].astype(F32) for k in range(9)]
+    w2b[64 * dx : 64 * dx + 64] = jnp.concatenate(blocks[::-1], axis=0).T.astype(BF16)
+
+
 def train_kernel(
     grad_scale,
-    patch_live,
-    corner_x,
-    corner_z,
-    patch_dest,
+    table,
     own,
     wlo,
     whi,
+    first,
+    mid,
+    last_w,
+    out,
     w1,
     w2,
     w2b,
     wl,
     wlt,
-    out,
+    small,
     wa,
     wb,
     wc,
@@ -347,7 +374,7 @@
 ):
     col = lax.axis_index("space")
     row = lax.axis_index("group") * lax.axis_size("dp") + lax.axis_index("dp")
-    live = patch_live[col, row]
+    live, bx, bz, _, dest = entries(table[col, row])
 
     @pl.when(live == 0)
     def _():
@@ -355,12 +382,14 @@
 
     @pl.when(live != 0)
     def _():
-        bx, bz, dest = corner_x[col, row], corner_z[col, row], patch_dest[col, row]
-        window_fields(bx, own, wlo, whi, wa, wb, wc, fields)
+        layer_weights(first, mid, last_w, w1, w2, wl, wlt, small)
+        along_y = window_steps(bx, own, wlo, whi, wa, wb, wc)
         src[...] = jnp.zeros(src.shape, F32)
         tgt[...] = jnp.zeros(tgt.shape, F32)
         lane16 = lane_of((PE, LANES)) // PE
-        for f in range(9):
+
+        def extract(f):
+            window_field(f, along_y, wc, fields)
             halves = [jnp.zeros((PE, LANES), F32)] * 2
             for z in range(PE):
                 deep = bz + z
@@ -372,6 +401,9 @@
             for half in range(2):
                 to[half, PE * g : PE * g + PE] = halves[half].astype(BF16).astype(F32)
 
+        for f in range(3):
+            extract(f)
+
         def row_of(ref, x):
             return jnp.concatenate(
                 [ref[half, pl.ds(x, 8, stride=PE), :] for half in range(2)], axis=1
@@ -415,6 +447,10 @@
 
         for x in range(1, PE):
             ahead(x)
+            if 3 <= x < 9:
+                extract(x)
+            elif 9 <= x < 12:
+                backward_weights(x - 9, mid, w2b)
         yb[:, cols(PE)] = dot_nn(w2[...], vv[:, cols(PE - 1)])
 
         def last(x, carry):
@@ -495,6 +531,10 @@
         out[122] = jnp.where((deep == 7) & (corner == 64 + dest), loss, padded)
         for i in range(123, 128):
             out[i] = jnp.zeros((8, LANES), F32)
+
+
+def sum_kernel(shares, out):
+    out[...] = jnp.broadcast_to(jnp.sum(shares[...], axis=0, keepdims=True), out.shape)
 
 
 def unpack_kernel(parts, first, mid, last, loss):
@@ -534,16 +574,22 @@
     return pltpu.CompilerParams(vmem_limit_bytes=mib * 1024 * 1024)
 
 
-def train_call(tables, own, wlo, whi, weights, row_count):
+def train_call(table, own, wlo, whi, weights, row_count):
     grad_scale = 2.0 / (PE**3 * row_count * LIVE_ROW)
     whole = PE * CELLS
     height = own.shape[1] + 2 * HALO
     return pl.pallas_call(
         functools.partial(train_kernel, grad_scale),
         out_shape=jax.ShapeDtypeStruct((128, 8, LANES), F32),
-        in_specs=[SMEM] * 4 + [HERE] * 3 + [VMEM] * 5,
-        out_specs=HERE,
+        in_specs=[SMEM] + [VMEM] * 6,
+        out_specs=VMEM,
         scratch_shapes=[
+            pltpu.VMEM((192, 72), BF16),
+            pltpu.VMEM((192, 576), BF16),
+            pltpu.VMEM((192, 576), BF16),
+            pltpu.VMEM((8, 64), BF16),
+            pltpu.VMEM((64, 8), BF16),
+            pltpu.VMEM((3, 72, 64), F32),
             pltpu.VMEM((3, height, 8, LANES), F32),
             pltpu.VMEM((3, height, 8, LANES), F32),
             pltpu.VMEM((3, height, 8, LANES), F32),
@@ -559,45 +605,9 @@
             pltpu.VMEM((192, whole + 2 * CELLS), BF16),
             pltpu.VMEM((192, 576), F32),
         ],
-        compiler_params=params(40),
+        compiler_params=params(60),
         cost_estimate=pl.CostEstimate(flops=10**7, bytes_accessed=6 * 10**7, transcendentals=0),
-    )(*tables, own, wlo, whi, *weights)
-
-
-def weight_kernel(first_h, mid_h, last_h, w1, w2, w2b, wl, wlt, small, first, mid, last, sems):
-    fetch((first_h, mid_h, last_h), (first, mid, last), sems)
-    small[...] = jnp.zeros(small.shape, F32)
-    for c in range(3):
-        value = first[c].astype(F32)
-        for dx in range(3):
-            small[dx, pl.ds(c, 9, stride=8), :] = value[9 * dx : 9 * dx + 9]
-    for dx in range(3):
-        rows = slice(64 * dx, 64 * dx + 64)
-        w1[rows] = small[dx].T.astype(BF16)
-        blocks = [mid[9 * dx + k].astype(F32) for k in range(9)]
-        w2[rows] = jnp.concatenate(blocks, axis=1).astype(BF16)
-        w2b[rows] = jnp.concatenate(blocks[::-1], axis=0).T.astype(BF16)
-    padded = jnp.concatenate([last[...].astype(F32), jnp.zeros((2, 64), F32)], axis=0)
-    wl[...] = padded.astype(BF16)
-    wlt[...] = padded.T.astype(BF16)
-
-
-def layer_weights(conv_first, conv_mid, conv_last):
-    shapes = ((192, 72), (192, 576), (192, 576), (8, 64), (64, 8))
-    return pl.pallas_call(
-        weight_kernel,
-        out_shape=tuple(jax.ShapeDtypeStruct(s, BF16) for s in shapes),
-        in_specs=[AWAY] * 3,
-        out_specs=(HERE,) * 5,
-        scratch_shapes=[
-            pltpu.VMEM((3, 72, 64), F32),
-            pltpu.VMEM((3, 27, 64), BF16),
-            pltpu.VMEM((27, 64, 64), BF16),
-            pltpu.VMEM((6, 64), BF16),
-            pltpu.SemaphoreType.DMA((3,)),
-        ],
-        compiler_params=params(8),
-    )(conv_first.transpose(2, 0, 1), conv_mid, conv_last)
+    )(table, own, wlo, whi, *weights)
 
 
 def local(
@@ -612,45 +622,40 @@
     up_col = [(i, (i + 1) % cols_n) for i in range(cols_n)]
     down_col = [(j, i) for i, j in up_col]
 
-    tables = (patch_live.T, corner_x.T, corner_z.T, patch_dest.T)
-    corner_y = corner_y.T
-    corner_scratch = [pltpu.SMEM(corner_y.shape, jnp.int32), pltpu.SemaphoreType.DMA((1,))]
-    lo, hi = pl.pallas_call(
+    table = (patch_live + 2 * corner_x + 16 * corner_z + 1024 * corner_y + 2**18 * patch_dest).T
+    rows5 = jax.ShapeDtypeStruct((3, HALO, levels, LANES), F32)
+    lo, hi, low_rows, high_rows = pl.pallas_call(
         pack_kernel,
-        out_shape=(strip, strip),
+        out_shape=(strip, strip, rows5, rows5),
         in_specs=[VMEM],
-        out_specs=(HERE, HERE),
+        out_specs=(HERE,) * 4,
         compiler_params=params(8),
     )(velocity)
     left = lax.ppermute(hi, "space", up_col)
     right = lax.ppermute(lo, "space", down_col)
     edge = jax.ShapeDtypeStruct((3, HALO, 8, LANES), F32)
     up, down = pl.pallas_call(
-        functools.partial(edge_kernel, row_count),
+        functools.partial(edge_kernel, row_count, count),
         out_shape=(edge, edge),
-        in_specs=[AWAY, VMEM, HERE, HERE],
+        in_specs=[SMEM] + [HERE] * 4,
         out_specs=(HERE, HERE),
-        scratch_shapes=corner_scratch,
         compiler_params=params(8),
-    )(corner_y, velocity, left, right)
+    )(table, low_rows, high_rows, left, right)
     wlo = lax.ppermute(up, ROWS, up_row)
     whi = lax.ppermute(down, ROWS, down_row)
     face = jax.ShapeDtypeStruct((3, HALO + 1, levels, LANES), F32)
     own, to_up, to_down = pl.pallas_call(
         own_kernel,
         out_shape=(jax.ShapeDtypeStruct((3, count, 8, LANES), F32), face, face),
-        in_specs=[AWAY, VMEM, HERE, HERE],
+        in_specs=[SMEM, VMEM, HERE, HERE],
         out_specs=(HERE,) * 3,
-        scratch_shapes=corner_scratch,
         compiler_params=params(12),
-    )(corner_y, velocity, left, right)
-    weights = layer_weights(conv_first, conv_mid, conv_last)
-    to_up, to_down, wlo, whi, weights = lax.optimization_barrier(
-        (to_up, to_down, wlo, whi, weights)
-    )
+    )(table, velocity, left, right)
+    weights = (conv_first.transpose(2, 0, 1), conv_mid, conv_last)
+    to_up, to_down, wlo, whi = lax.optimization_barrier((to_up, to_down, wlo, whi))
     xlo = lax.ppermute(to_up, ROWS, up_row)
     xhi = lax.ppermute(to_down, ROWS, down_row)
-    parts = train_call(tables, own, wlo, whi, weights, row_count)
+    parts = train_call(table, own, wlo, whi, weights, row_count)
 
     parts, velocity, xlo, xhi = lax.optimization_barrier((parts, velocity, xlo, xhi))
     shares = lax.all_to_all(parts, EVERY, 0, 0, tiled=True)
@@ -673,7 +678,7 @@
             pltpu.VMEM(right.shape, F32),
             pltpu.SemaphoreType.DMA((4,)),
         ],
-        compiler_params=params(24),
+        compiler_params=params(60),
         cost_estimate=pl.CostEstimate(flops=10**7, bytes_accessed=4 * 10**7, transcendentals=0),
     )(velocity, xlo, xhi, left, right)
     shares, wide_next = lax.optimization_barrier((shares, wide_next))
@@ -689,8 +694,14 @@
         compiler_params=params(24),
         cost_estimate=pl.CostEstimate(flops=10**7, bytes_accessed=4 * 10**7, transcendentals=0),
     )(wide_next)
-    mine = jnp.sum(shares, axis=0, keepdims=True)
-    summed = lax.all_to_all(jnp.broadcast_to(mine, parts.shape), EVERY, 0, 0, tiled=True)
+    mine = pl.pallas_call(
+        sum_kernel,
+        out_shape=jax.ShapeDtypeStruct(parts.shape, F32),
+        in_specs=[VMEM],
+        out_specs=VMEM,
+        compiler_params=params(8),
+    )(shares)
+    summed = lax.all_to_all(mine, EVERY, 0, 0, tiled=True)
     grad_first, grad_mid, grad_last, loss = pl.pallas_call(
         unpack_kernel,
         out_shape=(

time: 85.3 us -> 79.4 us (0.931)
  local copies, waits for them, and re-layouts: 10.8 us -> 4.83 us
  Pallas kernels: 18.6 us -> 22.2 us
  waiting for transfers between devices: 23.9 us -> 22 us
    unnamed x38 -> x22, local copies, waits for them, and re-layouts: 9.98 us -> 4.83 us
    pallas_call x1, Pallas kernels: 6.23 us -> 9.11 us  [local(): pl.pallas_call(solver_kernel, out_shape=(jax.ShapeDtypeStruct(velocity.sh...]
    all_to_all x1, waiting for transfers between devices: 8.4 us -> 6.68 us  [local(): summed = lax.all_to_all(mine, EVERY, 0, 0, tiled=True)]
    reduce_sum x1 -> x0, other arithmetic: 1.18 us -> none  [local(): mine = jnp.sum(shares, axis=0, keepdims=True)]
    all_to_all x1, starting transfers between devices: 6.32 us -> 5.36 us  [local(): summed = lax.all_to_all(mine, EVERY, 0, 0, tiled=True)]
    all_to_all x1, waiting for transfers between devices: 3.45 us -> 4.41 us  [local(): shares = lax.all_to_all(parts, EVERY, 0, 0, tiled=True)]
  transfers between devices with their start and end apart: 8 -> 8, of which waited for: 5 -> 5; matrix products, arithmetic and copies ran while one was open for 0% -> 1% of each run, Pallas kernels for 19% -> 23%
where the time goes in v4:
time: 79.4 us; the launch traced here: 79.3 us
  starting transfers between devices  28.6 us (36%)
  Pallas kernels  22.2 us (28%)
  waiting for transfers between devices  22 us (28%)
  local copies, waits for them, and re-layouts  4.83 us (6%)
  between operations  0.94 us (1%)
    all_to_all x1, starting transfers between devices, local(): shares = lax.all_to_all(parts, EVERY, 0, 0, tiled=True)  9.6 us
    pallas_call x1, Pallas kernels, local(): pl.pallas_call(solver_kernel, out_shape=(jax.ShapeDtypeStruct(velocity.sh...  9.11 us
    ppermute x1, waiting for transfers between devices, local(): xlo = lax.ppermute(to_up, ROWS, up_row)  8.17 us
    all_to_all x1, waiting for transfers between devices, local(): summed = lax.all_to_all(mine, EVERY, 0, 0, tiled=True)  6.68 us
    all_to_all x1, starting transfers between devices, local(): summed = lax.all_to_all(mine, EVERY, 0, 0, tiled=True)  5.36 us
    pallas_call x1, Pallas kernels, local(): pl.pallas_call(filter_kernel, out_shape=(jax.ShapeDtypeStruct(velocity.sh...  5.18 us
    unnamed x22, local copies, waits for them, and re-layouts  4.83 us
    all_to_all x1, waiting for transfers between devices, local(): shares = lax.all_to_all(parts, EVERY, 0, 0, tiled=True)  4.41 us
  transfers between devices with their start and end apart: 8, of which 5 were waited for; matrix products, arithmetic and copies ran while one was open for 1% of the time, Pallas kernels for 23%

profile of v4, /device:TPU:1, one launch (start us, length us, event | category | flops | bytes accessed | tf_op | source)
XLA Modules:
  0.0 79.3 jit_solution(16623958049453616405)
XLA Ops:
  0.6 0.0 copy-start
  0.6 1.2 %copy-done = f32[3,20,32,128]{3,2,1,0:T(8,128)S(1)} copy-done((f32[3,20,32,128]{3,2,1,0:T(8,128)S(1)}, f32[3,20,32,128]{3,2,1,0:T(8,128)}, u32[]{:S(2)}) %copy-start) | copy-done | bytes 983064
  1.8 0.6 shard_map.144
  2.4 2.7 %collective-permute-start = (f32[3,32,128]{2,1,0:T(8,128)S(1)}, f32[3,32,128]{2,1,0:T(8,128)S(1)}, u32[]{:S(2)}, u32[]{:S(2)}) collective-permute-start(f32[3,32,128]{2,1,0:T(8,128)S(1)} %get-tuple-element.34), channel_id=1, source_target_pairs={{0,1},{1,2},{2,3},{3,4},{4,5},{5,6},{6,7},{7,0},{8,9},{9,10},{10,1... | collective-permute-start | bytes 147464 | tf_op jit(solution)/shard_map/ppermute | solution.py:634
  5.1 0.0 collective-permute-start.1
  5.1 0.8 add_bitcast_fusion.table
  5.9 0.0 copy-start.6
  5.9 0.4 collective-permute-done.left.left_h
  6.3 0.0 copy-start.3
  6.3 2.3 %collective-permute-done.1.right.right_h = f32[3,32,128]{2,1,0:T(8,128)S(1)} collective-permute-done((f32[3,32,128]{2,1,0:T(8,128)S(1)}, f32[3,32,128]{2,1,0:T(8,128)S(1)}, u32[]{:S(2)}, u32[]{:S(2)}) %collective-permute-start.1) | collective-permute-done | bytes 49184 | tf_op jit(solution)/shard_map/ppermute | solution.py:635
  8.6 0.0 copy-start.4
  8.6 1.1 %shard_map.146 = (f32[3,5,8,128]{3,2,1,0:T(8,128)S(1)}, f32[3,5,8,128]{3,2,1,0:T(8,128)S(1)}) custom-call(s32[8,16]{1,0:T(8,128)S(1)} %add_bitcast_fusion.table, f32[3,5,32,128]{3,2,1,0:T(8,128)S(1)} %get-tuple-element.39.low_rows, f32[3,5,32,128]{3,2,1,0:T(8,128)S(1)} %get-tuple-element.40.high_rows, f32[3,32,128]{2,1,0:T(8,128)S(1)} %collective-permute-done.left.left_h, ...), custom_call_target="tpu_custom_call" | custom-call | tf_op jit(solution)/shard_map/pallas_call | solution.py:637
  9.7 3.7 %collective-permute-start.2 = (f32[3,5,8,128]{3,2,1,0:T(8,128)S(1)}, f32[3,5,8,128]{3,2,1,0:T(8,128)S(1)}, u32[]{:S(2)}, u32[]{:S(2)}) collective-permute-start(f32[3,5,8,128]{3,2,1,0:T(8,128)S(1)} %get-tuple-element.41), channel_id=1, source_target_pairs={{0,8},{8,16},{16,24},{24,32},{32,40},{40,48},{48,56},{56,64},{64,7... | collective-permute-start | bytes 184328 | tf_op jit(solution)/shard_map/ppermute | solution.py:644
  13.4 2.4 %collective-permute-start.3 = (f32[3,5,8,128]{3,2,1,0:T(8,128)S(1)}, f32[3,5,8,128]{3,2,1,0:T(8,128)S(1)}, u32[]{:S(2)}, u32[]{:S(2)}) collective-permute-start(f32[3,5,8,128]{3,2,1,0:T(8,128)S(1)} %get-tuple-element.42), channel_id=1, source_target_pairs={{8,0},{16,8},{24,16},{32,24},{40,32},{48,40},{56,48},{64,56},{72,6... | collective-permute-start | bytes 184328 | tf_op jit(solution)/shard_map/ppermute | solution.py:645
  15.8 0.0 copy-start.1
  15.8 1.2 %copy-done.1 = f32[3,20,32,128]{3,2,1,0:T(8,128)S(1)} copy-done((f32[3,20,32,128]{3,2,1,0:T(8,128)S(1)}, f32[3,20,32,128]{3,2,1,0:T(8,128)}, u32[]{:S(2)}) %copy-start.1) | copy-done | bytes 983064
  17.0 1.9 %shard_map.145 = (f32[3,20,8,128]{3,2,1,0:T(8,128)S(1)}, f32[3,6,32,128]{3,2,1,0:T(8,128)S(1)}, f32[3,6,32,128]{3,2,1,0:T(8,128)S(1)}) custom-call(s32[8,16]{1,0:T(8,128)S(1)} %add_bitcast_fusion.table, f32[3,20,32,128]{3,2,1,0:T(8,128)S(1)} %copy-done.1, f32[3,32,128]{2,1,0:T(8,128)S(1)} %collective-permute-done.left.left_h, ...), custom_call_target="tpu_custom_call" | custom-call | tf_op jit(solution)/shard_map/pallas_call | solution.py:647
  18.9 0.0 copy-start.5
  18.9 0.7 copy-done.5
  19.6 0.0 collective-permute-done.2.wlo
  19.6 0.0 copy-start.9
  19.6 0.0 collective-permute-done.3.whi
  19.6 0.0 copy-start.10
  19.6 0.6 collective-permute-start.4
  20.2 4.3 %collective-permute-start.5 = (f32[3,6,32,128]{3,2,1,0:T(8,128)S(1)}, f32[3,6,32,128]{3,2,1,0:T(8,128)S(1)}, u32[]{:S(2)}, u32[]{:S(2)}) collective-permute-start(f32[3,6,32,128]{3,2,1,0:T(8,128)S(1)} %get-tuple-element.46), channel_id=1, source_target_pairs={{8,0},{16,8},{24,16},{32,24},{40,32},{48,40},{56,48},{64,56},{72,6... | collective-permute-start | bytes 884744 | tf_op jit(solution)/shard_map/ppermute | solution.py:657
  24.5 0.0 copy-done.6
  24.5 0.0 copy-done.9
  24.5 0.0 copy-done.10
  24.5 2.3 %shard_map.147 = f32[128,8,128]{2,1,0:T(8,128)} custom-call(s32[8,16]{1,0:T(8,128)} %copy-done.6, f32[3,20,8,128]{3,2,1,0:T(8,128)} %copy-done.5, f32[3,5,8,128]{3,2,1,0:T(8,128)} %copy-done.9, f32[3,5,8,128]{3,2,1,0:T(8,128)} %copy-done.10, bf16[3,27,64]{2,1,0:T(8,128)(2,1)} %bitcast.4, bf16[27,64,64]{2,1,0:T(8,128)(2,1)} %mid.1, bf16[6,64]{1,0:T(8,128)(2,1)} %last_w.1), custom_call_target="tpu_custom_call" | custom-call | flops 10000000 | bytes 60000000 | tf_op jit(solution)/shard_map/pallas_call | solution.py:581
  26.8 8.2 %collective-permute-done.4.xlo_h = f32[3,6,32,128]{3,2,1,0:T(8,128)S(1)} collective-permute-done((f32[3,6,32,128]{3,2,1,0:T(8,128)S(1)}, f32[3,6,32,128]{3,2,1,0:T(8,128)S(1)}, u32[]{:S(2)}, u32[]{:S(2)}) %collective-permute-start.4) | collective-permute-done | bytes 294944 | tf_op jit(solution)/shard_map/ppermute | solution.py:656
  34.9 0.0 copy-start.7
  34.9 0.0 collective-permute-done.5.xhi_h
  34.9 0.0 copy-start.8
  34.9 9.6 %all-to-all-start = ((f32[128,8,128]{2,1,0:T(8,128)}), f32[128,8,128]{2,1,0:T(8,128)S(1)}, u32[]{:S(2)}, u32[]{:S(2)}) async-start(f32[128,8,128]{2,1,0:T(8,128)} %shard_map.147), calls=%async_computation | async-start | bytes 1048576 | tf_op jit(solution)/shard_map/all_to_all | solution.py:661
  44.5 0.0 copy-done.3
  44.6 0.0 copy-done.4
  44.6 0.0 copy-done.7
  44.6 0.0 copy-done.8
  44.6 9.1 %shard_map.148 = (f32[3,20,32,128]{3,2,1,0:T(8,128)}, f32[3,26,32,256]{3,2,1,0:T(8,128)}) custom-call(f32[3,20,32,128]{3,2,1,0:T(8,128)} %vel.4, f32[3,6,32,128]{3,2,1,0:T(8,128)} %copy-done.7, f32[3,6,32,128]{3,2,1,0:T(8,128)} %copy-done.8, f32[3,32,128]{2,1,0:T(8,128)} %copy-done.3, f32[3,32,128]{2,1,0:T(8,128)} %copy-done.4), custom_call_target="tpu_custom_call" | custom-call | flops 10000000 | bytes 40000000 | tf_op jit(solution)/shard_map/pallas_call | solution.py:664
  53.7 4.4 %all-to-all-done.shares = f32[128,8,128]{2,1,0:T(8,128)S(1)} async-done(((f32[128,8,128]{2,1,0:T(8,128)}), f32[128,8,128]{2,1,0:T(8,128)S(1)}, u32[]{:S(2)}, u32[]{:S(2)}) %all-to-all-start) | async-done | bytes 524320 | tf_op jit(solution)/shard_map/all_to_all | solution.py:661
  58.1 1.0 %shard_map.150 = f32[128,8,128]{2,1,0:T(8,128)} custom-call(f32[128,8,128]{2,1,0:T(8,128)S(1)} %all-to-all-done.shares), custom_call_target="tpu_custom_call" | custom-call | tf_op jit(solution)/shard_map/pallas_call | solution.py:697
  59.1 5.4 %all-to-all-start.1 = ((f32[128,8,128]{2,1,0:T(8,128)}), f32[128,8,128]{2,1,0:T(8,128)S(1)}, u32[]{:S(2)}, u32[]{:S(2)}) async-start(f32[128,8,128]{2,1,0:T(8,128)} %shard_map.150), calls=%async_computation.1 | async-start | bytes 1048576 | tf_op jit(solution)/shard_map/all_to_all | solution.py:704
  64.4 0.0 copy-start.2
  64.5 1.7 %copy-done.2 = f32[3,26,32,256]{3,2,1,0:T(8,128)S(1)} copy-done((f32[3,26,32,256]{3,2,1,0:T(8,128)S(1)}, f32[3,26,32,256]{3,2,1,0:T(8,128)}, u32[]{:S(2)}) %copy-start.2) | copy-done | bytes 2555928
  66.2 5.2 %shard_map.149 = (f32[3,20,32,128]{3,2,1,0:T(8,128)}, f32[6,20,32,128]{3,2,1,0:T(8,128)}) custom-call(f32[3,26,32,256]{3,2,1,0:T(8,128)S(1)} %copy-done.2), custom_call_target="tpu_custom_call" | custom-call | flops 10000000 | bytes 40000000 | tf_op jit(solution)/shard_map/pallas_call | solution.py:685
  71.3 6.7 %all-to-all-done.1.parts = f32[128,8,128]{2,1,0:T(8,128)S(1)} async-done(((f32[128,8,128]{2,1,0:T(8,128)}), f32[128,8,128]{2,1,0:T(8,128)S(1)}, u32[]{:S(2)}, u32[]{:S(2)}) %all-to-all-start.1) | async-done | bytes 524320 | tf_op jit(solution)/shard_map/all_to_all | solution.py:704
  78.0 1.1 %shard_map.151 = (f32[3,27,64]{2,1,0:T(8,128)}, f32[27,64,64]{2,1,0:T(8,128)}, f32[6,64]{1,0:T(8,128)}, f32[1]{0:T(128)}) custom-call(f32[128,8,128]{2,1,0:T(8,128)S(1)} %all-to-all-done.1.parts), custom_call_target="tpu_custom_call" | custom-call | tf_op jit(solution)/shard_map/pallas_call | solution.py:705
Async XLA Ops:
  0.6 1.2 %copy-start = (f32[3,20,32,128]{3,2,1,0:T(8,128)S(1)}, f32[3,20,32,128]{3,2,1,0:T(8,128)}, u32[]{:S(2)}) copy-start(f32[3,20,32,128]{3,2,1,0:T(8,128)} %vel.4) | copy-start | bytes 2949124
  2.4 3.9 %collective-permute-start = (f32[3,32,128]{2,1,0:T(8,128)S(1)}, f32[3,32,128]{2,1,0:T(8,128)S(1)}, u32[]{:S(2)}, u32[]{:S(2)}) collective-permute-start(f32[3,32,128]{2,1,0:T(8,128)S(1)} %get-tuple-element.34), channel_id=1, source_target_pairs={{0,1},{1,2},{2,3},{3,4},{4,5},{5,6},{6,7},{7,0},{8,9},{9,10},{10,1... | collective-permute-start | bytes 147464 | tf_op jit(solution)/shard_map/ppermute | solution.py:634
  5.1 3.5 %collective-permute-start.1 = (f32[3,32,128]{2,1,0:T(8,128)S(1)}, f32[3,32,128]{2,1,0:T(8,128)S(1)}, u32[]{:S(2)}, u32[]{:S(2)}) collective-permute-start(f32[3,32,128]{2,1,0:T(8,128)S(1)} %get-tuple-element.35), channel_id=1, source_target_pairs={{1,0},{2,1},{3,2},{4,3},{5,4},{6,5},{7,6},{0,7},{9,8},{10,9},{11,1... | collective-permute-start | bytes 147464 | tf_op jit(solution)/shard_map/ppermute | solution.py:635
  5.9 18.6 %copy-start.6 = (s32[8,16]{1,0:T(8,128)}, s32[8,16]{1,0:T(8,128)S(1)}, u32[]{:S(2)}) copy-start(s32[8,16]{1,0:T(8,128)S(1)} %add_bitcast_fusion.table) | copy-start | bytes 1540
  6.3 38.3 %copy-start.3 = (f32[3,32,128]{2,1,0:T(8,128)}, f32[3,32,128]{2,1,0:T(8,128)S(1)}, u32[]{:S(2)}) copy-start(f32[3,32,128]{2,1,0:T(8,128)S(1)} %collective-permute-done.left.left_h) | copy-start | bytes 147460
  8.6 35.9 %copy-start.4 = (f32[3,32,128]{2,1,0:T(8,128)}, f32[3,32,128]{2,1,0:T(8,128)S(1)}, u32[]{:S(2)}) copy-start(f32[3,32,128]{2,1,0:T(8,128)S(1)} %collective-permute-done.1.right.right_h) | copy-start | bytes 147460
  9.7 9.9 %collective-permute-start.2 = (f32[3,5,8,128]{3,2,1,0:T(8,128)S(1)}, f32[3,5,8,128]{3,2,1,0:T(8,128)S(1)}, u32[]{:S(2)}, u32[]{:S(2)}) collective-permute-start(f32[3,5,8,128]{3,2,1,0:T(8,128)S(1)} %get-tuple-element.41), channel_id=1, source_target_pairs={{0,8},{8,16},{16,24},{24,32},{32,40},{40,48},{48,56},{56,64},{64,7... | collective-permute-start | bytes 184328 | tf_op jit(solution)/shard_map/ppermute | solution.py:644
  13.4 6.2 %collective-permute-start.3 = (f32[3,5,8,128]{3,2,1,0:T(8,128)S(1)}, f32[3,5,8,128]{3,2,1,0:T(8,128)S(1)}, u32[]{:S(2)}, u32[]{:S(2)}) collective-permute-start(f32[3,5,8,128]{3,2,1,0:T(8,128)S(1)} %get-tuple-element.42), channel_id=1, source_target_pairs={{8,0},{16,8},{24,16},{32,24},{40,32},{48,40},{56,48},{64,56},{72,6... | collective-permute-start | bytes 184328 | tf_op jit(solution)/shard_map/ppermute | solution.py:645
  15.8 1.2 %copy-start.1 = (f32[3,20,32,128]{3,2,1,0:T(8,128)S(1)}, f32[3,20,32,128]{3,2,1,0:T(8,128)}, u32[]{:S(2)}) copy-start(f32[3,20,32,128]{3,2,1,0:T(8,128)} %vel.4) | copy-start | bytes 2949124
  18.9 0.7 copy-start.5
  19.6 4.9 %copy-start.9 = (f32[3,5,8,128]{3,2,1,0:T(8,128)}, f32[3,5,8,128]{3,2,1,0:T(8,128)S(1)}, u32[]{:S(2)}) copy-start(f32[3,5,8,128]{3,2,1,0:T(8,128)S(1)} %collective-permute-done.2.wlo) | copy-start | bytes 184324
  19.6 4.9 %copy-start.10 = (f32[3,5,8,128]{3,2,1,0:T(8,128)}, f32[3,5,8,128]{3,2,1,0:T(8,128)S(1)}, u32[]{:S(2)}) copy-start(f32[3,5,8,128]{3,2,1,0:T(8,128)S(1)} %collective-permute-done.3.whi) | copy-start | bytes 184324
  19.6 15.3 %collective-permute-start.4 = (f32[3,6,32,128]{3,2,1,0:T(8,128)S(1)}, f32[3,6,32,128]{3,2,1,0:T(8,128)S(1)}, u32[]{:S(2)}, u32[]{:S(2)}) collective-permute-start(f32[3,6,32,128]{3,2,1,0:T(8,128)S(1)} %get-tuple-element.45), channel_id=1, source_target_pairs={{0,8},{8,16},{16,24},{24,32},{32,40},{40,48},{48,56},{56,64},{64,7... | collective-permute-start | bytes 884744 | tf_op jit(solution)/shard_map/ppermute | solution.py:656
  20.2 14.7 %collective-permute-start.5 = (f32[3,6,32,128]{3,2,1,0:T(8,128)S(1)}, f32[3,6,32,128]{3,2,1,0:T(8,128)S(1)}, u32[]{:S(2)}, u32[]{:S(2)}) collective-permute-start(f32[3,6,32,128]{3,2,1,0:T(8,128)S(1)} %get-tuple-element.46), channel_id=1, source_target_pairs={{8,0},{16,8},{24,16},{32,24},{40,32},{48,40},{56,48},{64,56},{72,6... | collective-permute-start | bytes 884744 | tf_op jit(solution)/shard_map/ppermute | solution.py:657
  34.9 9.6 %copy-start.7 = (f32[3,6,32,128]{3,2,1,0:T(8,128)}, f32[3,6,32,128]{3,2,1,0:T(8,128)S(1)}, u32[]{:S(2)}) copy-start(f32[3,6,32,128]{3,2,1,0:T(8,128)S(1)} %collective-permute-done.4.xlo_h) | copy-start | bytes 884740
  34.9 9.6 %copy-start.8 = (f32[3,6,32,128]{3,2,1,0:T(8,128)}, f32[3,6,32,128]{3,2,1,0:T(8,128)S(1)}, u32[]{:S(2)}) copy-start(f32[3,6,32,128]{3,2,1,0:T(8,128)S(1)} %collective-permute-done.5.xhi_h) | copy-start | bytes 884740
  34.9 23.2 %all-to-all-start = ((f32[128,8,128]{2,1,0:T(8,128)}), f32[128,8,128]{2,1,0:T(8,128)S(1)}, u32[]{:S(2)}, u32[]{:S(2)}) async-start(f32[128,8,128]{2,1,0:T(8,128)} %shard_map.147), calls=%async_computation | async-start | bytes 1048576 | tf_op jit(solution)/shard_map/all_to_all | solution.py:661
  59.1 18.9 %all-to-all-start.1 = ((f32[128,8,128]{2,1,0:T(8,128)}), f32[128,8,128]{2,1,0:T(8,128)S(1)}, u32[]{:S(2)}, u32[]{:S(2)}) async-start(f32[128,8,128]{2,1,0:T(8,128)} %shard_map.150), calls=%async_computation.1 | async-start | bytes 1048576 | tf_op jit(solution)/shard_map/all_to_all | solution.py:704
  64.4 1.7 %copy-start.2 = (f32[3,26,32,256]{3,2,1,0:T(8,128)S(1)}, f32[3,26,32,256]{3,2,1,0:T(8,128)}, u32[]{:S(2)}) copy-start(f32[3,26,32,256]{3,2,1,0:T(8,128)} %get-tuple-element.53.wa) | copy-start | bytes 7667716
